TPU v7x, 32 devices: a whole 2x2x4 slice. The times are simulated.
32 devices in a mesh: section: 2 (over core), dp: 4 (over z), expert: 4 (over y, x).
Axes of the slice: x: 2, y: 2, z: 4, core: 2. Of those that a mesh axis runs over, the one named last changes fastest.
Arguments:
- tokens: bfloat16 [2, 768, 3072], P('section', 'expert'), may hold values from -6 to 6
- expert_ids: int32 [2, 768, 2], P('section', 'expert'), may hold values from 0 to 7, all different within a row; in each aligned block of 192 rows (0 to 191, 192 to 383, ..., all dimensions but the last counted through in order) at most 72 rows name the same one
- gate_probs: float32 [2, 768, 2], P('section', 'expert'), may hold values from 0.2 to 1
- cotangent: bfloat16 [2, 768, 3072], P('section', 'expert'), may hold values from -6 to 6
- w_gate: bfloat16 [2, 8, 3072, 8192], P('section', 'expert', None, 'dp'), may hold values from -0.109375 to 0.109375
- w_up: bfloat16 [2, 8, 3072, 8192], P('section', 'expert', None, 'dp'), may hold values from -0.109375 to 0.109375
- w_down: bfloat16 [2, 8, 8192, 3072], P('section', 'expert', 'dp'), may hold values from -0.0625 to 0.0625
Outputs:
- moe_out: bfloat16 [2, 768, 3072], P('section', 'expert')
- grad_handoff: bfloat16 [2, 768, 3072], P('section', 'expert')
Inputs may be any that keep to these rules, and one draw needn't show every extreme that they name: `expert_ids`: A token's two experts differ. Among the 192 tokens of one device (aligned blocks of a section's tokens) no expert is named more than 72 times, a bound that some block reaches.
All inputs are finite; a program needn't handle non-finite values.
Results may differ from a plain program's by a relative error of at most 0.013.
Values may be sent and summed in bfloat16 or wider, within the bound.
No kernel may reach another device: no remote copies, remote signals or barrier semaphores. Data moves between devices by JAX's collectives and lax.ppermute only.
A program may use at most 256 MiB of HBM per device.

v0:
```python
import jax
import jax.numpy as jnp
from jax import lax
from jax.sharding import PartitionSpec as P

CAP = 72


def from_behind(block, axis, distance):
    devices = range(lax.axis_size(axis))
    route = [((i - distance) % len(devices), i) for i in devices]
    return lax.ppermute(block, axis, route)


def slot_tables(chosen, weights_two, experts, capacity):
    number = chosen.shape[0]
    flattened = chosen.reshape(-1)
    one_hot = (flattened[:, None] == jnp.arange(experts, dtype=jnp.int32)[None, :]).astype(
        jnp.int32
    )
    earlier = jnp.cumsum(one_hot, axis=0) - one_hot
    position = jnp.sum(earlier * one_hot, axis=1)
    slot_index = flattened * capacity + position
    selection = (
        slot_index[:, None] == jnp.arange(experts * capacity, dtype=jnp.int32)[None, :]
    ).astype(jnp.float32)
    selection = selection.reshape(number, 2, experts * capacity)
    routing = jnp.sum(selection, axis=1)
    slot_weight = jnp.sum(selection * weights_two[:, :, None], axis=(0, 1))
    return (routing, slot_weight, slot_index.reshape(number, 2))


def combine(values, slot_pair, factors):
    first = jnp.take(values, slot_pair[:, 0], axis=0)
    second = jnp.take(values, slot_pair[:, 1], axis=0)
    return (factors[:, 0:1] * first + factors[:, 1:2] * second).astype(jnp.bfloat16)


def project(piece, gate_local, up_local, capacity):
    number = piece.shape[0]
    grid = piece.reshape(number, gate_local.shape[0], capacity, piece.shape[2])
    gate = jnp.einsum("sxcd,xdf->sxcf", grid, gate_local, preferred_element_type=jnp.float32)
    upper = jnp.einsum("sxcd,xdf->sxcf", grid, up_local, preferred_element_type=jnp.float32)
    return jnp.concatenate([gate, upper], axis=3)


def forward_partial(gate_up, down_local):
    width = down_local.shape[1]
    gate = gate_up[..., :width]
    upper = gate_up[..., width:]
    hidden = (gate * jax.nn.sigmoid(gate) * upper).astype(jnp.bfloat16)
    partial_out = jnp.einsum(
        "sxcf,xfd->sxcd", hidden, down_local, preferred_element_type=jnp.float32
    )
    return partial_out.astype(jnp.bfloat16)


def backward_partial(piece, gate_up, gate_local, up_local, down_local, capacity):
    number = piece.shape[0]
    width = down_local.shape[1]
    grid = piece.reshape(number, gate_local.shape[0], capacity, piece.shape[2])
    hidden_cot = jnp.einsum("sxcd,xfd->sxcf", grid, down_local, preferred_element_type=jnp.float32)
    gate = gate_up[..., :width]
    upper = gate_up[..., width:]
    sigma = jax.nn.sigmoid(gate)
    active = gate * sigma
    slope = sigma * (1.0 + gate * (1.0 - sigma))
    gate_cot = (hidden_cot * upper * slope).astype(jnp.bfloat16)
    up_cot = (hidden_cot * active).astype(jnp.bfloat16)
    partial_grad = jnp.einsum(
        "sxcf,xdf->sxcd", gate_cot, gate_local, preferred_element_type=jnp.float32
    )
    partial_grad = partial_grad + jnp.einsum(
        "sxcf,xdf->sxcd", up_cot, up_local, preferred_element_type=jnp.float32
    )
    return partial_grad.astype(jnp.bfloat16)


def body(tokens, expert_ids, gate_probs, cotangent, w_gate, w_up, w_down):
    activations = tokens[0]
    chosen = expert_ids[0]
    weights_two = gate_probs[0]
    upstream = cotangent[0]
    gate_local = w_gate[0]
    up_local = w_up[0]
    down_local = w_down[0]
    local = gate_local.shape[0]
    model = activations.shape[1]
    groups = lax.axis_size("expert")
    experts = local * groups
    capacity = CAP
    routing, slot_weight, slot_pair = slot_tables(chosen, weights_two, experts, capacity)
    picker = routing.T.astype(jnp.bfloat16)
    slot_rows = jnp.dot(picker, activations, preferred_element_type=jnp.float32).astype(
        jnp.bfloat16
    )
    cot_plain = jnp.dot(picker, upstream, preferred_element_type=jnp.float32)
    cot_rows = (cot_plain * slot_weight[:, None]).astype(jnp.bfloat16)
    ones_two = jnp.ones_like(weights_two)
    send_shape = (groups, local * capacity, model)
    arrived = lax.all_to_all(
        slot_rows.reshape(send_shape), "expert", split_axis=0, concat_axis=0, tiled=True
    )
    gate_up = project(arrived, gate_local, up_local, capacity)
    panel_out = forward_partial(gate_up, down_local).reshape(send_shape)
    summed_out = lax.psum(panel_out.astype(jnp.float32).astype(jnp.bfloat16), "dp").astype(
        jnp.float32
    )
    expert_back = lax.all_to_all(
        summed_out.astype(jnp.bfloat16), "expert", split_axis=0, concat_axis=0, tiled=True
    ).astype(summed_out.dtype)
    outputs = combine(expert_back.reshape(experts * capacity, model), slot_pair, weights_two)
    cot_arrived = lax.all_to_all(
        cot_rows.reshape(send_shape), "expert", split_axis=0, concat_axis=0, tiled=True
    )
    panel_grad = backward_partial(
        cot_arrived, gate_up, gate_local, up_local, down_local, capacity
    ).reshape(send_shape)
    summed_grad = lax.psum(panel_grad.astype(jnp.float32).astype(jnp.bfloat16), "dp").astype(
        jnp.float32
    )
    grad_back = lax.all_to_all(
        summed_grad.astype(jnp.bfloat16), "expert", split_axis=0, concat_axis=0, tiled=True
    ).astype(summed_grad.dtype)
    gradient = combine(grad_back.reshape(experts * capacity, model), slot_pair, ones_two)
    handed = from_behind(gradient, "section", 1)
    return (outputs[None], handed[None])


def solution(mesh):
    placed = (
        P("section", "expert", None),
        P("section", "expert", None),
        P("section", "expert", None),
        P("section", "expert", None),
        P("section", "expert", None, "dp"),
        P("section", "expert", None, "dp"),
        P("section", "expert", "dp", None),
    )
    return jax.shard_map(
        body,
        mesh=mesh,
        in_specs=placed,
        out_specs=(P("section", "expert", None), P("section", "expert", None)),
        check_vma=False,
    )
```

profile of v0, /device:TPU:0, one launch (start us, length us, event | category | flops | bytes accessed | tf_op | source)
XLA Modules:
  0.0 557.8 jit_solution(10475668590824517613)
XLA Ops:
  7.2 0.0 copy-start
  7.2 0.9 copy.29
  8.1 0.1 eq.43
  8.2 0.1 eq.39
  8.4 0.9 reduce-window.6
  9.2 0.2 slice_reduce_fusion.2
  9.5 0.1 fusion.48
  9.6 0.1 reduce_sum.30
  9.8 0.1 copy.32
  9.8 1.0 select_reduce_fusion
  10.8 0.0 copy-done
  10.8 2.9 convolution_convert_fusion
  13.8 0.0 copy-start.3
  13.8 5.3 all-to-all-start
  19.1 0.0 copy-done.3
  19.1 2.9 multiply_convert_fusion
  21.9 38.6 %all-to-all-done = bf16[4,144,3072]{2,1,0:T(8,128)(2,1)} async-done(((bf16[4,144,3072]{2,1,0:T(8,128)(2,1)}), bf16[4,144,3072]{2,1,0:T(8,128)(2,1)}, u32[]{:S(2)}, u32[]{:S(2)}) %all-to-all-start) | async-done | bytes 3538976 | tf_op jit(solution)/shard_map/all_to_all | solution.py:101
  60.5 4.7 all-to-all-start.2
  65.2 0.2 all-reduce.3.cloned.1.call-start
  65.5 14.7 %fusion.6 = f32[2,4,72,2048]{3,2,1,0:T(8,128)} fusion(bf16[1,2,3072,2048]{3,2,1,0:T(8,128)(2,1)} %param.13, bf16[4,2,72,3072]{3,2,1,0:T(8,128)(2,1)} %bitcast.7), kind=kOutput, calls=%fused_computation.10 | convolution fusion | flops 7247757312 | bytes 33423360 | tf_op jit(solution)/shard_map/sxcd,xdf->sxcf/dot_general | solution.py:42
  80.2 14.8 %fusion.2 = f32[2,4,72,2048]{3,2,1,0:T(8,128)} fusion(bf16[1,2,3072,2048]{3,2,1,0:T(8,128)(2,1)} %param.14, bf16[4,2,72,3072]{3,2,1,0:T(8,128)(2,1)} %bitcast.7), kind=kOutput, calls=%fused_computation.6 | convolution fusion | flops 7247757312 | bytes 33423360 | tf_op jit(solution)/shard_map/sxcd,xdf->sxcf/dot_general | solution.py:43
  95.0 10.4 %all-to-all-done.2 = bf16[4,144,3072]{2,1,0:T(8,128)(2,1)} async-done(((bf16[4,144,3072]{2,1,0:T(8,128)(2,1)}), bf16[4,144,3072]{2,1,0:T(8,128)(2,1)}, u32[]{:S(2)}, u32[]{:S(2)}) %all-to-all-start.2) | async-done | bytes 3538976 | tf_op jit(solution)/shard_map/all_to_all | solution.py:113
  105.3 15.2 %fusion.8 = f32[2,4,72,2048]{3,2,1,0:T(8,128)} fusion(bf16[1,2,2048,3072]{3,2,1,0:T(8,128)(2,1)} %param.15, bf16[4,2,72,3072]{3,2,1,0:T(8,128)(2,1)} %bitcast.27), kind=kOutput, calls=%fused_computation.12 | convolution fusion | flops 7247757312 | bytes 33423360 | tf_op jit(solution)/shard_map/sxcd,xfd->sxcf/dot_general | solution.py:62
  120.5 18.0 %fusion = f32[2,4,72,3072]{3,2,1,0:T(8,128)} fusion(bf16[1,2,3072,2048]{3,2,1,0:T(8,128)(2,1)} %param.14, f32[2,4,72,2048]{3,2,1,0:T(8,128)} %fusion.8, f32[2,4,72,2048]{3,2,1,0:T(8,128)} %fusion.6), kind=kOutput, calls=%fused_computation.4 | convolution fusion | flops 7254835200 | bytes 41680896 | tf_op jit(solution)/shard_map/sxcf,xdf->sxcd/dot_general | solution.py:73
  138.5 17.6 %fusion.24 = bf16[4,2,72,3072]{3,2,0,1:T(8,128)(2,1)S(1)} fusion(bf16[1,2,2048,3072]{3,2,1,0:T(8,128)(2,1)} %param.15, f32[2,4,72,2048]{3,2,1,0:T(8,128)} %fusion.2, f32[2,4,72,2048]{3,2,1,0:T(8,128)} %fusion.6), kind=kOutput, calls=%fused_computation.35 | convolution fusion | flops 7256604672 | bytes 38141952 | tf_op jit(solution)/shard_map/sxcf,xfd->sxcd/dot_general | solution.py:52
  156.1 19.8 %fusion.29 = bf16[4,2,72,3072]{3,2,0,1:T(8,128)(2,1)} fusion(f32[2,4,72,3072]{3,2,1,0:T(8,128)} %fusion, bf16[1,2,3072,2048]{3,2,1,0:T(8,128)(2,1)} %param.13, f32[2,4,72,2048]{3,2,1,0:T(8,128)} %fusion.8, f32[2,4,72,2048]{3,2,1,0:T(8,128)} %fusion.2, f32[2,4,72,2048]{3,2,1,0:T(8,128)} %fusion.6), kind=kOutput, calls=%fused_computation.36 | convolution fusion | flops 7263092736 | bytes 49938432 | tf_op jit(solution)/shard_map/sxcf,xdf->sxcd/dot_general | solution.py:70
  176.0 4.1 copy.37
  180.1 2.1 copy.35
  182.2 0.0 all-reduce.3.cloned.1.call-update
  182.2 249.1 %all-reduce.3.cloned.1.call-done = (bf16[4,144,3072]{2,1,0:T(8,128)(2,1)}, bf16[4,144,3072]{2,1,0:T(8,128)(2,1)}) async-done(((bf16[4,144,3072]{2,1,0:T(8,128)(2,1)}, bf16[4,144,3072]{2,1,0:T(8,128)(2,1)}), (bf16[4,144,3072]{2,1,0:T(8,128)(2,1)}, bf16[4,144,3072]{2,1,0:T(8,128)(2,1)})) %all-reduce.3.cloned.1.call-update) | async-done | bytes 7077904 | tf_op jit(solution)/shard_map/psum | solution.py:106
  431.3 46.6 %all_to_all.20 = bf16[4,144,3072]{2,1,0:T(8,128)(2,1)} all-to-all(bf16[4,144,3072]{2,1,0:T(8,128)(2,1)} %get-tuple-element.7), channel_id=1, replica_groups=mesh['section'=2,'dp'=4,'expert'=4] {'expert'}, dimensions={0} | all-to-all | bytes 7077888 | tf_op jit(solution)/shard_map/all_to_all | solution.py:109
  477.9 0.0 copy-start.2
  477.9 5.1 all-to-all-start.3
  483.1 0.2 slice_reduce_fusion.1
  483.3 0.0 copy-done.2
  483.3 5.8 %bitcast_convert_fusion.1 = f32[576,3072]{1,0:T(8,128)} fusion(bf16[4,144,3072]{2,1,0:T(8,128)(2,1)} %all_to_all.20), kind=kLoop, calls=%fused_computation.38 | loop fusion | flops 1769472 | bytes 10616832 | tf_op jit(solution)/shard_map/reshape | solution.py:112
  489.2 5.5 gather_fusion
  494.7 6.8 %gather_fusion.1 = f32[192,3072]{1,0:T(8,128)} fusion(f32[576,3072]{1,0:T(8,128)} %bitcast_convert_fusion.1, s32[1024]{0:T(1024)S(1)} %pad_clamp_fusion), kind=kCustom, calls=%fused_computation.1.clone | custom fusion | bytes 4719360 | tf_op jit(solution)/shard_map/jit(_take)/gather | solution.py:35
  501.5 20.5 %all-to-all-done.3 = bf16[4,144,3072]{2,1,0:T(8,128)(2,1)} async-done(((bf16[4,144,3072]{2,1,0:T(8,128)(2,1)}), bf16[4,144,3072]{2,1,0:T(8,128)(2,1)}, u32[]{:S(2)}, u32[]{:S(2)}) %all-to-all-start.3) | async-done | bytes 3538976 | tf_op jit(solution)/shard_map/all_to_all | solution.py:122
  522.0 5.8 %bitcast_convert_fusion = f32[576,3072]{1,0:T(8,128)} fusion(bf16[4,144,3072]{2,1,0:T(8,128)(2,1)} %all-to-all-done.3), kind=kLoop, calls=%fused_computation.37 | loop fusion | flops 1769472 | bytes 10616832 | tf_op jit(solution)/shard_map/reshape | solution.py:125
  527.9 6.8 %gather_fusion.2 = f32[192,3072]{1,0:T(8,128)} fusion(f32[576,3072]{1,0:T(8,128)} %bitcast_convert_fusion, s32[1024]{0:T(1024)S(1)} %pad_clamp_fusion.1), kind=kCustom, calls=%fused_computation.2.clone | custom fusion | bytes 4719360 | tf_op jit(solution)/shard_map/jit(_take)/gather | solution.py:34
  534.7 6.9 %gather_fusion.3 = f32[192,3072]{1,0:T(8,128)} fusion(f32[576,3072]{1,0:T(8,128)} %bitcast_convert_fusion, s32[1024]{0:T(1024)S(1)} %pad_clamp_fusion), kind=kCustom, calls=%fused_computation.3.clone | custom fusion | bytes 4719360 | tf_op jit(solution)/shard_map/jit(_take)/gather | solution.py:35
  541.6 0.0 copy-start.1
  541.6 5.6 %fusion.38 = (bf16[192,3072]{1,0:T(8,128)(2,1)S(1)}, bf16[1,192,3072]{2,1,0:T(8,128)(2,1)}) fusion(f32[192,3072]{1,0:T(8,128)} %gather_fusion.3, f32[192,3072]{1,0:T(8,128)} %gather_fusion.2, pred[192]{0:T(512)(128)(4,1)S(1)} %get-tuple-element.15, pred[192]{0:T(512)(128)(4,1)S(1)} %get-tuple-element.16, f32[192,3072]{1,0:T(8,128)} %gather_fusion.1, ...), kind=kLoop, calls=%fused_computation.43 | loop fusion | flops 5898240 | bytes 11798400 | tf_op jit(solution)/shard_map/convert_element_type | solution.py:36
  547.1 0.0 collective-permute-start
  547.1 2.8 collective-permute-done
  550.0 1.0 copy.50
  551.0 0.0 copy-done.1
  (8 shorter events, 0.1 us)
Async XLA Ops:
  7.2 3.7 copy-start
  13.8 5.3 copy-start.3
  13.8 46.7 %all-to-all-start = ((bf16[4,144,3072]{2,1,0:T(8,128)(2,1)}), bf16[4,144,3072]{2,1,0:T(8,128)(2,1)}, u32[]{:S(2)}, u32[]{:S(2)}) async-start(bf16[4,144,3072]{2,1,0:T(8,128)(2,1)} %bitcast.118), calls=%async_computation | async-start | bytes 7077888 | tf_op jit(solution)/shard_map/all_to_all | solution.py:101
  60.5 44.8 %all-to-all-start.2 = ((bf16[4,144,3072]{2,1,0:T(8,128)(2,1)}), bf16[4,144,3072]{2,1,0:T(8,128)(2,1)}, u32[]{:S(2)}, u32[]{:S(2)}) async-start(bf16[4,144,3072]{2,1,0:T(8,128)(2,1)} %bitcast.121), calls=%async_computation.2 | async-start | bytes 7077888 | tf_op jit(solution)/shard_map/all_to_all | solution.py:113
  65.2 366.0 %all-reduce.3.cloned.1.call-start = ((), (), s32[]{:S(2)}) async-start(), calls=%async_computation.4 | async-start | bytes 14155776 | tf_op jit(solution)/shard_map/psum | solution.py:106
  477.9 5.4 copy-start.2
  477.9 44.1 %all-to-all-start.3 = ((bf16[4,144,3072]{2,1,0:T(8,128)(2,1)}), bf16[4,144,3072]{2,1,0:T(8,128)(2,1)}, u32[]{:S(2)}, u32[]{:S(2)}) async-start(bf16[4,144,3072]{2,1,0:T(8,128)(2,1)} %get-tuple-element.8), calls=%async_computation.3 | async-start | bytes 7077888 | tf_op jit(solution)/shard_map/all_to_all | solution.py:122
  541.6 9.4 %copy-start.1 = (bf16[1,192,3072]{2,1,0:T(8,128)(2,1)S(1)}, bf16[1,192,3072]{2,1,0:T(8,128)(2,1)}, u32[]{:S(2)}) copy-start(bf16[1,192,3072]{2,1,0:T(8,128)(2,1)} %param.9) | copy-start | bytes 3538948
  547.1 2.8 collective-permute-start
Sparse Core Ops, SparseCore 0:
  182.3 248.9 all-reduce.2
where the time goes:
time: 559 us; the launch traced here: 558 us
  waiting for transfers between devices  321 us (57%)
  matrix products  106 us (19%)
  blocking collectives  46.6 us (8%)
  local copies, waits for them, and re-layouts  35.1 us (6%)
  other arithmetic  19.3 us (3%)
  starting transfers between devices  15.4 us (3%)
  between operations  14.2 us (3%)
    psum x1, waiting for transfers between devices, body(): lax.psum(panel_out.astype(jnp.float32).astype(jnp.bfloat16), 'dp')  249 us
    all_to_all x1, blocking collectives, body(): lax.all_to_all(summed_out.astype(jnp.bfloat16), 'expert', split_axis=0, c...  46.6 us
    all_to_all x1, waiting for transfers between devices, body(): lax.all_to_all(slot_rows.reshape(send_shape), 'expert', split_axis=0, con...  38.6 us
    all_to_all x1, waiting for transfers between devices, body(): lax.all_to_all(summed_grad.astype(jnp.bfloat16), 'expert', split_axis=0,...  20.5 us
    dot_general x1, matrix products, backward_partial(): jnp.einsum('sxcf,xdf->sxcd', gate_cot, gate_local, preferred_element_type...  19.8 us
    dot_general x1, matrix products, backward_partial(): jnp.einsum('sxcf,xdf->sxcd', up_cot, up_local, preferred_element_type=jnp...  18 us
    dot_general x1, matrix products, forward_partial(): jnp.einsum('sxcf,xfd->sxcd', hidden, down_local, preferred_element_type=j...  17.6 us
    dot_general x1, matrix products, backward_partial(): jnp.einsum('sxcd,xfd->sxcf', grid, down_local, preferred_element_type=jnp...  15.2 us
  transfers between devices with their start and end apart: 5, of which 5 were waited for; matrix products, arithmetic and copies ran while one was open for 9% of the time, Pallas kernels for 0%

commit v1 on v0

v1 whole, which is shorter than its diff:
```python
import jax
import jax.numpy as jnp
from jax import lax
from jax.sharding import PartitionSpec as P

CAP = 72
BF = jnp.bfloat16
F32 = jnp.float32


def swap(block, axis, flip):
    size = lax.axis_size(axis)
    return lax.ppermute(block, axis, [(i, i ^ flip) for i in range(size)])


def slot_tables(chosen, weights_two, experts, local, capacity, me):
    number = chosen.shape[0]
    relative = ((chosen // local) ^ me) * local + chosen % local
    flattened = relative.reshape(-1)
    one_hot = (flattened[:, None] == jnp.arange(experts, dtype=jnp.int32)[None, :]).astype(
        jnp.int32
    )
    earlier = jnp.cumsum(one_hot, axis=0) - one_hot
    position = jnp.sum(earlier * one_hot, axis=1)
    slot_index = flattened * capacity + position
    selection = (
        slot_index[:, None] == jnp.arange(experts * capacity, dtype=jnp.int32)[None, :]
    ).astype(F32)
    selection = selection.reshape(number, 2, experts * capacity)
    routing = jnp.sum(selection, axis=1)
    weighting = jnp.sum(selection * weights_two[:, :, None], axis=1)
    slot_weight = jnp.sum(weighting, axis=0)
    return routing, weighting, slot_weight


def dot(a, b, dims):
    return lax.dot_general(a, b, dims, preferred_element_type=F32)


def sum_over(block, axis):
    size = lax.axis_size(axis)
    if size != 4:
        return lax.psum(block, axis)
    half = block.shape[1] // 2
    z = lax.axis_index(axis)
    first = (z == 0) | (z == 3)
    left, right = block[:, :half], block[:, half:]
    mine = jnp.where(first, left, right)
    other = jnp.where(first, right, left)
    mine = mine.astype(F32) + swap(other, axis, 1).astype(F32)
    mine = mine.astype(BF)
    mine = (mine.astype(F32) + swap(mine, axis, 3).astype(F32)).astype(BF)
    other = swap(mine, axis, 1)
    return jnp.concatenate([jnp.where(first, mine, other), jnp.where(first, other, mine)], axis=1)


def body(tokens, expert_ids, gate_probs, cotangent, w_gate, w_up, w_down):
    activations, chosen, weights_two, upstream = tokens[0], expert_ids[0], gate_probs[0], cotangent[0]
    gate_local, up_local, down_local = w_gate[0], w_up[0], w_down[0]
    local = gate_local.shape[0]
    model = activations.shape[1]
    groups = lax.axis_size("expert")
    me = lax.axis_index("expert")
    experts = local * groups
    routing, weighting, slot_weight = slot_tables(
        chosen, weights_two, experts, local, CAP, me
    )
    picker = routing.T.astype(BF)
    block = (local, CAP, model)
    rows = local * CAP

    def part(array, d):
        return array[d * rows : (d + 1) * rows]

    def picked(source, d, scale):
        found = jnp.dot(part(picker, d), source, preferred_element_type=F32)
        if scale:
            found = found * part(slot_weight, d)[:, None]
        return found.astype(BF)

    def dispatch(source, scale):
        sent = [picked(source, d, scale) for d in range(groups)]
        got = [sent[0]] + [swap(sent[d], "expert", d) for d in range(1, groups)]
        return jnp.stack([g.reshape(block) for g in got], axis=1).reshape(
            local, groups * CAP, model
        )

    x = dispatch(activations, False)
    c = dispatch(upstream, True)
    gate = dot(x, gate_local, (((2,), (1,)), ((0,), (0,))))
    upper = dot(x, up_local, (((2,), (1,)), ((0,), (0,))))
    sigma = jax.nn.sigmoid(gate)
    hidden = (gate * sigma * upper).astype(BF)
    out = dot(hidden, down_local, (((2,), (1,)), ((0,), (0,)))).astype(BF)
    hidden_cot = dot(c, down_local, (((2,), (2,)), ((0,), (0,))))
    slope = sigma * (1.0 + gate * (1.0 - sigma))
    gate_cot = (hidden_cot * upper * slope).astype(BF)
    up_cot = (hidden_cot * gate * sigma).astype(BF)
    grad = dot(gate_cot, gate_local, (((2,), (2,)), ((0,), (0,))))
    grad = (grad + dot(up_cot, up_local, (((2,), (2,)), ((0,), (0,))))).astype(BF)

    high = weighting.astype(BF)
    low = (weighting - high.astype(F32)).astype(BF)

    def back(values, weighted):
        grid = values.reshape(local, groups, CAP, model)
        total = None
        for d in range(groups):
            piece = grid[:, d].reshape(rows, model)
            if d:
                piece = swap(piece, "expert", d)
            cols = slice(d * rows, (d + 1) * rows)
            if weighted:
                term = dot(
                    jnp.concatenate([high[:, cols], low[:, cols]], axis=1),
                    jnp.concatenate([piece, piece], axis=0),
                    (((1,), (0,)), ((), ())),
                )
            else:
                term = dot(picker[cols].T, piece, (((1,), (0,)), ((), ())))
            total = term if total is None else total + term
        return total.astype(BF)

    outputs = lax.psum(back(out, True), "dp")
    gradient = sum_over(back(grad, False), "dp")
    handed = swap(gradient, "section", 1)
    return (outputs[None], handed[None])


def solution(mesh):
    placed = (
        P("section", "expert", None),
        P("section", "expert", None),
        P("section", "expert", None),
        P("section", "expert", None),
        P("section", "expert", None, "dp"),
        P("section", "expert", None, "dp"),
        P("section", "expert", "dp", None),
    )
    return jax.shard_map(
        body,
        mesh=mesh,
        in_specs=placed,
        out_specs=(P("section", "expert", None), P("section", "expert", None)),
        check_vma=False,
    )
```

time: 559 us -> 355 us (0.64)
  waiting for transfers between devices: 321 us -> 175 us
  blocking collectives: 46.6 us -> 0 us
  local copies, waits for them, and re-layouts: 35.1 us -> 11.4 us
  starting transfers between devices: 15.4 us -> 34.9 us
  other arithmetic: 19.3 us -> 5.44 us
  matrix products: 106 us -> 114 us
    psum x1, waiting for transfers between devices: 249 us -> 52.6 us  [body(): outputs = lax.psum(back(out, True), 'dp')]
    ppermute x1 -> x16, waiting for transfers between devices: 2.84 us -> 122 us  [swap(): return lax.ppermute(block, axis, [(i, i ^ flip) for i in range(size)])]
    all_to_all x3 -> x0, waiting for transfers between devices: 69.4 us -> none  [the longest x1 38.6 us: body(): lax.all_to_all(slot_rows.reshape(send_shape), 'expert', split_axis=0, con...]
    all_to_all x1 -> x0, blocking collectives: 46.6 us -> none  [body(): lax.all_to_all(summed_out.astype(jnp.bfloat16), 'expert', split_axis=0, c...]
    ppermute x1 -> x16, starting transfers between devices: 0.01 us -> 34.8 us  [swap(): return lax.ppermute(block, axis, [(i, i ^ flip) for i in range(size)])]
    gather x4 -> x0, local copies, waits for them, and re-layouts: 26 us -> none  [the longest x2 13.7 us: combine(): second = jnp.take(values, slot_pair[:, 1], axis=0)]
    all_to_all x3 -> x0, starting transfers between devices: 15.1 us -> none  [the longest x1 5.29 us: body(): lax.all_to_all(slot_rows.reshape(send_shape), 'expert', split_axis=0, con...]
    reshape x2 -> x0, other arithmetic: 11.7 us -> none  [the longest x1 5.85 us: body(): expert_back.reshape(experts * capacity, model)]
  transfers between devices with their start and end apart: 5 -> 17, of which waited for: 5 -> 10; matrix products, arithmetic and copies ran while one was open for 9% -> 10% of each run, Pallas kernels for 0% -> 0%
where the time goes in v1:
time: 355 us
  waiting for transfers between devices  175 us (49%)
  matrix products  114 us (32%)
  starting transfers between devices  34.9 us (10%)
  between operations  14.3 us (4%)
  local copies, waits for them, and re-layouts  11.4 us (3%)
  other arithmetic  5.44 us (2%)
    ppermute x16, waiting for transfers between devices, swap(): return lax.ppermute(block, axis, [(i, i ^ flip) for i in range(size)])  122 us
    dot_general x14, matrix products, dot(): return lax.dot_general(a, b, dims, preferred_element_type=F32)  109 us
    psum x1, waiting for transfers between devices, body(): outputs = lax.psum(back(out, True), 'dp')  52.6 us
    ppermute x16, starting transfers between devices, swap(): return lax.ppermute(block, axis, [(i, i ^ flip) for i in range(size)])  34.8 us
  transfers between devices with their start and end apart: 17, of which 10 were waited for; matrix products, arithmetic and copies ran while one was open for 10% of the time, Pallas kernels for 0%

profile of v1, /device:TPU:0, one launch (start us, length us, event | category | flops | bytes accessed | tf_op | source)
XLA Modules:
  0.0 355.0 jit_solution(1989892274480534666)
XLA Ops:
  7.2 0.9 copy.25
  8.2 0.1 squeeze.24
  8.3 0.1 squeeze.23
  8.5 0.9 reduce-window.6
  9.4 0.2 slice_reduce_fusion
  9.8 0.1 reduce_sum.39
  10.0 0.7 multiply_add_fusion
  10.7 1.0 select_reduce_fusion
  11.8 1.8 fusion.22
  13.6 3.0 collective-permute-start.6
  16.6 0.5 fusion.23
  17.0 1.6 collective-permute-start.7
  18.6 0.5 fusion.24
  19.2 0.5 convolution_convert_fusion.2
  19.7 2.0 collective-permute-start
  21.7 0.5 convolution_convert_fusion.1
  22.2 1.6 collective-permute-start.1
  23.8 0.5 convolution_convert_fusion
  24.3 12.7 %collective-permute-done.6 = bf16[144,3072]{1,0:T(8,128)(2,1)S(1)} collective-permute-done((bf16[144,3072]{1,0:T(8,128)(2,1)S(1)}, bf16[144,3072]{1,0:T(8,128)(2,1)S(1)}, u32[]{:S(2)}, u32[]{:S(2)}) %collective-permute-start.6) | collective-permute-done | bytes 884768 | tf_op jit(solution)/shard_map/ppermute | solution.py:13
  37.0 3.0 collective-permute-start.2
  40.0 0.4 convolution_convert_fusion.3
  40.5 0.4 fusion.21
  40.9 17.8 %collective-permute-done.7 = bf16[144,3072]{1,0:T(8,128)(2,1)S(1)} collective-permute-done((bf16[144,3072]{1,0:T(8,128)(2,1)S(1)}, bf16[144,3072]{1,0:T(8,128)(2,1)S(1)}, u32[]{:S(2)}, u32[]{:S(2)}) %collective-permute-start.7) | collective-permute-done | bytes 884768 | tf_op jit(solution)/shard_map/ppermute | solution.py:13
  58.6 0.5 pad_maximum_fusion.1
  59.1 2.0 copy.29
  61.1 13.8 %collective-permute-done = bf16[144,3072]{1,0:T(8,128)(2,1)S(1)} collective-permute-done((bf16[144,3072]{1,0:T(8,128)(2,1)S(1)}, bf16[144,3072]{1,0:T(8,128)(2,1)S(1)}, u32[]{:S(2)}, u32[]{:S(2)}) %collective-permute-start) | collective-permute-done | bytes 884768 | tf_op jit(solution)/shard_map/ppermute | solution.py:13
  75.0 20.1 %collective-permute-done.1 = bf16[144,3072]{1,0:T(8,128)(2,1)S(1)} collective-permute-done((bf16[144,3072]{1,0:T(8,128)(2,1)S(1)}, bf16[144,3072]{1,0:T(8,128)(2,1)S(1)}, u32[]{:S(2)}, u32[]{:S(2)}) %collective-permute-start.1) | collective-permute-done | bytes 884768 | tf_op jit(solution)/shard_map/ppermute | solution.py:13
  95.1 0.5 pad_maximum_fusion
  95.6 0.2 copy.28
  95.8 14.2 %fusion.10 = f32[2,288,2048]{2,1,0:T(8,128)} fusion(bf16[2,288,3072]{2,1,0:T(8,128)(2,1)S(1)} %bitcast.109, bf16[1,2,3072,2048]{3,2,1,0:T(8,128)(2,1)} %param.11), kind=kOutput, calls=%fused_computation.10 | convolution fusion | flops 7247757312 | bytes 33423360 | tf_op jit(solution)/shard_map/dot_general | solution.py:37
  110.1 14.3 %fusion.6 = f32[2,288,2048]{2,1,0:T(8,128)} fusion(bf16[2,288,3072]{2,1,0:T(8,128)(2,1)S(1)} %bitcast.110, bf16[1,2,3072,2048]{3,2,1,0:T(8,128)(2,1)} %param.12), kind=kOutput, calls=%fused_computation.6 | convolution fusion | flops 7247757312 | bytes 33423360 | tf_op jit(solution)/shard_map/dot_general | solution.py:37
  124.4 15.1 %fusion = f32[2,288,2048]{2,1,0:T(8,128)} fusion(bf16[2,288,3072]{2,1,0:T(8,128)(2,1)} %bitcast.106, bf16[1,2,2048,3072]{3,2,1,0:T(8,128)(2,1)} %param.13), kind=kOutput, calls=%fused_computation | convolution fusion | flops 7247757312 | bytes 33423360 | tf_op jit(solution)/shard_map/dot_general | solution.py:37
  139.5 17.9 %fusion.4 = f32[2,288,3072]{2,1,0:T(8,128)} fusion(bf16[1,2,3072,2048]{3,2,1,0:T(8,128)(2,1)} %param.12, f32[2,288,2048]{2,1,0:T(8,128)} %fusion, f32[2,288,2048]{2,1,0:T(8,128)} %fusion.10), kind=kOutput, calls=%fused_computation.4 | convolution fusion | flops 7254835200 | bytes 41680896 | tf_op jit(solution)/shard_map/dot_general | solution.py:37
  157.5 20.5 %add_convert_fusion = bf16[2,288,3072]{2,1,0:T(8,128)(2,1)} fusion(f32[2,288,3072]{2,1,0:T(8,128)} %fusion.4, bf16[1,2,3072,2048]{3,2,1,0:T(8,128)(2,1)} %param.11, f32[2,288,2048]{2,1,0:T(8,128)} %fusion.10, f32[2,288,2048]{2,1,0:T(8,128)} %fusion, f32[2,288,2048]{2,1,0:T(8,128)} %fusion.6), kind=kOutput, calls=%fused_computation.12 | convolution fusion | flops 7263092736 | bytes 49938432 | tf_op jit(solution)/shard_map/dot_general | solution.py:37
  178.0 3.5 fusion.98
  181.5 1.5 collective-permute-start.11
  183.0 1.5 collective-permute-start.9
  184.5 0.6 collective-permute-start.10
  185.1 0.5 fusion.73
  185.5 19.8 %collective-permute-done.11 = bf16[144,3072]{1,0:T(8,128)(2,1)} collective-permute-done((bf16[144,3072]{1,0:T(8,128)(2,1)}, bf16[144,3072]{1,0:T(8,128)(2,1)}, u32[]{:S(2)}, u32[]{:S(2)}) %collective-permute-start.11) | collective-permute-done | bytes 884768 | tf_op jit(solution)/shard_map/ppermute | solution.py:13
  205.3 1.7 fusion.63
  207.0 14.9 %collective-permute-done.9 = bf16[144,3072]{1,0:T(8,128)(2,1)} collective-permute-done((bf16[144,3072]{1,0:T(8,128)(2,1)}, bf16[144,3072]{1,0:T(8,128)(2,1)}, u32[]{:S(2)}, u32[]{:S(2)}) %collective-permute-start.9) | collective-permute-done | bytes 884768 | tf_op jit(solution)/shard_map/ppermute | solution.py:13
  221.9 1.7 convolution_add_fusion.1
  223.6 0.5 fusion.20
  224.2 1.7 collective-permute-start.12
  225.9 18.1 %fusion.12 = bf16[2,288,3072]{2,1,0:T(8,128)(2,1)S(1)} fusion(bf16[1,2,2048,3072]{3,2,1,0:T(8,128)(2,1)} %param.13, f32[2,288,2048]{2,1,0:T(8,128)} %fusion.6, f32[2,288,2048]{2,1,0:T(8,128)} %fusion.10), kind=kOutput, calls=%fused_computation.17 | convolution fusion | flops 7256604672 | bytes 38141952 | tf_op jit(solution)/shard_map/dot_general | solution.py:37
  244.0 0.3 add_convert_fusion.2
  244.3 2.5 collective-permute-start.13
  246.8 0.2 fusion.99
  247.2 1.5 collective-permute-start.5
  248.6 0.3 fusion.100
  248.9 2.0 collective-permute-start.4
  250.9 8.1 %collective-permute-done.13 = bf16[192,1536]{1,0:T(8,128)(2,1)S(1)} collective-permute-done((bf16[192,1536]{1,0:T(8,128)(2,1)S(1)}, bf16[192,1536]{1,0:T(8,128)(2,1)S(1)}, u32[]{:S(2)}, u32[]{:S(2)}) %collective-permute-start.13) | collective-permute-done | bytes 589856 | tf_op jit(solution)/shard_map/ppermute | solution.py:13
  259.1 12.2 %collective-permute-start.14 = (bf16[192,1536]{1,0:T(8,128)(2,1)S(1)}, bf16[192,1536]{1,0:T(8,128)(2,1)S(1)}, u32[]{:S(2)}, u32[]{:S(2)}) collective-permute-start(bf16[192,1536]{1,0:T(8,128)(2,1)S(1)} %add_convert_fusion.1), channel_id=1, source_target_pairs={{0,4},{4,0},{8,12},{12,8},{1,5},{5,1},{9,13},{13,9},{2,6},{6,2},{1... | collective-permute-start | bytes 1769480 | tf_op jit(solution)/shard_map/ppermute | solution.py:13
  271.3 0.8 fusion.29
  272.1 14.1 %collective-permute-done.5 = bf16[144,3072]{1,0:T(8,128)(2,1)S(1)} collective-permute-done((bf16[144,3072]{1,0:T(8,128)(2,1)S(1)}, bf16[144,3072]{1,0:T(8,128)(2,1)S(1)}, u32[]{:S(2)}, u32[]{:S(2)}) %collective-permute-start.5) | collective-permute-done | bytes 884768 | tf_op jit(solution)/shard_map/ppermute | solution.py:13
  286.2 0.8 fusion.39
  287.0 0.8 convolution_add_fusion.3
  288.0 1.2 pad_maximum_fusion.2
  289.1 1.9 fusion.25
  291.0 1.2 collective-permute-done.15
  292.2 52.6 %all-reduce.2.cloned.1.call-done = bf16[1,192,3072]{2,1,0:T(8,128)(2,1)} async-done(((bf16[1,192,3072]{2,1,0:T(8,128)(2,1)}), bf16[1,192,3072]{2,1,0:T(8,128)(2,1)}) %all-reduce.2.cloned.1.call-update) | async-done | bytes 1179664 | tf_op jit(solution)/shard_map/psum | solution.py:124
  344.8 2.4 copy.32
  347.1 1.0 copy.33
  (29 shorter events, 0.9 us)
Async XLA Ops:
  7.2 12.0 %copy-start = (bf16[1,192,3072]{2,1,0:T(8,128)(2,1)S(1)}, bf16[1,192,3072]{2,1,0:T(8,128)(2,1)}, u32[]{:S(2)}) copy-start(bf16[1,192,3072]{2,1,0:T(8,128)(2,1)} %param.7) | copy-start | bytes 3538948
  7.2 9.4 %copy-start.2 = (bf16[1,192,3072]{2,1,0:T(8,128)(2,1)S(1)}, bf16[1,192,3072]{2,1,0:T(8,128)(2,1)}, u32[]{:S(2)}) copy-start(bf16[1,192,3072]{2,1,0:T(8,128)(2,1)} %param.10) | copy-start | bytes 3538948
  7.2 337.6 %all-reduce.2.cloned.1.call-start = ((), (), s32[]{:S(2)}) async-start(), calls=%async_computation | async-start | bytes 2359296 | tf_op jit(solution)/shard_map/psum | solution.py:124
  13.6 23.5 %collective-permute-start.6 = (bf16[144,3072]{1,0:T(8,128)(2,1)S(1)}, bf16[144,3072]{1,0:T(8,128)(2,1)S(1)}, u32[]{:S(2)}, u32[]{:S(2)}) collective-permute-start(bf16[144,3072]{1,0:T(8,128)(2,1)S(1)} %fusion.22), channel_id=1, source_target_pairs={{0,1},{1,0},{2,3},{3,2},{4,5},{5,4},{6,7},{7,6},{8,9},{9,8},{10,11... | collective-permute-start | bytes 2654216 | tf_op jit(solution)/shard_map/ppermute | solution.py:13
  17.0 41.6 %collective-permute-start.7 = (bf16[144,3072]{1,0:T(8,128)(2,1)S(1)}, bf16[144,3072]{1,0:T(8,128)(2,1)S(1)}, u32[]{:S(2)}, u32[]{:S(2)}) collective-permute-start(bf16[144,3072]{1,0:T(8,128)(2,1)S(1)} %fusion.23), channel_id=1, source_target_pairs={{0,2},{1,3},{2,0},{3,1},{4,6},{5,7},{6,4},{7,5},{8,10},{9,11},{10,... | collective-permute-start | bytes 2654216 | tf_op jit(solution)/shard_map/ppermute | solution.py:13
  19.1 39.5 %collective-permute-start.8 = (bf16[144,3072]{1,0:T(8,128)(2,1)S(1)}, bf16[144,3072]{1,0:T(8,128)(2,1)S(1)}, u32[]{:S(2)}, u32[]{:S(2)}) collective-permute-start(bf16[144,3072]{1,0:T(8,128)(2,1)S(1)} %fusion.24), channel_id=1, source_target_pairs={{0,3},{1,2},{2,1},{3,0},{4,7},{5,6},{6,5},{7,4},{8,11},{9,10},{10,... | collective-permute-start | bytes 2654216 | tf_op jit(solution)/shard_map/ppermute | solution.py:13
  19.7 55.3 %collective-permute-start = (bf16[144,3072]{1,0:T(8,128)(2,1)S(1)}, bf16[144,3072]{1,0:T(8,128)(2,1)S(1)}, u32[]{:S(2)}, u32[]{:S(2)}) collective-permute-start(bf16[144,3072]{1,0:T(8,128)(2,1)S(1)} %convolution_convert_fusion.2), channel_id=1, source_target_pairs={{0,1},{1,0},{2,3},{3,2},{4,5},{5,4},{6,7},{7,6},{8,9},{9,8},{10,11... | collective-permute-start | bytes 2654216 | tf_op jit(solution)/shard_map/ppermute | solution.py:13
  22.2 72.9 %collective-permute-start.1 = (bf16[144,3072]{1,0:T(8,128)(2,1)S(1)}, bf16[144,3072]{1,0:T(8,128)(2,1)S(1)}, u32[]{:S(2)}, u32[]{:S(2)}) collective-permute-start(bf16[144,3072]{1,0:T(8,128)(2,1)S(1)} %convolution_convert_fusion.1), channel_id=1, source_target_pairs={{0,2},{1,3},{2,0},{3,1},{4,6},{5,7},{6,4},{7,5},{8,10},{9,11},{10,... | collective-permute-start | bytes 2654216 | tf_op jit(solution)/shard_map/ppermute | solution.py:13
  37.0 58.1 %collective-permute-start.2 = (bf16[144,3072]{1,0:T(8,128)(2,1)S(1)}, bf16[144,3072]{1,0:T(8,128)(2,1)S(1)}, u32[]{:S(2)}, u32[]{:S(2)}) collective-permute-start(bf16[144,3072]{1,0:T(8,128)(2,1)S(1)} %convolution_convert_fusion), channel_id=1, source_target_pairs={{0,3},{1,2},{2,1},{3,0},{4,7},{5,6},{6,5},{7,4},{8,11},{9,10},{10,... | collective-permute-start | bytes 2654216 | tf_op jit(solution)/shard_map/ppermute | solution.py:13
  181.5 23.8 %collective-permute-start.11 = (bf16[144,3072]{1,0:T(8,128)(2,1)}, bf16[144,3072]{1,0:T(8,128)(2,1)}, u32[]{:S(2)}, u32[]{:S(2)}) collective-permute-start(bf16[144,3072]{1,0:T(8,128)(2,1)} %bitcast.30), channel_id=1, source_target_pairs={{0,3},{1,2},{2,1},{3,0},{4,7},{5,6},{6,5},{7,4},{8,11},{9,10},{10,... | collective-permute-start | bytes 2654216 | tf_op jit(solution)/shard_map/ppermute | solution.py:13
  183.0 39.0 %collective-permute-start.9 = (bf16[144,3072]{1,0:T(8,128)(2,1)}, bf16[144,3072]{1,0:T(8,128)(2,1)}, u32[]{:S(2)}, u32[]{:S(2)}) collective-permute-start(bf16[144,3072]{1,0:T(8,128)(2,1)} %bitcast.28), channel_id=1, source_target_pairs={{0,1},{1,0},{2,3},{3,2},{4,5},{5,4},{6,7},{7,6},{8,9},{9,8},{10,11... | collective-permute-start | bytes 2654216 | tf_op jit(solution)/shard_map/ppermute | solution.py:13
  184.5 39.1 %collective-permute-start.10 = (bf16[144,3072]{1,0:T(8,128)(2,1)S(1)}, bf16[144,3072]{1,0:T(8,128)(2,1)S(1)}, u32[]{:S(2)}, u32[]{:S(2)}) collective-permute-start(bf16[144,3072]{1,0:T(8,128)(2,1)S(1)} %bitcast.116), channel_id=1, source_target_pairs={{0,2},{1,3},{2,0},{3,1},{4,6},{5,7},{6,4},{7,5},{8,10},{9,11},{10,... | collective-permute-start | bytes 2654216 | tf_op jit(solution)/shard_map/ppermute | solution.py:13
  224.2 19.8 %collective-permute-start.12 = (bf16[192,1536]{1,0:T(8,128)(2,1)S(1)}, bf16[192,1536]{1,0:T(8,128)(2,1)S(1)}, u32[]{:S(2)}, u32[]{:S(2)}) collective-permute-start(bf16[192,1536]{1,0:T(8,128)(2,1)S(1)} %broadcast_select_fusion.2), channel_id=1, source_target_pairs={{0,4},{4,0},{8,12},{12,8},{1,5},{5,1},{9,13},{13,9},{2,6},{6,2},{1... | collective-permute-start | bytes 1769480 | tf_op jit(solution)/shard_map/ppermute | solution.py:13
  244.3 14.7 %collective-permute-start.13 = (bf16[192,1536]{1,0:T(8,128)(2,1)S(1)}, bf16[192,1536]{1,0:T(8,128)(2,1)S(1)}, u32[]{:S(2)}, u32[]{:S(2)}) collective-permute-start(bf16[192,1536]{1,0:T(8,128)(2,1)S(1)} %add_convert_fusion.2), channel_id=1, source_target_pairs={{0,12},{4,8},{8,4},{12,0},{1,13},{5,9},{9,5},{13,1},{2,14},{6,10},... | collective-permute-start | bytes 1769480 | tf_op jit(solution)/shard_map/ppermute | solution.py:13
  247.0 40.0 %collective-permute-start.3 = (bf16[144,3072]{1,0:T(8,128)(2,1)S(1)}, bf16[144,3072]{1,0:T(8,128)(2,1)S(1)}, u32[]{:S(2)}, u32[]{:S(2)}) collective-permute-start(bf16[144,3072]{1,0:T(8,128)(2,1)S(1)} %bitcast.117), channel_id=1, source_target_pairs={{0,1},{1,0},{2,3},{3,2},{4,5},{5,4},{6,7},{7,6},{8,9},{9,8},{10,11... | collective-permute-start | bytes 2654216 | tf_op jit(solution)/shard_map/ppermute | solution.py:13
  247.2 39.0 %collective-permute-start.5 = (bf16[144,3072]{1,0:T(8,128)(2,1)S(1)}, bf16[144,3072]{1,0:T(8,128)(2,1)S(1)}, u32[]{:S(2)}, u32[]{:S(2)}) collective-permute-start(bf16[144,3072]{1,0:T(8,128)(2,1)S(1)} %bitcast.121), channel_id=1, source_target_pairs={{0,3},{1,2},{2,1},{3,0},{4,7},{5,6},{6,5},{7,4},{8,11},{9,10},{10,... | collective-permute-start | bytes 2654216 | tf_op jit(solution)/shard_map/ppermute | solution.py:13
  248.9 40.2 %collective-permute-start.4 = (bf16[144,3072]{1,0:T(8,128)(2,1)S(1)}, bf16[144,3072]{1,0:T(8,128)(2,1)S(1)}, u32[]{:S(2)}, u32[]{:S(2)}) collective-permute-start(bf16[144,3072]{1,0:T(8,128)(2,1)S(1)} %bitcast.115), channel_id=1, source_target_pairs={{0,2},{1,3},{2,0},{3,1},{4,6},{5,7},{6,4},{7,5},{8,10},{9,11},{10,... | collective-permute-start | bytes 2654216 | tf_op jit(solution)/shard_map/ppermute | solution.py:13
  259.1 28.7 %collective-permute-start.14 = (bf16[192,1536]{1,0:T(8,128)(2,1)S(1)}, bf16[192,1536]{1,0:T(8,128)(2,1)S(1)}, u32[]{:S(2)}, u32[]{:S(2)}) collective-permute-start(bf16[192,1536]{1,0:T(8,128)(2,1)S(1)} %add_convert_fusion.1), channel_id=1, source_target_pairs={{0,4},{4,0},{8,12},{12,8},{1,5},{5,1},{9,13},{13,9},{2,6},{6,2},{1... | collective-permute-start | bytes 1769480 | tf_op jit(solution)/shard_map/ppermute | solution.py:13
  289.1 3.1 collective-permute-start.15
  289.1 59.0 %copy-start.1 = (bf16[1,192,3072]{2,1,0:T(8,128)(2,1)S(1)}, bf16[1,192,3072]{2,1,0:T(8,128)(2,1)}, u32[]{:S(2)}) copy-start(bf16[1,192,3072]{2,1,0:T(8,128)(2,1)} %param.7) | copy-start | bytes 3538948
Sparse Core Ops, SparseCore 0:
  291.1 53.5 all-reduce.1

commit v2 on v1

v2 whole, which is shorter than its diff:
```python
import functools

import jax
import jax.numpy as jnp
from jax import lax
from jax.experimental import pallas as pl
from jax.experimental.pallas import tpu as pltpu
from jax.sharding import PartitionSpec as P

CAP = 72
TILE = 512
CHUNKS = 3
PAIR = 896
BF = jnp.bfloat16
F32 = jnp.float32


def swap(block, axis, flip):
    size = lax.axis_size(axis)
    return lax.ppermute(block, axis, [(i, i ^ flip) for i in range(size)])


def slot_tables(chosen, weights_two, experts, local, capacity, me):
    number = chosen.shape[0]
    relative = ((chosen // local) ^ me) * local + chosen % local
    flattened = relative.reshape(-1)
    one_hot = (flattened[:, None] == jnp.arange(experts, dtype=jnp.int32)[None, :]).astype(
        jnp.int32
    )
    earlier = jnp.cumsum(one_hot, axis=0) - one_hot
    position = jnp.sum(earlier * one_hot, axis=1)
    slot_index = flattened * capacity + position
    selection = (
        slot_index[:, None] == jnp.arange(experts * capacity, dtype=jnp.int32)[None, :]
    ).astype(F32)
    selection = selection.reshape(number, 2, experts * capacity)
    routing = jnp.sum(selection, axis=1)
    weighting = jnp.sum(selection * weights_two[:, :, None], axis=1)
    slot_weight = jnp.sum(weighting, axis=0)
    return routing, weighting, slot_weight


def nn(a, b):
    return lax.dot_general(a, b, (((1,), (0,)), ((), ())), preferred_element_type=F32)


def nt(a, b):
    return lax.dot_general(a, b, (((1,), (1,)), ((), ())), preferred_element_type=F32)


def rows_of(arrays):
    return jnp.concatenate([a.astype(F32) for a in arrays], axis=0).astype(BF)


def gather_rows(half_ref, refs, x):
    own = refs[0][0]
    model = own.shape[1]
    pieces = [[r[0] for r in one] for one in refs[1]]
    if len(pieces[0]) == 1:
        x[...] = rows_of([own] + [one[0] for one in pieces])
        return
    direct = pieces[0][0].shape[1]
    width = (model - direct) // 2
    odd = half_ref[0] == 1
    x[:, :direct] = rows_of([own[:, :direct]] + [one[0] for one in pieces])
    low, high = slice(direct, direct + width), slice(direct + width, model)
    pairs = [(one[1].astype(F32), one[2].astype(F32)) for one in pieces]
    x[:, low] = rows_of([own[:, low]] + [jnp.where(odd, b, a) for a, b in pairs])
    x[:, high] = rows_of([own[:, high]] + [jnp.where(odd, a, b) for a, b in pairs])


def hand_out(acc, refs, groups):
    chunks = len(refs) // groups
    width = acc.shape[1] // chunks
    rows = acc.shape[0] // groups
    for g in range(groups):
        for k in range(chunks):
            refs[g * chunks + k][0] = acc[
                g * rows : (g + 1) * rows, k * width : (k + 1) * width
            ].astype(BF)


def grouped(refs, counts):
    found, at = [], 1
    for count in counts:
        found.append(refs[at : at + count])
        at += count
    return refs[0], found


def forward_kernel(counts, half_ref, *refs):
    groups, pieces = 1 + len(counts), 1 + sum(counts)
    wg_ref, wu_ref, wd_ref = refs[pieces : pieces + 3]
    out_refs, (p_ref, q_ref, x, acc) = refs[pieces + 3 : -4], refs[-4:]
    j = pl.program_id(1)

    @pl.when(j == 0)
    def _():
        gather_rows(half_ref, grouped(refs, counts), x)
        acc[...] = jnp.zeros_like(acc)

    gate = nn(x[...], wg_ref[0])
    upper = nn(x[...], wu_ref[0])
    sigma = jax.nn.sigmoid(gate)
    active = gate * sigma
    q_ref[0] = active.astype(BF)
    p_ref[0] = (upper * (sigma * (1.0 + gate * (1.0 - sigma)))).astype(BF)
    acc[...] += nn((active * upper).astype(BF), wd_ref[0])

    @pl.when(j == pl.num_programs(1) - 1)
    def _():
        hand_out(acc, out_refs, groups)


def backward_kernel(counts, half_ref, *refs):
    groups, pieces = 1 + len(counts), 1 + sum(counts)
    p_ref, q_ref, wg_ref, wu_ref, wd_ref = refs[pieces : pieces + 5]
    out_refs, (c, acc) = refs[pieces + 5 : -2], refs[-2:]
    j = pl.program_id(1)

    @pl.when(j == 0)
    def _():
        gather_rows(half_ref, grouped(refs, counts), c)
        acc[...] = jnp.zeros_like(acc)

    hidden_cot = nt(c[...], wd_ref[0])
    gate_cot = (hidden_cot * p_ref[0].astype(F32)).astype(BF)
    up_cot = (hidden_cot * q_ref[0].astype(F32)).astype(BF)
    acc[...] += nt(gate_cot, wg_ref[0]) + nt(up_cot, wu_ref[0])

    @pl.when(j == pl.num_programs(1) - 1)
    def _():
        hand_out(acc, out_refs, groups)


def expert_call(kernel, half, own, others, kept, weights, chunks, keep):
    counts = tuple(len(one) for one in others)
    pieces = [own] + [a for one in others for a in one]
    groups = 1 + len(others)
    local, capacity, model = own.shape
    width = weights[0].shape[2]
    tile = min(TILE, width)
    rows = groups * capacity

    def row_block(columns):
        return pl.BlockSpec((1, capacity, columns), lambda e, j: (e, 0, 0))

    wide = pl.BlockSpec((1, model, tile), lambda e, j: (e, 0, j))
    tall = pl.BlockSpec((1, tile, model), lambda e, j: (e, j, 0))
    act = pl.BlockSpec((1, rows, tile), lambda e, j: (e, 0, j))
    flops = 6 * local * rows * model * width
    return list(
        pl.pallas_call(
            functools.partial(kernel, counts),
            grid=(local, width // tile),
            in_specs=[pl.BlockSpec(memory_space=pltpu.SMEM)]
            + [row_block(a.shape[2]) for a in pieces]
            + [act] * len(kept)
            + [wide, wide, tall],
            out_specs=[row_block(model // chunks)] * (groups * chunks) + [act] * keep,
            out_shape=[jax.ShapeDtypeStruct((local, capacity, model // chunks), BF)]
            * (groups * chunks)
            + [jax.ShapeDtypeStruct((local, rows, width), BF)] * keep,
            scratch_shapes=[pltpu.VMEM((rows, model), BF), pltpu.VMEM((rows, model), F32)],
            compiler_params=pltpu.CompilerParams(vmem_limit_bytes=52 << 20),
            cost_estimate=pl.CostEstimate(
                flops=flops, bytes_accessed=6 * local * model * width, transcendentals=0
            ),
        )(half, *pieces, *kept, *weights)
    )


def sum_over(blocks, axis):
    if lax.axis_size(axis) != 4:
        return [lax.psum(one, axis) for one in blocks]
    z = lax.axis_index(axis)
    middle = (z == 1) | (z == 2)
    count = len(blocks)
    sums, totals, done = {}, {}, []
    for t in range(count + 2):
        sent = totals.get(t - 2) if t >= count else blocks[t]
        if 2 <= t < count:
            sent = jnp.where(middle, totals[t - 2], blocks[t])
        got = swap(sent, axis, 1)
        if 1 <= t <= count:
            crossed = lax.ppermute(sums[t - 1], axis, [(0, 0), (1, 2), (2, 1), (3, 3)])
            totals[t - 1] = (sums[t - 1].astype(F32) + crossed.astype(F32)).astype(BF)
        if t < count:
            sums[t] = (blocks[t].astype(F32) + got.astype(F32)).astype(BF)
        if t >= 2:
            done.append(jnp.where(middle, totals[t - 2], got))
    return done


def body(tokens, expert_ids, gate_probs, cotangent, w_gate, w_up, w_down):
    activations, chosen, weights_two, upstream = tokens[0], expert_ids[0], gate_probs[0], cotangent[0]
    weights = (w_gate[0], w_up[0], w_down[0])
    local, model = weights[0].shape[:2]
    groups = lax.axis_size("expert")
    me = lax.axis_index("expert")
    routing, weighting, slot_weight = slot_tables(
        chosen, weights_two, local * groups, local, CAP, me
    )
    picker = routing.T.astype(BF)
    rows = local * CAP
    part = [slice(d * rows, (d + 1) * rows) for d in range(groups)]

    def exchange(pieces):
        return [pieces[0]] + [swap(pieces[d], "expert", d) for d in range(1, groups)]

    def picked(d, source, scaled):
        found = nn(picker[part[d]], source)
        if scaled:
            found = found * slot_weight[part[d]][:, None]
        return found.astype(BF).reshape(local, CAP, source.shape[1])

    others = range(1, groups)
    half = lax.rem(lax.axis_index("dp"), 2)
    helped = PAIR if model > 2 * PAIR else 0
    direct = model - 2 * helped
    low, high = activations[:, direct : direct + helped], activations[:, direct + helped :]
    fetched = jnp.where(half == 1, high, low)
    near = [swap(picked(d, fetched, False), "expert", d) for d in others]
    straight = [picked(d, activations[:, :direct], False) for d in others]
    near, straight = lax.optimization_barrier((near, straight))
    straight = [swap(straight[d - 1], "expert", d) for d in others]
    far = [swap(one, "dp", 1) for one in near]
    x = [[straight[d], near[d], far[d]] for d in range(groups - 1)]
    c_sent = [picked(d, upstream, True) for d in others]
    x, c_sent = lax.optimization_barrier((x, c_sent))
    c = [[swap(c_sent[d - 1], "expert", d)] for d in others]
    chip_half = half.astype(jnp.int32).reshape(1)
    *out, p, q = expert_call(
        forward_kernel, chip_half, picked(0, activations, False), x, (), weights, 1, 2
    )
    out = exchange(out)
    grad = expert_call(
        backward_kernel, chip_half, picked(0, upstream, True), c, (p, q), weights, CHUNKS, 0
    )

    high = weighting.astype(BF)
    low = (weighting - high.astype(F32)).astype(BF)
    total = 0.0
    for d in range(groups):
        piece = out[d].reshape(rows, model)
        total = total + nn(high[:, part[d]], piece) + nn(low[:, part[d]], piece)
    total = total.astype(BF)
    wide = model // CHUNKS
    blocks = [total[:, k * wide : (k + 1) * wide] for k in range(CHUNKS)]
    later = [grad[d * CHUNKS + k] for d in range(groups) for k in range(1, CHUNKS)]
    blocks, later = lax.optimization_barrier((blocks, later))
    plain = routing.astype(BF)
    for k in range(CHUNKS):
        if k:
            pieces = exchange(later[k - 1 :: CHUNKS - 1])
        else:
            pieces = exchange(grad[0::CHUNKS])
        total = 0.0
        for d in range(groups):
            total = total + nn(plain[:, part[d]], pieces[d].reshape(rows, wide))
        blocks.append(swap(total.astype(BF), "section", 1))
    done = sum_over(blocks, "dp")
    outputs, handed = [jnp.concatenate(done[at : at + CHUNKS], axis=1) for at in (0, CHUNKS)]
    return (outputs[None], handed[None])


def solution(mesh):
    placed = (
        P("section", "expert", None),
        P("section", "expert", None),
        P("section", "expert", None),
        P("section", "expert", None),
        P("section", "expert", None, "dp"),
        P("section", "expert", None, "dp"),
        P("section", "expert", "dp", None),
    )
    return jax.shard_map(
        body,
        mesh=mesh,
        in_specs=placed,
        out_specs=(P("section", "expert", None), P("section", "expert", None)),
        check_vma=False,
    )
```

time: 355 us -> 239 us (0.67)
  waiting for transfers between devices: 175 us -> 54.2 us
  matrix products: 114 us -> 21.5 us
  Pallas kernels: 0 us -> 69.1 us
  starting transfers between devices: 34.9 us -> 77.9 us
  between operations: 14.3 us -> 1.31 us
  local copies, waits for them, and re-layouts: 11.4 us -> 5.34 us
    dot_general x22 -> x31, matrix products: 114 us -> 21.5 us  [nn(): lax.dot_general(a, b, (((1,), (0,)), ((), ())), preferred_element_type=F32)]
    pallas_call x0 -> x2, Pallas kernels: none -> 69.1 us  [expert_call(): pl.pallas_call(functools.partial(kernel, counts), grid=(local, width // t...]
    ppermute x16 -> x35, waiting for transfers between devices: 122 us -> 54.2 us  [swap(): return lax.ppermute(block, axis, [(i, i ^ flip) for i in range(size)])]
    psum x1 -> x0, waiting for transfers between devices: 52.6 us -> none  [body(): outputs = lax.psum(back(out, True), 'dp')]
    ppermute x16 -> x35, starting transfers between devices: 34.8 us -> 73.8 us  [swap(): return lax.ppermute(block, axis, [(i, i ^ flip) for i in range(size)])]
    ppermute x0 -> x6, starting transfers between devices: none -> 4.1 us  [sum_over(): crossed = lax.ppermute(sums[t - 1], axis, [(0, 0), (1, 2), (2, 1), (3, 3)])]
    slice x5 -> x3, local copies, waits for them, and re-layouts: 4.29 us -> 0.39 us  [the longest x2 3.74 us: back(): piece = grid[:, d].reshape(rows, model)]
  transfers between devices with their start and end apart: 17 -> 41, of which waited for: 10 -> 16; matrix products, arithmetic and copies ran while one was open for 10% -> 11% of each run, Pallas kernels for 0% -> 29%
where the time goes in v2:
time: 239 us; the launch traced here: 238 us
  starting transfers between devices  77.9 us (33%)
  Pallas kernels  69.1 us (29%)
  waiting for transfers between devices  54.2 us (23%)
  matrix products  21.5 us (9%)
  other arithmetic  8.95 us (4%)
  local copies, waits for them, and re-layouts  5.34 us (2%)
    ppermute x35, starting transfers between devices, swap(): return lax.ppermute(block, axis, [(i, i ^ flip) for i in range(size)])  73.8 us
    pallas_call x2, Pallas kernels, expert_call(): pl.pallas_call(functools.partial(kernel, counts), grid=(local, width // t...  69.1 us
    ppermute x35, waiting for transfers between devices, swap(): return lax.ppermute(block, axis, [(i, i ^ flip) for i in range(size)])  54.2 us
    dot_general x31, matrix products, nn(): lax.dot_general(a, b, (((1,), (0,)), ((), ())), preferred_element_type=F32)  21.5 us
  transfers between devices with their start and end apart: 41, of which 16 were waited for; matrix products, arithmetic and copies ran while one was open for 11% of the time, Pallas kernels for 29%

profile of v2, /device:TPU:0, one launch (start us, length us, event | category | flops | bytes accessed | tf_op | source)
XLA Modules:
  0.0 238.4 jit_solution(16717744139596305745)
XLA Ops:
  0.6 0.9 copy.19
  1.9 0.9 reduce-window.6
  3.3 0.7 multiply_add_fusion
  4.1 1.2 slice_select_fusion
  5.3 1.0 select_reduce_fusion.1
  6.7 3.0 %collective-permute-start.1 = (bf16[2,72,896]{2,1,0:T(8,128)(2,1)S(1)}, bf16[2,72,896]{2,1,0:T(8,128)(2,1)S(1)}, u32[]{:S(2)}, u32[]{:S(2)}) collective-permute-start(bf16[2,72,896]{2,1,0:T(8,128)(2,1)S(1)} %bitcast.142), channel_id=1, source_target_pairs={{0,2},{1,3},{2,0},{3,1},{4,6},{5,7},{6,4},{7,5},{8,10},{9,11},{10,... | collective-permute-start | bytes 774152 | tf_op jit(solution)/shard_map/ppermute | solution.py:20
  10.0 1.6 collective-permute-start
  12.4 1.4 fusion.6
  13.9 1.4 fusion.7
  15.3 1.5 fusion.8
  16.8 1.1 convolution_convert_fusion.2
  17.9 1.1 convolution_convert_fusion.1
  19.2 3.8 %collective-permute-done.2.refs_8_ = bf16[2,72,896]{2,1,0:T(8,128)(2,1)S(1)} collective-permute-done((bf16[2,72,896]{2,1,0:T(8,128)(2,1)S(1)}, bf16[2,72,896]{2,1,0:T(8,128)(2,1)S(1)}, u32[]{:S(2)}, u32[]{:S(2)}) %collective-permute-start.2) | collective-permute-done | bytes 258080 | tf_op jit(solution)/shard_map/ppermute | solution.py:20
  23.0 1.8 collective-permute-start.4
  24.8 1.3 fusion.9
  26.4 1.8 collective-permute-start.8
  28.2 1.5 collective-permute-start.3
  29.7 1.5 collective-permute-start.5
  31.2 1.0 collective-permute-done.4.refs_3_
  32.2 2.7 %collective-permute-start.7 = (bf16[2,72,1280]{2,1,0:T(8,128)(2,1)}, bf16[2,72,1280]{2,1,0:T(8,128)(2,1)}, u32[]{:S(2)}, u32[]{:S(2)}) collective-permute-start(bf16[2,72,1280]{2,1,0:T(8,128)(2,1)} %bitcast.13), channel_id=1, source_target_pairs={{0,3},{1,2},{2,1},{3,0},{4,7},{5,6},{6,5},{7,4},{8,11},{9,10},{10,... | collective-permute-start | bytes 1105928 | tf_op jit(solution)/shard_map/ppermute | solution.py:20
  34.8 1.4 convolution_convert_fusion
  36.3 1.4 collective-permute-done.6.refs_6_
  37.7 3.5 %collective-permute-done.8.refs_9_ = bf16[2,72,896]{2,1,0:T(8,128)(2,1)S(1)} collective-permute-done((bf16[2,72,896]{2,1,0:T(8,128)(2,1)S(1)}, bf16[2,72,896]{2,1,0:T(8,128)(2,1)S(1)}, u32[]{:S(2)}, u32[]{:S(2)}) %collective-permute-start.8) | collective-permute-done | bytes 258080 | tf_op jit(solution)/shard_map/ppermute | solution.py:20
  41.2 4.7 %collective-permute-done.5.refs_4_ = bf16[2,72,1280]{2,1,0:T(8,128)(2,1)} collective-permute-done((bf16[2,72,1280]{2,1,0:T(8,128)(2,1)}, bf16[2,72,1280]{2,1,0:T(8,128)(2,1)}, u32[]{:S(2)}, u32[]{:S(2)}) %collective-permute-start.5) | collective-permute-done | bytes 368672 | tf_op jit(solution)/shard_map/ppermute | solution.py:20
  45.9 1.2 collective-permute-start.12
  47.1 1.2 collective-permute-start.13
  48.3 1.1 collective-permute-start.14
  49.4 34.8 %shard_map.86 = (bf16[2,72,3072]{2,1,0:T(8,128)(2,1)}, bf16[2,72,3072]{2,1,0:T(8,128)(2,1)}, bf16[2,72,3072]{2,1,0:T(8,128)(2,1)}, bf16[2,72,3072]{2,1,0:T(8,128...) custom-call(s32[1]{0:T(128)} %bitcast.4.half_ref, bf16[2,72,3072]{2,1,0:T(8,128)(2,1)} %bitcast.131, ...), custom_call_target="tpu_custom_call" | custom-call | flops 21743271936 | bytes 75497472 | tf_op jit(solution)/shard_map/pallas_call | solution.py:153
  84.2 1.3 collective-permute-start.9
  85.5 1.2 collective-permute-start.10
  86.7 1.6 fusion.36
  88.3 1.9 convolution_add_fusion.1
  90.3 1.2 collective-permute-start.11
  91.4 0.9 copy-done.10
  92.7 34.3 %shard_map.87 = (bf16[2,72,1024]{2,1,0:T(8,128)(2,1)S(1)}, bf16[2,72,1024]{2,1,0:T(8,128)(2,1)S(1)}, bf16[2,72,1024]{2,1,0:T(8,128)(2,1)S(1)}, bf16[2,72,1024]{2...) custom-call(s32[1]{0:T(128)} %bitcast.4.half_ref, ...), custom_call_target="tpu_custom_call" | custom-call | flops 21743271936 | bytes 75497472 | tf_op jit(solution)/shard_map/pallas_call | solution.py:153
  127.0 1.4 collective-permute-start.20
  128.3 1.1 collective-permute-start.21
  129.4 1.1 collective-permute-start.22
  133.6 1.1 copy-done.3
  134.7 1.3 fusion.5
  136.2 1.4 collective-permute-start.26
  137.5 1.4 collective-permute-start.27
  139.5 4.5 %collective-permute-done.22 = bf16[2,72,1024]{2,1,0:T(8,128)(2,1)S(1)} collective-permute-done((bf16[2,72,1024]{2,1,0:T(8,128)(2,1)}, bf16[2,72,1024]{2,1,0:T(8,128)(2,1)S(1)}, u32[]{:S(2)}, u32[]{:S(2)}) %collective-permute-start.22) | collective-permute-done | bytes 294944 | tf_op jit(solution)/shard_map/ppermute | solution.py:20
  145.1 3.2 %collective-permute-start.33 = (bf16[2,72,1024]{2,1,0:T(8,128)(2,1)S(1)}, bf16[2,72,1024]{2,1,0:T(8,128)(2,1)S(1)}, u32[]{:S(2)}, u32[]{:S(2)}) collective-permute-start(bf16[2,72,1024]{2,1,0:T(8,128)(2,1)S(1)} %copy-done.13), channel_id=1, source_target_pairs={{0,2},{1,3},{2,0},{3,1},{4,6},{5,7},{6,4},{7,5},{8,10},{9,11},{10,... | collective-permute-start | bytes 884744 | tf_op jit(solution)/shard_map/ppermute | solution.py:20
  150.1 6.6 %collective-permute-done.28 = bf16[2,72,1024]{2,1,0:T(8,128)(2,1)S(1)} collective-permute-done((bf16[2,72,1024]{2,1,0:T(8,128)(2,1)S(1)}, bf16[2,72,1024]{2,1,0:T(8,128)(2,1)S(1)}, u32[]{:S(2)}, u32[]{:S(2)}) %collective-permute-start.28) | collective-permute-done | bytes 294944 | tf_op jit(solution)/shard_map/ppermute | solution.py:20
  157.0 2.1 collective-permute-start.18
  159.8 4.7 %collective-permute-done.15 = bf16[192,1024]{1,0:T(8,128)(2,1)S(1)} collective-permute-done((bf16[192,1024]{1,0:T(8,128)(2,1)S(1)}, bf16[192,1024]{1,0:T(8,128)(2,1)S(1)}, u32[]{:S(2)}, u32[]{:S(2)}) %collective-permute-start.15) | collective-permute-done | bytes 393248 | tf_op jit(solution)/shard_map/ppermute | solution.py:20
  164.6 4.1 %collective-permute-done.18 = bf16[192,1024]{1,0:T(8,128)(2,1)S(1)} collective-permute-done((bf16[192,1024]{1,0:T(8,128)(2,1)S(1)}, bf16[192,1024]{1,0:T(8,128)(2,1)S(1)}, u32[]{:S(2)}, u32[]{:S(2)}) %collective-permute-start.18) | collective-permute-done | bytes 393248 | tf_op jit(solution)/shard_map/ppermute | solution.py:20
  170.7 13.1 %collective-permute-start.17 = (bf16[192,1024]{1,0:T(8,128)(2,1)S(1)}, bf16[192,1024]{1,0:T(8,128)(2,1)S(1)}, u32[]{:S(2)}, u32[]{:S(2)}) collective-permute-start(bf16[192,1024]{1,0:T(8,128)(2,1)S(1)} %broadcast_select_fusion.9), channel_id=1, source_target_pairs={{0,4},{4,0},{8,12},{12,8},{1,5},{5,1},{9,13},{13,9},{2,6},{6,2},{1... | collective-permute-start | bytes 1179656 | tf_op jit(solution)/shard_map/ppermute | solution.py:20
  184.0 4.0 %collective-permute-start.24 = (bf16[192,1024]{1,0:T(8,128)(2,1)S(1)}, bf16[192,1024]{1,0:T(8,128)(2,1)S(1)}, u32[]{:S(2)}, u32[]{:S(2)}) collective-permute-start(bf16[192,1024]{1,0:T(8,128)(2,1)S(1)} %broadcast_select_fusion.7), channel_id=1, source_target_pairs={{0,4},{4,0},{8,12},{12,8},{1,5},{5,1},{9,13},{13,9},{2,6},{6,2},{1... | collective-permute-start | bytes 1179656 | tf_op jit(solution)/shard_map/ppermute | solution.py:20
  188.4 4.7 %collective-permute-done.17 = bf16[192,1024]{1,0:T(8,128)(2,1)S(1)} collective-permute-done((bf16[192,1024]{1,0:T(8,128)(2,1)S(1)}, bf16[192,1024]{1,0:T(8,128)(2,1)S(1)}, u32[]{:S(2)}, u32[]{:S(2)}) %collective-permute-start.17) | collective-permute-done | bytes 393248 | tf_op jit(solution)/shard_map/ppermute | solution.py:20
  193.3 0.7 collective-permute-start.25
  194.0 3.4 %collective-permute-done.24 = bf16[192,1024]{1,0:T(8,128)(2,1)S(1)} collective-permute-done((bf16[192,1024]{1,0:T(8,128)(2,1)S(1)}, bf16[192,1024]{1,0:T(8,128)(2,1)S(1)}, u32[]{:S(2)}, u32[]{:S(2)}) %collective-permute-start.24) | collective-permute-done | bytes 393248 | tf_op jit(solution)/shard_map/ppermute | solution.py:20
  197.5 0.7 collective-permute-start.31
  198.6 8.8 %collective-permute-start.30 = (bf16[192,1024]{1,0:T(8,128)(2,1)S(1)}, bf16[192,1024]{1,0:T(8,128)(2,1)S(1)}, u32[]{:S(2)}, u32[]{:S(2)}) collective-permute-start(bf16[192,1024]{1,0:T(8,128)(2,1)S(1)} %broadcast_select_fusion.5), channel_id=1, source_target_pairs={{0,4},{4,0},{8,12},{12,8},{1,5},{5,1},{9,13},{13,9},{2,6},{6,2},{1... | collective-permute-start | bytes 1179656 | tf_op jit(solution)/shard_map/ppermute | solution.py:20
  207.6 4.8 %collective-permute-start.36 = (bf16[192,1024]{1,0:T(8,128)(2,1)S(1)}, bf16[192,1024]{1,0:T(8,128)(2,1)S(1)}, u32[]{:S(2)}, u32[]{:S(2)}) collective-permute-start(bf16[192,1024]{1,0:T(8,128)(2,1)S(1)} %broadcast_select_fusion.3), channel_id=1, source_target_pairs={{0,4},{4,0},{8,12},{12,8},{1,5},{5,1},{9,13},{13,9},{2,6},{6,2},{1... | collective-permute-start | bytes 1179656 | tf_op jit(solution)/shard_map/ppermute | solution.py:20
  212.5 2.4 collective-permute-done.30
  215.7 3.8 %collective-permute-done.36 = bf16[192,1024]{1,0:T(8,128)(2,1)S(1)} collective-permute-done((bf16[192,1024]{1,0:T(8,128)(2,1)S(1)}, bf16[192,1024]{1,0:T(8,128)(2,1)S(1)}, u32[]{:S(2)}, u32[]{:S(2)}) %collective-permute-start.36) | collective-permute-done | bytes 393248 | tf_op jit(solution)/shard_map/ppermute | solution.py:20
  220.6 1.1 maximum_bitcast_fusion
  221.8 5.4 %collective-permute-start.38 = (bf16[192,1024]{1,0:T(8,128)(2,1)S(1)}, bf16[192,1024]{1,0:T(8,128)(2,1)S(1)}, u32[]{:S(2)}, u32[]{:S(2)}) collective-permute-start(bf16[192,1024]{1,0:T(8,128)(2,1)S(1)} %add_convert_fusion.2), channel_id=1, source_target_pairs={{0,4},{4,0},{8,12},{12,8},{1,5},{5,1},{9,13},{13,9},{2,6},{6,2},{1... | collective-permute-start | bytes 1179656 | tf_op jit(solution)/shard_map/ppermute | solution.py:20
  227.4 4.1 %collective-permute-start.40 = (bf16[192,1024]{1,0:T(8,128)(2,1)S(1)}, bf16[192,1024]{1,0:T(8,128)(2,1)S(1)}, u32[]{:S(2)}, u32[]{:S(2)}) collective-permute-start(bf16[192,1024]{1,0:T(8,128)(2,1)S(1)} %add_convert_fusion), channel_id=1, source_target_pairs={{0,4},{4,0},{8,12},{12,8},{1,5},{5,1},{9,13},{13,9},{2,6},{6,2},{1... | collective-permute-start | bytes 1179656 | tf_op jit(solution)/shard_map/ppermute | solution.py:20
  231.7 1.3 collective-permute-done.38
  233.0 4.2 %collective-permute-done.40 = bf16[192,1024]{1,0:T(8,128)(2,1)S(1)} collective-permute-done((bf16[192,1024]{1,0:T(8,128)(2,1)S(1)}, bf16[192,1024]{1,0:T(8,128)(2,1)S(1)}, u32[]{:S(2)}, u32[]{:S(2)}) %collective-permute-start.40) | collective-permute-done | bytes 393248 | tf_op jit(solution)/shard_map/ppermute | solution.py:20
  237.3 1.1 maximum_bitcast_fusion.1
  (123 shorter events, 16.9 us)
Async XLA Ops:
  0.6 11.8 %copy-start = (bf16[1,192,3072]{2,1,0:T(8,128)(2,1)S(1)}, bf16[1,192,3072]{2,1,0:T(8,128)(2,1)}, u32[]{:S(2)}) copy-start(bf16[1,192,3072]{2,1,0:T(8,128)(2,1)} %param.10) | copy-start | bytes 3538948
  4.0 7.9 %copy-start.2 = (bf16[1,192,3072]{2,1,0:T(8,128)(2,1)S(1)}, bf16[1,192,3072]{2,1,0:T(8,128)(2,1)}, u32[]{:S(2)}) copy-start(bf16[1,192,3072]{2,1,0:T(8,128)(2,1)} %param.7) | copy-start | bytes 3538948
  6.7 12.4 %collective-permute-start.1 = (bf16[2,72,896]{2,1,0:T(8,128)(2,1)S(1)}, bf16[2,72,896]{2,1,0:T(8,128)(2,1)S(1)}, u32[]{:S(2)}, u32[]{:S(2)}) collective-permute-start(bf16[2,72,896]{2,1,0:T(8,128)(2,1)S(1)} %bitcast.142), channel_id=1, source_target_pairs={{0,2},{1,3},{2,0},{3,1},{4,6},{5,7},{6,4},{7,5},{8,10},{9,11},{10,... | collective-permute-start | bytes 774152 | tf_op jit(solution)/shard_map/ppermute | solution.py:20
  10.0 9.2 %collective-permute-start = (bf16[2,72,896]{2,1,0:T(8,128)(2,1)S(1)}, bf16[2,72,896]{2,1,0:T(8,128)(2,1)S(1)}, u32[]{:S(2)}, u32[]{:S(2)}) collective-permute-start(bf16[2,72,896]{2,1,0:T(8,128)(2,1)S(1)} %bitcast.143), channel_id=1, source_target_pairs={{0,1},{1,0},{2,3},{3,2},{4,5},{5,4},{6,7},{7,6},{8,9},{9,8},{10,11... | collective-permute-start | bytes 774152 | tf_op jit(solution)/shard_map/ppermute | solution.py:20
  11.9 11.1 %collective-permute-start.2 = (bf16[2,72,896]{2,1,0:T(8,128)(2,1)S(1)}, bf16[2,72,896]{2,1,0:T(8,128)(2,1)S(1)}, u32[]{:S(2)}, u32[]{:S(2)}) collective-permute-start(bf16[2,72,896]{2,1,0:T(8,128)(2,1)S(1)} %bitcast.144), channel_id=1, source_target_pairs={{0,3},{1,2},{2,1},{3,0},{4,7},{5,6},{6,5},{7,4},{8,11},{9,10},{10,... | collective-permute-start | bytes 774152 | tf_op jit(solution)/shard_map/ppermute | solution.py:20
  23.0 9.2 %collective-permute-start.4 = (bf16[2,72,896]{2,1,0:T(8,128)(2,1)S(1)}, bf16[2,72,896]{2,1,0:T(8,128)(2,1)S(1)}, u32[]{:S(2)}, u32[]{:S(2)}) collective-permute-start(bf16[2,72,896]{2,1,0:T(8,128)(2,1)S(1)} %collective-permute-done.refs_2_), channel_id=1, source_target_pairs={{0,4},{4,0},{8,12},{12,8},{1,5},{5,1},{9,13},{13,9},{2,6},{6,2},{1... | collective-permute-start | bytes 774152 | tf_op jit(solution)/shard_map/ppermute | solution.py:20
  26.2 11.6 %collective-permute-start.6 = (bf16[2,72,896]{2,1,0:T(8,128)(2,1)S(1)}, bf16[2,72,896]{2,1,0:T(8,128)(2,1)S(1)}, u32[]{:S(2)}, u32[]{:S(2)}) collective-permute-start(bf16[2,72,896]{2,1,0:T(8,128)(2,1)S(1)} %collective-permute-done.1.refs_5_), channel_id=1, source_target_pairs={{0,4},{4,0},{8,12},{12,8},{1,5},{5,1},{9,13},{13,9},{2,6},{6,2},{1... | collective-permute-start | bytes 774152 | tf_op jit(solution)/shard_map/ppermute | solution.py:20
  26.4 14.8 %collective-permute-start.8 = (bf16[2,72,896]{2,1,0:T(8,128)(2,1)S(1)}, bf16[2,72,896]{2,1,0:T(8,128)(2,1)S(1)}, u32[]{:S(2)}, u32[]{:S(2)}) collective-permute-start(bf16[2,72,896]{2,1,0:T(8,128)(2,1)S(1)} %collective-permute-done.2.refs_8_), channel_id=1, source_target_pairs={{0,4},{4,0},{8,12},{12,8},{1,5},{5,1},{9,13},{13,9},{2,6},{6,2},{1... | collective-permute-start | bytes 774152 | tf_op jit(solution)/shard_map/ppermute | solution.py:20
  28.2 13.0 %collective-permute-start.3 = (bf16[2,72,1280]{2,1,0:T(8,128)(2,1)S(1)}, bf16[2,72,1280]{2,1,0:T(8,128)(2,1)S(1)}, u32[]{:S(2)}, u32[]{:S(2)}) collective-permute-start(bf16[2,72,1280]{2,1,0:T(8,128)(2,1)S(1)} %bitcast.132), channel_id=1, source_target_pairs={{0,1},{1,0},{2,3},{3,2},{4,5},{5,4},{6,7},{7,6},{8,9},{9,8},{10,11... | collective-permute-start | bytes 1105928 | tf_op jit(solution)/shard_map/ppermute | solution.py:20
  29.7 16.2 %collective-permute-start.5 = (bf16[2,72,1280]{2,1,0:T(8,128)(2,1)}, bf16[2,72,1280]{2,1,0:T(8,128)(2,1)}, u32[]{:S(2)}, u32[]{:S(2)}) collective-permute-start(bf16[2,72,1280]{2,1,0:T(8,128)(2,1)} %bitcast.12), channel_id=1, source_target_pairs={{0,2},{1,3},{2,0},{3,1},{4,6},{5,7},{6,4},{7,5},{8,10},{9,11},{10,... | collective-permute-start | bytes 1105928 | tf_op jit(solution)/shard_map/ppermute | solution.py:20
  32.2 13.7 %collective-permute-start.7 = (bf16[2,72,1280]{2,1,0:T(8,128)(2,1)}, bf16[2,72,1280]{2,1,0:T(8,128)(2,1)}, u32[]{:S(2)}, u32[]{:S(2)}) collective-permute-start(bf16[2,72,1280]{2,1,0:T(8,128)(2,1)} %bitcast.13), channel_id=1, source_target_pairs={{0,3},{1,2},{2,1},{3,0},{4,7},{5,6},{6,5},{7,4},{8,11},{9,10},{10,... | collective-permute-start | bytes 1105928 | tf_op jit(solution)/shard_map/ppermute | solution.py:20
  36.3 94.3 %copy-start.7 = (bf16[192,576]{1,0:T(8,128)(2,1)}, bf16[192,576]{1,0:T(8,128)(2,1)S(1)}, u32[]{:S(2)}) copy-start(bf16[192,576]{1,0:T(8,128)(2,1)S(1)} %get-tuple-element.99) | copy-start | bytes 663556
  36.3 94.8 %copy-start.5 = (bf16[192,576]{1,0:T(8,128)(2,1)}, bf16[192,576]{1,0:T(8,128)(2,1)S(1)}, u32[]{:S(2)}) copy-start(bf16[192,576]{1,0:T(8,128)(2,1)S(1)} %get-tuple-element.100) | copy-start | bytes 663556
  45.9 44.3 %collective-permute-start.12 = (bf16[2,72,3072]{2,1,0:T(8,128)(2,1)}, bf16[2,72,3072]{2,1,0:T(8,128)(2,1)S(1)}, u32[]{:S(2)}, u32[]{:S(2)}) collective-permute-start(bf16[2,72,3072]{2,1,0:T(8,128)(2,1)} %bitcast.130), channel_id=1, source_target_pairs={{0,1},{1,0},{2,3},{3,2},{4,5},{5,4},{6,7},{7,6},{8,9},{9,8},{10,11... | collective-permute-start | bytes 2654216 | tf_op jit(solution)/shard_map/ppermute | solution.py:20
  47.1 44.3 %collective-permute-start.13 = (bf16[2,72,3072]{2,1,0:T(8,128)(2,1)}, bf16[2,72,3072]{2,1,0:T(8,128)(2,1)S(1)}, u32[]{:S(2)}, u32[]{:S(2)}) collective-permute-start(bf16[2,72,3072]{2,1,0:T(8,128)(2,1)} %bitcast.129), channel_id=1, source_target_pairs={{0,2},{1,3},{2,0},{3,1},{4,6},{5,7},{6,4},{7,5},{8,10},{9,11},{10,... | collective-permute-start | bytes 2654216 | tf_op jit(solution)/shard_map/ppermute | solution.py:20
  48.3 43.1 %collective-permute-start.14 = (bf16[2,72,3072]{2,1,0:T(8,128)(2,1)}, bf16[2,72,3072]{2,1,0:T(8,128)(2,1)S(1)}, u32[]{:S(2)}, u32[]{:S(2)}) collective-permute-start(bf16[2,72,3072]{2,1,0:T(8,128)(2,1)} %bitcast.128), channel_id=1, source_target_pairs={{0,3},{1,2},{2,1},{3,0},{4,7},{5,6},{6,5},{7,4},{8,11},{9,10},{10,... | collective-permute-start | bytes 2654216 | tf_op jit(solution)/shard_map/ppermute | solution.py:20
  84.2 4.1 %copy-start.4 = (bf16[2,72,3072]{2,1,0:T(8,128)(2,1)S(1)}, bf16[2,72,3072]{2,1,0:T(8,128)(2,1)}, u32[]{:S(2)}) copy-start(bf16[2,72,3072]{2,1,0:T(8,128)(2,1)} %get-tuple-element.64) | copy-start | bytes 2654212
  84.2 48.9 %collective-permute-start.9 = (bf16[2,72,3072]{2,1,0:T(8,128)(2,1)}, bf16[2,72,3072]{2,1,0:T(8,128)(2,1)S(1)}, u32[]{:S(2)}, u32[]{:S(2)}) collective-permute-start(bf16[2,72,3072]{2,1,0:T(8,128)(2,1)} %get-tuple-element.65), channel_id=1, source_target_pairs={{0,1},{1,0},{2,3},{3,2},{4,5},{5,4},{6,7},{7,6},{8,9},{9,8},{10,11... | collective-permute-start | bytes 2654216 | tf_op jit(solution)/shard_map/ppermute | solution.py:20
  85.5 46.1 %collective-permute-start.10 = (bf16[2,72,3072]{2,1,0:T(8,128)(2,1)}, bf16[2,72,3072]{2,1,0:T(8,128)(2,1)S(1)}, u32[]{:S(2)}, u32[]{:S(2)}) collective-permute-start(bf16[2,72,3072]{2,1,0:T(8,128)(2,1)} %get-tuple-element.66), channel_id=1, source_target_pairs={{0,2},{1,3},{2,0},{3,1},{4,6},{5,7},{6,4},{7,5},{8,10},{9,11},{10,... | collective-permute-start | bytes 2654216 | tf_op jit(solution)/shard_map/ppermute | solution.py:20
  88.3 1.9 copy-start.12
  90.2 1.2 copy-start.9
  90.3 39.2 %collective-permute-start.11 = (bf16[2,72,3072]{2,1,0:T(8,128)(2,1)S(1)}, bf16[2,72,3072]{2,1,0:T(8,128)(2,1)S(1)}, u32[]{:S(2)}, u32[]{:S(2)}) collective-permute-start(bf16[2,72,3072]{2,1,0:T(8,128)(2,1)S(1)} %copy-done.12), channel_id=1, source_target_pairs={{0,3},{1,2},{2,1},{3,0},{4,7},{5,6},{6,5},{7,4},{8,11},{9,10},{10,... | collective-permute-start | bytes 2654216 | tf_op jit(solution)/shard_map/ppermute | solution.py:20
  91.4 0.9 copy-start.10
  91.4 1.3 copy-start.11
  127.0 18.1 %collective-permute-start.20 = (bf16[2,72,1024]{2,1,0:T(8,128)(2,1)S(1)}, bf16[2,72,1024]{2,1,0:T(8,128)(2,1)S(1)}, u32[]{:S(2)}, u32[]{:S(2)}) collective-permute-start(bf16[2,72,1024]{2,1,0:T(8,128)(2,1)S(1)} %get-tuple-element.85), channel_id=1, source_target_pairs={{0,1},{1,0},{2,3},{3,2},{4,5},{5,4},{6,7},{7,6},{8,9},{9,8},{10,11... | collective-permute-start | bytes 884744 | tf_op jit(solution)/shard_map/ppermute | solution.py:20
  128.3 16.0 %collective-permute-start.21 = (bf16[2,72,1024]{2,1,0:T(8,128)(2,1)}, bf16[2,72,1024]{2,1,0:T(8,128)(2,1)S(1)}, u32[]{:S(2)}, u32[]{:S(2)}) collective-permute-start(bf16[2,72,1024]{2,1,0:T(8,128)(2,1)} %get-tuple-element.86), channel_id=1, source_target_pairs={{0,2},{1,3},{2,0},{3,1},{4,6},{5,7},{6,4},{7,5},{8,10},{9,11},{10,... | collective-permute-start | bytes 884744 | tf_op jit(solution)/shard_map/ppermute | solution.py:20
  129.4 14.6 %collective-permute-start.22 = (bf16[2,72,1024]{2,1,0:T(8,128)(2,1)}, bf16[2,72,1024]{2,1,0:T(8,128)(2,1)S(1)}, u32[]{:S(2)}, u32[]{:S(2)}) collective-permute-start(bf16[2,72,1024]{2,1,0:T(8,128)(2,1)} %get-tuple-element.87), channel_id=1, source_target_pairs={{0,3},{1,2},{2,1},{3,0},{4,7},{5,6},{6,5},{7,4},{8,11},{9,10},{10,... | collective-permute-start | bytes 884744 | tf_op jit(solution)/shard_map/ppermute | solution.py:20
  131.1 0.9 copy-start.8
  131.6 1.0 copy-start.6
  133.1 1.7 copy-start.3
  136.0 1.5 copy-start.15
  136.2 7.8 %copy-start.16 = (bf16[2,72,1024]{2,1,0:T(8,128)(2,1)S(1)}, bf16[2,72,1024]{2,1,0:T(8,128)(2,1)}, u32[]{:S(2)}) copy-start(bf16[2,72,1024]{2,1,0:T(8,128)(2,1)} %get-tuple-element.91) | copy-start | bytes 884740
  136.2 12.7 %collective-permute-start.26 = (bf16[2,72,1024]{2,1,0:T(8,128)(2,1)S(1)}, bf16[2,72,1024]{2,1,0:T(8,128)(2,1)S(1)}, u32[]{:S(2)}, u32[]{:S(2)}) collective-permute-start(bf16[2,72,1024]{2,1,0:T(8,128)(2,1)S(1)} %get-tuple-element.89), channel_id=1, source_target_pairs={{0,1},{1,0},{2,3},{3,2},{4,5},{5,4},{6,7},{7,6},{8,9},{9,8},{10,11... | collective-permute-start | bytes 884744 | tf_op jit(solution)/shard_map/ppermute | solution.py:20
  137.5 19.5 %collective-permute-start.27 = (bf16[2,72,1024]{2,1,0:T(8,128)(2,1)S(1)}, bf16[2,72,1024]{2,1,0:T(8,128)(2,1)S(1)}, u32[]{:S(2)}, u32[]{:S(2)}) collective-permute-start(bf16[2,72,1024]{2,1,0:T(8,128)(2,1)S(1)} %copy-done.15), channel_id=1, source_target_pairs={{0,2},{1,3},{2,0},{3,1},{4,6},{5,7},{6,4},{7,5},{8,10},{9,11},{10,... | collective-permute-start | bytes 884744 | tf_op jit(solution)/shard_map/ppermute | solution.py:20
  139.2 5.9 %copy-start.13 = (bf16[2,72,1024]{2,1,0:T(8,128)(2,1)S(1)}, bf16[2,72,1024]{2,1,0:T(8,128)(2,1)}, u32[]{:S(2)}) copy-start(bf16[2,72,1024]{2,1,0:T(8,128)(2,1)} %get-tuple-element.94) | copy-start | bytes 884740
  144.0 12.7 %collective-permute-start.28 = (bf16[2,72,1024]{2,1,0:T(8,128)(2,1)S(1)}, bf16[2,72,1024]{2,1,0:T(8,128)(2,1)S(1)}, u32[]{:S(2)}, u32[]{:S(2)}) collective-permute-start(bf16[2,72,1024]{2,1,0:T(8,128)(2,1)S(1)} %copy-done.16), channel_id=1, source_target_pairs={{0,3},{1,2},{2,1},{3,0},{4,7},{5,6},{6,5},{7,4},{8,11},{9,10},{10,... | collective-permute-start | bytes 884744 | tf_op jit(solution)/shard_map/ppermute | solution.py:20
  144.3 15.1 %collective-permute-start.32 = (bf16[2,72,1024]{2,1,0:T(8,128)(2,1)S(1)}, bf16[2,72,1024]{2,1,0:T(8,128)(2,1)S(1)}, u32[]{:S(2)}, u32[]{:S(2)}) collective-permute-start(bf16[2,72,1024]{2,1,0:T(8,128)(2,1)S(1)} %get-tuple-element.93), channel_id=1, source_target_pairs={{0,1},{1,0},{2,3},{3,2},{4,5},{5,4},{6,7},{7,6},{8,9},{9,8},{10,11... | collective-permute-start | bytes 884744 | tf_op jit(solution)/shard_map/ppermute | solution.py:20
  145.1 43.0 %collective-permute-start.33 = (bf16[2,72,1024]{2,1,0:T(8,128)(2,1)S(1)}, bf16[2,72,1024]{2,1,0:T(8,128)(2,1)S(1)}, u32[]{:S(2)}, u32[]{:S(2)}) collective-permute-start(bf16[2,72,1024]{2,1,0:T(8,128)(2,1)S(1)} %copy-done.13), channel_id=1, source_target_pairs={{0,2},{1,3},{2,0},{3,1},{4,6},{5,7},{6,4},{7,5},{8,10},{9,11},{10,... | collective-permute-start | bytes 884744 | tf_op jit(solution)/shard_map/ppermute | solution.py:20
  148.6 1.0 copy-start.14
  149.5 20.0 %collective-permute-start.34 = (bf16[2,72,1024]{2,1,0:T(8,128)(2,1)S(1)}, bf16[2,72,1024]{2,1,0:T(8,128)(2,1)S(1)}, u32[]{:S(2)}, u32[]{:S(2)}) collective-permute-start(bf16[2,72,1024]{2,1,0:T(8,128)(2,1)S(1)} %copy-done.14), channel_id=1, source_target_pairs={{0,3},{1,2},{2,1},{3,0},{4,7},{5,6},{6,5},{7,4},{8,11},{9,10},{10,... | collective-permute-start | bytes 884744 | tf_op jit(solution)/shard_map/ppermute | solution.py:20
  156.7 7.8 %collective-permute-start.15 = (bf16[192,1024]{1,0:T(8,128)(2,1)S(1)}, bf16[192,1024]{1,0:T(8,128)(2,1)S(1)}, u32[]{:S(2)}, u32[]{:S(2)}) collective-permute-start(bf16[192,1024]{1,0:T(8,128)(2,1)S(1)} %get-tuple-element.81), channel_id=1, source_target_pairs={{0,4},{4,0},{8,12},{12,8},{1,5},{5,1},{9,13},{13,9},{2,6},{6,2},{1... | collective-permute-start | bytes 1179656 | tf_op jit(solution)/shard_map/ppermute | solution.py:20
  157.0 11.7 %collective-permute-start.18 = (bf16[192,1024]{1,0:T(8,128)(2,1)S(1)}, bf16[192,1024]{1,0:T(8,128)(2,1)S(1)}, u32[]{:S(2)}, u32[]{:S(2)}) collective-permute-start(bf16[192,1024]{1,0:T(8,128)(2,1)S(1)} %get-tuple-element.83), channel_id=1, source_target_pairs={{0,4},{4,0},{8,12},{12,8},{1,5},{5,1},{9,13},{13,9},{2,6},{6,2},{1... | collective-permute-start | bytes 1179656 | tf_op jit(solution)/shard_map/ppermute | solution.py:20
  159.4 24.4 %collective-permute-start.23 = (bf16[192,1024]{1,0:T(8,128)(2,1)S(1)}, bf16[192,1024]{1,0:T(8,128)(2,1)S(1)}, u32[]{:S(2)}, u32[]{:S(2)}) collective-permute-start(bf16[192,1024]{1,0:T(8,128)(2,1)S(1)} %fusion.16), channel_id=1, source_target_pairs={{0,16},{16,0},{1,17},{17,1},{2,18},{18,2},{3,19},{19,3},{4,20},{20... | collective-permute-start | bytes 1179656 | tf_op jit(solution)/shard_map/ppermute | solution.py:20
  164.5 33.9 %collective-permute-start.29 = (bf16[192,1024]{1,0:T(8,128)(2,1)S(1)}, bf16[192,1024]{1,0:T(8,128)(2,1)S(1)}, u32[]{:S(2)}, u32[]{:S(2)}) collective-permute-start(bf16[192,1024]{1,0:T(8,128)(2,1)S(1)} %fusion.14), channel_id=1, source_target_pairs={{0,16},{16,0},{1,17},{17,1},{2,18},{18,2},{3,19},{19,3},{4,20},{20... | collective-permute-start | bytes 1179656 | tf_op jit(solution)/shard_map/ppermute | solution.py:20
  168.7 1.8 collective-permute-start.16
  169.5 14.3 %collective-permute-start.19 = (bf16[192,1024]{1,0:T(8,128)(2,1)S(1)}, bf16[192,1024]{1,0:T(8,128)(2,1)S(1)}, u32[]{:S(2)}, u32[]{:S(2)}) collective-permute-start(bf16[192,1024]{1,0:T(8,128)(2,1)S(1)} %add_convert_fusion.9), channel_id=1, source_target_pairs={{0,0},{4,8},{8,4},{12,12},{1,1},{5,9},{9,5},{13,13},{2,2},{6,10},{... | collective-permute-start | bytes 1179656 | tf_op jit(solution)/shard_map/ppermute | solution.py:186
  170.7 22.4 %collective-permute-start.17 = (bf16[192,1024]{1,0:T(8,128)(2,1)S(1)}, bf16[192,1024]{1,0:T(8,128)(2,1)S(1)}, u32[]{:S(2)}, u32[]{:S(2)}) collective-permute-start(bf16[192,1024]{1,0:T(8,128)(2,1)S(1)} %broadcast_select_fusion.9), channel_id=1, source_target_pairs={{0,4},{4,0},{8,12},{12,8},{1,5},{5,1},{9,13},{13,9},{2,6},{6,2},{1... | collective-permute-start | bytes 1179656 | tf_op jit(solution)/shard_map/ppermute | solution.py:20
  184.0 13.3 %collective-permute-start.24 = (bf16[192,1024]{1,0:T(8,128)(2,1)S(1)}, bf16[192,1024]{1,0:T(8,128)(2,1)S(1)}, u32[]{:S(2)}, u32[]{:S(2)}) collective-permute-start(bf16[192,1024]{1,0:T(8,128)(2,1)S(1)} %broadcast_select_fusion.7), channel_id=1, source_target_pairs={{0,4},{4,0},{8,12},{12,8},{1,5},{5,1},{9,13},{13,9},{2,6},{6,2},{1... | collective-permute-start | bytes 1179656 | tf_op jit(solution)/shard_map/ppermute | solution.py:20
  188.4 19.0 %collective-permute-start.35 = (bf16[192,1024]{1,0:T(8,128)(2,1)S(1)}, bf16[192,1024]{1,0:T(8,128)(2,1)S(1)}, u32[]{:S(2)}, u32[]{:S(2)}) collective-permute-start(bf16[192,1024]{1,0:T(8,128)(2,1)S(1)} %fusion.15), channel_id=1, source_target_pairs={{0,16},{16,0},{1,17},{17,1},{2,18},{18,2},{3,19},{19,3},{4,20},{20... | collective-permute-start | bytes 1179656 | tf_op jit(solution)/shard_map/ppermute | solution.py:20
  193.3 5.1 %collective-permute-start.25 = (bf16[192,1024]{1,0:T(8,128)(2,1)S(1)}, bf16[192,1024]{1,0:T(8,128)(2,1)S(1)}, u32[]{:S(2)}, u32[]{:S(2)}) collective-permute-start(bf16[192,1024]{1,0:T(8,128)(2,1)S(1)} %add_convert_fusion.7), channel_id=1, source_target_pairs={{0,0},{4,8},{8,4},{12,12},{1,1},{5,9},{9,5},{13,13},{2,2},{6,10},{... | collective-permute-start | bytes 1179656 | tf_op jit(solution)/shard_map/ppermute | solution.py:186
  197.5 9.9 %collective-permute-start.31 = (bf16[192,1024]{1,0:T(8,128)(2,1)S(1)}, bf16[192,1024]{1,0:T(8,128)(2,1)S(1)}, u32[]{:S(2)}, u32[]{:S(2)}) collective-permute-start(bf16[192,1024]{1,0:T(8,128)(2,1)S(1)} %add_convert_fusion.5), channel_id=1, source_target_pairs={{0,0},{4,8},{8,4},{12,12},{1,1},{5,9},{9,5},{13,13},{2,2},{6,10},{... | collective-permute-start | bytes 1179656 | tf_op jit(solution)/shard_map/ppermute | solution.py:186
  198.6 16.3 %collective-permute-start.30 = (bf16[192,1024]{1,0:T(8,128)(2,1)S(1)}, bf16[192,1024]{1,0:T(8,128)(2,1)S(1)}, u32[]{:S(2)}, u32[]{:S(2)}) collective-permute-start(bf16[192,1024]{1,0:T(8,128)(2,1)S(1)} %broadcast_select_fusion.5), channel_id=1, source_target_pairs={{0,4},{4,0},{8,12},{12,8},{1,5},{5,1},{9,13},{13,9},{2,6},{6,2},{1... | collective-permute-start | bytes 1179656 | tf_op jit(solution)/shard_map/ppermute | solution.py:20
  207.6 12.0 %collective-permute-start.36 = (bf16[192,1024]{1,0:T(8,128)(2,1)S(1)}, bf16[192,1024]{1,0:T(8,128)(2,1)S(1)}, u32[]{:S(2)}, u32[]{:S(2)}) collective-permute-start(bf16[192,1024]{1,0:T(8,128)(2,1)S(1)} %broadcast_select_fusion.3), channel_id=1, source_target_pairs={{0,4},{4,0},{8,12},{12,8},{1,5},{5,1},{9,13},{13,9},{2,6},{6,2},{1... | collective-permute-start | bytes 1179656 | tf_op jit(solution)/shard_map/ppermute | solution.py:20
  215.0 6.6 %collective-permute-start.37 = (bf16[192,1024]{1,0:T(8,128)(2,1)S(1)}, bf16[192,1024]{1,0:T(8,128)(2,1)S(1)}, u32[]{:S(2)}, u32[]{:S(2)}) collective-permute-start(bf16[192,1024]{1,0:T(8,128)(2,1)S(1)} %add_convert_fusion.3), channel_id=1, source_target_pairs={{0,0},{4,8},{8,4},{12,12},{1,1},{5,9},{9,5},{13,13},{2,2},{6,10},{... | collective-permute-start | bytes 1179656 | tf_op jit(solution)/shard_map/ppermute | solution.py:186
  219.7 7.6 %collective-permute-start.39 = (bf16[192,1024]{1,0:T(8,128)(2,1)S(1)}, bf16[192,1024]{1,0:T(8,128)(2,1)S(1)}, u32[]{:S(2)}, u32[]{:S(2)}) collective-permute-start(bf16[192,1024]{1,0:T(8,128)(2,1)S(1)} %add_convert_fusion.1), channel_id=1, source_target_pairs={{0,0},{4,8},{8,4},{12,12},{1,1},{5,9},{9,5},{13,13},{2,2},{6,10},{... | collective-permute-start | bytes 1179656 | tf_op jit(solution)/shard_map/ppermute | solution.py:186
  221.8 11.2 %collective-permute-start.38 = (bf16[192,1024]{1,0:T(8,128)(2,1)S(1)}, bf16[192,1024]{1,0:T(8,128)(2,1)S(1)}, u32[]{:S(2)}, u32[]{:S(2)}) collective-permute-start(bf16[192,1024]{1,0:T(8,128)(2,1)S(1)} %add_convert_fusion.2), channel_id=1, source_target_pairs={{0,4},{4,0},{8,12},{12,8},{1,5},{5,1},{9,13},{13,9},{2,6},{6,2},{1... | collective-permute-start | bytes 1179656 | tf_op jit(solution)/shard_map/ppermute | solution.py:20
  227.4 9.8 %collective-permute-start.40 = (bf16[192,1024]{1,0:T(8,128)(2,1)S(1)}, bf16[192,1024]{1,0:T(8,128)(2,1)S(1)}, u32[]{:S(2)}, u32[]{:S(2)}) collective-permute-start(bf16[192,1024]{1,0:T(8,128)(2,1)S(1)} %add_convert_fusion), channel_id=1, source_target_pairs={{0,4},{4,0},{8,12},{12,8},{1,5},{5,1},{9,13},{13,9},{2,6},{6,2},{1... | collective-permute-start | bytes 1179656 | tf_op jit(solution)/shard_map/ppermute | solution.py:20
  233.0 5.4 %copy-start.1 = (bf16[1,192,3072]{2,1,0:T(8,128)(2,1)S(1)}, bf16[1,192,3072]{2,1,0:T(8,128)(2,1)}, u32[]{:S(2)}) copy-start(bf16[1,192,3072]{2,1,0:T(8,128)(2,1)} %param.10) | copy-start | bytes 3538948

commit v3 on v2

--- a/solution.py
+++ b/solution.py
@@ -170,12 +170,13 @@
     )
 
 
-def sum_over(blocks, axis):
+def sum_over(blocks, count, axis, supply):
     if lax.axis_size(axis) != 4:
+        for t in range(count):
+            supply(t, blocks[0])
         return [lax.psum(one, axis) for one in blocks]
     z = lax.axis_index(axis)
     middle = (z == 1) | (z == 2)
-    count = len(blocks)
     sums, totals, done = {}, {}, []
     for t in range(count + 2):
         sent = totals.get(t - 2) if t >= count else blocks[t]
@@ -184,9 +185,11 @@
         got = swap(sent, axis, 1)
         if 1 <= t <= count:
             crossed = lax.ppermute(sums[t - 1], axis, [(0, 0), (1, 2), (2, 1), (3, 3)])
+            got, crossed = lax.optimization_barrier((got, crossed))
             totals[t - 1] = (sums[t - 1].astype(F32) + crossed.astype(F32)).astype(BF)
         if t < count:
             sums[t] = (blocks[t].astype(F32) + got.astype(F32)).astype(BF)
+            sums[t] = supply(t, sums[t])
         if t >= 2:
             done.append(jnp.where(middle, totals[t - 2], got))
     return done
@@ -222,12 +225,12 @@
     fetched = jnp.where(half == 1, high, low)
     near = [swap(picked(d, fetched, False), "expert", d) for d in others]
     straight = [picked(d, activations[:, :direct], False) for d in others]
-    near, straight = lax.optimization_barrier((near, straight))
     straight = [swap(straight[d - 1], "expert", d) for d in others]
     far = [swap(one, "dp", 1) for one in near]
     x = [[straight[d], near[d], far[d]] for d in range(groups - 1)]
     c_sent = [picked(d, upstream, True) for d in others]
-    x, c_sent = lax.optimization_barrier((x, c_sent))
+    c_own = picked(0, upstream, True)
+    x, c_sent, c_own = lax.optimization_barrier((x, c_sent, c_own))
     c = [[swap(c_sent[d - 1], "expert", d)] for d in others]
     chip_half = half.astype(jnp.int32).reshape(1)
     *out, p, q = expert_call(
@@ -235,9 +238,10 @@
     )
     out = exchange(out)
     grad = expert_call(
-        backward_kernel, chip_half, picked(0, upstream, True), c, (p, q), weights, CHUNKS, 0
-    )
-
+        backward_kernel, chip_half, c_own, c, (p, q), weights, CHUNKS, 0
+    )
+
+    out[0], grad[0] = lax.optimization_barrier((out[0], grad[0]))
     high = weighting.astype(BF)
     low = (weighting - high.astype(F32)).astype(BF)
     total = 0.0
@@ -247,20 +251,29 @@
     total = total.astype(BF)
     wide = model // CHUNKS
     blocks = [total[:, k * wide : (k + 1) * wide] for k in range(CHUNKS)]
-    later = [grad[d * CHUNKS + k] for d in range(groups) for k in range(1, CHUNKS)]
-    blocks, later = lax.optimization_barrier((blocks, later))
     plain = routing.astype(BF)
-    for k in range(CHUNKS):
-        if k:
-            pieces = exchange(later[k - 1 :: CHUNKS - 1])
-        else:
-            pieces = exchange(grad[0::CHUNKS])
-        total = 0.0
-        for d in range(groups):
-            total = total + nn(plain[:, part[d]], pieces[d].reshape(rows, wide))
-        blocks.append(swap(total.astype(BF), "section", 1))
-    done = sum_over(blocks, "dp")
-    outputs, handed = [jnp.concatenate(done[at : at + CHUNKS], axis=1) for at in (0, CHUNKS)]
+
+    travelling = exchange(grad[0::CHUNKS])
+
+    def supply(t, arrived):
+        nonlocal travelling
+        if t < CHUNKS:
+            pieces, following, arrived = lax.optimization_barrier(
+                (travelling, grad[t + 1 :: CHUNKS] if t + 1 < CHUNKS else [], arrived)
+            )
+            total = 0.0
+            for d in range(groups):
+                total = total + nn(plain[:, part[d]], pieces[d].reshape(rows, wide))
+            blocks.append(swap(total.astype(BF), "section", 1))
+            if following:
+                travelling = exchange(following)
+        return arrived
+
+    done = sum_over(blocks, 2 * CHUNKS, "dp", supply)
+    outputs, handed = [
+        jnp.concatenate(done[:CHUNKS], axis=1),
+        jnp.concatenate(done[CHUNKS:], axis=1),
+    ]
     return (outputs[None], handed[None])
 
 

time: 239 us -> 228 us (0.954)
  starting transfers between devices: 77.9 us -> 60.4 us
  waiting for transfers between devices: 54.2 us -> 65.8 us
  matrix products: 21.5 us -> 16.1 us
    ppermute x35, starting transfers between devices: 73.8 us -> 56.4 us  [swap(): return lax.ppermute(block, axis, [(i, i ^ flip) for i in range(size)])]
    ppermute x35, waiting for transfers between devices: 54.2 us -> 65.8 us  [swap(): return lax.ppermute(block, axis, [(i, i ^ flip) for i in range(size)])]
    dot_general x31, matrix products: 21.5 us -> 16.1 us  [nn(): lax.dot_general(a, b, (((1,), (0,)), ((), ())), preferred_element_type=F32)]
  transfers between devices with their start and end apart: 41 -> 41, of which waited for: 16 -> 14; matrix products, arithmetic and copies ran while one was open for 11% -> 8% of each run, Pallas kernels for 29% -> 30%
where the time goes in v3:
time: 228 us; the launch traced here: 227 us
  Pallas kernels  69.1 us (30%)
  waiting for transfers between devices  65.8 us (29%)
  starting transfers between devices  60.4 us (26%)
  matrix products  16.1 us (7%)
  other arithmetic  9.93 us (4%)
  local copies, waits for them, and re-layouts  4.51 us (2%)
    pallas_call x2, Pallas kernels, expert_call(): pl.pallas_call(functools.partial(kernel, counts), grid=(local, width // t...  69.1 us
    ppermute x35, waiting for transfers between devices, swap(): return lax.ppermute(block, axis, [(i, i ^ flip) for i in range(size)])  65.8 us
    ppermute x35, starting transfers between devices, swap(): return lax.ppermute(block, axis, [(i, i ^ flip) for i in range(size)])  56.4 us
    dot_general x31, matrix products, nn(): lax.dot_general(a, b, (((1,), (0,)), ((), ())), preferred_element_type=F32)  16.1 us
  transfers between devices with their start and end apart: 41, of which 14 were waited for; matrix products, arithmetic and copies ran while one was open for 8% of the time, Pallas kernels for 30%

profile of v3, /device:TPU:0, one launch (start us, length us, event | category | flops | bytes accessed | tf_op | source)
XLA Modules:
  0.0 227.2 jit_solution(7495009988436043551)
XLA Ops:
  0.6 0.9 copy.19
  1.9 0.9 reduce-window.6
  3.3 0.7 multiply_add_fusion
  4.1 1.2 slice_select_fusion
  5.3 1.0 select_reduce_fusion
  6.7 3.0 %collective-permute-start.4 = (bf16[2,72,896]{2,1,0:T(8,128)(2,1)S(1)}, bf16[2,72,896]{2,1,0:T(8,128)(2,1)S(1)}, u32[]{:S(2)}, u32[]{:S(2)}) collective-permute-start(bf16[2,72,896]{2,1,0:T(8,128)(2,1)S(1)} %bitcast.144), channel_id=1, source_target_pairs={{0,2},{1,3},{2,0},{3,1},{4,6},{5,7},{6,4},{7,5},{8,10},{9,11},{10,... | collective-permute-start | bytes 774152 | tf_op jit(solution)/shard_map/ppermute | solution.py:20
  10.0 1.5 collective-permute-start.7
  12.4 2.0 collective-permute-start
  14.7 1.6 collective-permute-start.3
  17.9 1.3 fusion.9
  19.6 2.7 %collective-permute-done.4.refs_5_ = bf16[2,72,896]{2,1,0:T(8,128)(2,1)S(1)} collective-permute-done((bf16[2,72,896]{2,1,0:T(8,128)(2,1)S(1)}, bf16[2,72,896]{2,1,0:T(8,128)(2,1)S(1)}, u32[]{:S(2)}, u32[]{:S(2)}) %collective-permute-start.4) | collective-permute-done | bytes 258080 | tf_op jit(solution)/shard_map/ppermute | solution.py:20
  22.3 3.0 %collective-permute-start.6 = (bf16[2,72,1280]{2,1,0:T(8,128)(2,1)S(1)}, bf16[2,72,1280]{2,1,0:T(8,128)(2,1)S(1)}, u32[]{:S(2)}, u32[]{:S(2)}) collective-permute-start(bf16[2,72,1280]{2,1,0:T(8,128)(2,1)S(1)} %bitcast.134), channel_id=1, source_target_pairs={{0,3},{1,2},{2,1},{3,0},{4,7},{5,6},{6,5},{7,4},{8,11},{9,10},{10,... | collective-permute-start | bytes 1105928 | tf_op jit(solution)/shard_map/ppermute | solution.py:20
  25.2 1.6 collective-permute-start.5
  27.3 4.8 %collective-permute-done.refs_1_ = bf16[2,72,1280]{2,1,0:T(8,128)(2,1)S(1)} collective-permute-done((bf16[2,72,1280]{2,1,0:T(8,128)(2,1)S(1)}, bf16[2,72,1280]{2,1,0:T(8,128)(2,1)S(1)}, u32[]{:S(2)}, u32[]{:S(2)}) %collective-permute-start) | collective-permute-done | bytes 368672 | tf_op jit(solution)/shard_map/ppermute | solution.py:20
  32.1 2.1 collective-permute-start.2
  34.2 1.3 convolution_convert_fusion
  35.6 4.4 %collective-permute-done.6.refs_7_ = bf16[2,72,1280]{2,1,0:T(8,128)(2,1)S(1)} collective-permute-done((bf16[2,72,1280]{2,1,0:T(8,128)(2,1)S(1)}, bf16[2,72,1280]{2,1,0:T(8,128)(2,1)S(1)}, u32[]{:S(2)}, u32[]{:S(2)}) %collective-permute-start.6) | collective-permute-done | bytes 368672 | tf_op jit(solution)/shard_map/ppermute | solution.py:20
  40.0 1.9 collective-permute-done.2.refs_3_
  42.0 0.5 collective-permute-start.9
  42.5 0.6 collective-permute-start.10
  43.1 2.4 %collective-permute-start.11 = (bf16[2,72,3072]{2,1,0:T(8,128)(2,1)S(1)}, bf16[2,72,3072]{2,1,0:T(8,128)(2,1)S(1)}, u32[]{:S(2)}, u32[]{:S(2)}) collective-permute-start(bf16[2,72,3072]{2,1,0:T(8,128)(2,1)S(1)} %bitcast.128), channel_id=1, source_target_pairs={{0,3},{1,2},{2,1},{3,0},{4,7},{5,6},{6,5},{7,4},{8,11},{9,10},{10,... | collective-permute-start | bytes 2654216 | tf_op jit(solution)/shard_map/ppermute | solution.py:20
  45.5 34.8 %shard_map.86 = (bf16[2,72,3072]{2,1,0:T(8,128)(2,1)}, bf16[2,72,3072]{2,1,0:T(8,128)(2,1)}, bf16[2,72,3072]{2,1,0:T(8,128)(2,1)}, bf16[2,72,3072]{2,1,0:T(8,128...) custom-call(s32[1]{0:T(128)} %bitcast.half_ref, bf16[2,72,3072]{2,1,0:T(8,128)(2,1)} %bitcast.131, ...), custom_call_target="tpu_custom_call" | custom-call | flops 21743271936 | bytes 75497472 | tf_op jit(solution)/shard_map/pallas_call | solution.py:153
  80.2 0.6 collective-permute-start.15
  80.8 0.6 collective-permute-start.16
  81.4 2.4 %collective-permute-start.17 = (bf16[2,72,3072]{2,1,0:T(8,128)(2,1)}, bf16[2,72,3072]{2,1,0:T(8,128)(2,1)S(1)}, u32[]{:S(2)}, u32[]{:S(2)}) collective-permute-start(bf16[2,72,3072]{2,1,0:T(8,128)(2,1)} %get-tuple-element.98), channel_id=1, source_target_pairs={{0,3},{1,2},{2,1},{3,0},{4,7},{5,6},{6,5},{7,4},{8,11},{9,10},{10,... | collective-permute-start | bytes 2654216 | tf_op jit(solution)/shard_map/ppermute | solution.py:20
  83.8 1.0 copy-done.5
  85.0 34.3 %shard_map.87 = (bf16[2,72,1024]{2,1,0:T(8,128)(2,1)S(1)}, bf16[2,72,1024]{2,1,0:T(8,128)(2,1)S(1)}, bf16[2,72,1024]{2,1,0:T(8,128)(2,1)S(1)}, bf16[2,72,1024]{2...) custom-call(s32[1]{0:T(128)} %bitcast.half_ref, ...), custom_call_target="tpu_custom_call" | custom-call | flops 21743271936 | bytes 75497472 | tf_op jit(solution)/shard_map/pallas_call | solution.py:153
  122.0 0.6 copy-done.3
  123.6 1.0 fusion.5
  124.6 0.9 fusion.75
  125.5 1.6 collective-permute-start.18
  128.0 2.6 %collective-permute-start.14 = (bf16[2,72,1024]{2,1,0:T(8,128)(2,1)}, bf16[2,72,1024]{2,1,0:T(8,128)(2,1)}, u32[]{:S(2)}, u32[]{:S(2)}) collective-permute-start(bf16[2,72,1024]{2,1,0:T(8,128)(2,1)} %get-tuple-element.90), channel_id=1, source_target_pairs={{0,3},{1,2},{2,1},{3,0},{4,7},{5,6},{6,5},{7,4},{8,11},{9,10},{10,... | collective-permute-start | bytes 884744 | tf_op jit(solution)/shard_map/ppermute | solution.py:20
  131.0 5.1 %collective-permute-done.18 = bf16[192,1024]{1,0:T(8,128)(2,1)} collective-permute-done((bf16[192,1024]{1,0:T(8,128)(2,1)}, bf16[192,1024]{1,0:T(8,128)(2,1)}, u32[]{:S(2)}, u32[]{:S(2)}) %collective-permute-start.18) | collective-permute-done | bytes 393248 | tf_op jit(solution)/shard_map/ppermute | solution.py:20
  136.1 1.1 add_convert_fusion.11
  137.3 1.9 collective-permute-done.13
  139.2 2.1 collective-permute-start.22
  141.3 0.8 collective-permute-start.23
  142.1 0.7 collective-permute-start.24
  142.7 0.7 collective-permute-start.20
  143.4 1.3 fusion.46
  145.3 1.3 fusion.10
  146.8 4.3 %collective-permute-done.23 = bf16[2,72,1024]{2,1,0:T(8,128)(2,1)S(1)} collective-permute-done((bf16[2,72,1024]{2,1,0:T(8,128)(2,1)}, bf16[2,72,1024]{2,1,0:T(8,128)(2,1)S(1)}, u32[]{:S(2)}, u32[]{:S(2)}) %collective-permute-start.23) | collective-permute-done | bytes 294944 | tf_op jit(solution)/shard_map/ppermute | solution.py:20
  151.0 1.4 collective-permute-done.24
  152.4 1.9 collective-permute-start.28
  154.5 1.4 collective-permute-start.30
  156.1 1.5 collective-permute-start.21
  157.6 0.7 collective-permute-start.25
  159.5 4.5 %collective-permute-done.21 = bf16[192,1024]{1,0:T(8,128)(2,1)S(1)} collective-permute-done((bf16[192,1024]{1,0:T(8,128)(2,1)S(1)}, bf16[192,1024]{1,0:T(8,128)(2,1)S(1)}, u32[]{:S(2)}, u32[]{:S(2)}) %collective-permute-start.21) | collective-permute-done | bytes 393248 | tf_op jit(solution)/shard_map/ppermute | solution.py:20
  164.7 0.7 collective-permute-start.31
  165.9 6.3 %collective-permute-start.27 = (bf16[192,1024]{1,0:T(8,128)(2,1)S(1)}, bf16[192,1024]{1,0:T(8,128)(2,1)S(1)}, u32[]{:S(2)}, u32[]{:S(2)}) collective-permute-start(bf16[192,1024]{1,0:T(8,128)(2,1)S(1)} %broadcast_select_fusion.7), channel_id=1, source_target_pairs={{0,4},{4,0},{8,12},{12,8},{1,5},{5,1},{9,13},{13,9},{2,6},{6,2},{1... | collective-permute-start | bytes 1179656 | tf_op jit(solution)/shard_map/ppermute | solution.py:20
  172.8 8.9 %collective-permute-done.27 = bf16[192,1024]{1,0:T(8,128)(2,1)S(1)} collective-permute-done((bf16[192,1024]{1,0:T(8,128)(2,1)S(1)}, bf16[192,1024]{1,0:T(8,128)(2,1)S(1)}, u32[]{:S(2)}, u32[]{:S(2)}) %collective-permute-start.27) | collective-permute-done | bytes 393248 | tf_op jit(solution)/shard_map/ppermute | solution.py:20
  181.9 1.8 collective-permute-start.33
  183.9 0.7 collective-permute-start.34
  185.0 7.8 %collective-permute-done.33 = bf16[192,1024]{1,0:T(8,128)(2,1)S(1)} collective-permute-done((bf16[192,1024]{1,0:T(8,128)(2,1)S(1)}, bf16[192,1024]{1,0:T(8,128)(2,1)S(1)}, u32[]{:S(2)}, u32[]{:S(2)}) %collective-permute-start.33) | collective-permute-done | bytes 393248 | tf_op jit(solution)/shard_map/ppermute | solution.py:20
  193.0 3.8 %collective-permute-start.36 = (bf16[192,1024]{1,0:T(8,128)(2,1)S(1)}, bf16[192,1024]{1,0:T(8,128)(2,1)S(1)}, u32[]{:S(2)}, u32[]{:S(2)}) collective-permute-start(bf16[192,1024]{1,0:T(8,128)(2,1)S(1)} %broadcast_select_fusion.3), channel_id=1, source_target_pairs={{0,4},{4,0},{8,12},{12,8},{1,5},{5,1},{9,13},{13,9},{2,6},{6,2},{1... | collective-permute-start | bytes 1179656 | tf_op jit(solution)/shard_map/ppermute | solution.py:20
  196.9 0.7 collective-permute-start.37
  198.0 6.6 %collective-permute-done.36 = bf16[192,1024]{1,0:T(8,128)(2,1)S(1)} collective-permute-done((bf16[192,1024]{1,0:T(8,128)(2,1)S(1)}, bf16[192,1024]{1,0:T(8,128)(2,1)S(1)}, u32[]{:S(2)}, u32[]{:S(2)}) %collective-permute-start.36) | collective-permute-done | bytes 393248 | tf_op jit(solution)/shard_map/ppermute | solution.py:20
  204.9 0.7 collective-permute-start.39
  205.6 5.4 %collective-permute-start.38 = (bf16[192,1024]{1,0:T(8,128)(2,1)S(1)}, bf16[192,1024]{1,0:T(8,128)(2,1)S(1)}, u32[]{:S(2)}, u32[]{:S(2)}) collective-permute-start(bf16[192,1024]{1,0:T(8,128)(2,1)S(1)} %add_convert_fusion.2), channel_id=1, source_target_pairs={{0,4},{4,0},{8,12},{12,8},{1,5},{5,1},{9,13},{13,9},{2,6},{6,2},{1... | collective-permute-start | bytes 1179656 | tf_op jit(solution)/shard_map/ppermute | solution.py:20
  211.2 1.1 maximum_bitcast_fusion
  212.3 5.8 %collective-permute-done.38 = bf16[192,1024]{1,0:T(8,128)(2,1)S(1)} collective-permute-done((bf16[192,1024]{1,0:T(8,128)(2,1)S(1)}, bf16[192,1024]{1,0:T(8,128)(2,1)S(1)}, u32[]{:S(2)}, u32[]{:S(2)}) %collective-permute-start.38) | collective-permute-done | bytes 393248 | tf_op jit(solution)/shard_map/ppermute | solution.py:20
  218.2 2.0 collective-permute-start.40
  220.5 5.6 %collective-permute-done.40 = bf16[192,1024]{1,0:T(8,128)(2,1)S(1)} collective-permute-done((bf16[192,1024]{1,0:T(8,128)(2,1)S(1)}, bf16[192,1024]{1,0:T(8,128)(2,1)S(1)}, u32[]{:S(2)}, u32[]{:S(2)}) %collective-permute-start.40) | collective-permute-done | bytes 393248 | tf_op jit(solution)/shard_map/ppermute | solution.py:20
  226.1 1.1 maximum_bitcast_fusion.1
  (111 shorter events, 16.6 us)
Async XLA Ops:
  0.6 15.8 %copy-start = (bf16[1,192,3072]{2,1,0:T(8,128)(2,1)S(1)}, bf16[1,192,3072]{2,1,0:T(8,128)(2,1)}, u32[]{:S(2)}) copy-start(bf16[1,192,3072]{2,1,0:T(8,128)(2,1)} %param.10) | copy-start | bytes 3538948
  4.0 7.9 %copy-start.2 = (bf16[1,192,3072]{2,1,0:T(8,128)(2,1)S(1)}, bf16[1,192,3072]{2,1,0:T(8,128)(2,1)}, u32[]{:S(2)}) copy-start(bf16[1,192,3072]{2,1,0:T(8,128)(2,1)} %param.7) | copy-start | bytes 3538948
  6.7 15.6 %collective-permute-start.4 = (bf16[2,72,896]{2,1,0:T(8,128)(2,1)S(1)}, bf16[2,72,896]{2,1,0:T(8,128)(2,1)S(1)}, u32[]{:S(2)}, u32[]{:S(2)}) collective-permute-start(bf16[2,72,896]{2,1,0:T(8,128)(2,1)S(1)} %bitcast.144), channel_id=1, source_target_pairs={{0,2},{1,3},{2,0},{3,1},{4,6},{5,7},{6,4},{7,5},{8,10},{9,11},{10,... | collective-permute-start | bytes 774152 | tf_op jit(solution)/shard_map/ppermute | solution.py:20
  10.0 15.2 %collective-permute-start.7 = (bf16[2,72,896]{2,1,0:T(8,128)(2,1)S(1)}, bf16[2,72,896]{2,1,0:T(8,128)(2,1)S(1)}, u32[]{:S(2)}, u32[]{:S(2)}) collective-permute-start(bf16[2,72,896]{2,1,0:T(8,128)(2,1)S(1)} %bitcast.143), channel_id=1, source_target_pairs={{0,3},{1,2},{2,1},{3,0},{4,7},{5,6},{6,5},{7,4},{8,11},{9,10},{10,... | collective-permute-start | bytes 774152 | tf_op jit(solution)/shard_map/ppermute | solution.py:20
  11.9 15.0 %collective-permute-start.1 = (bf16[2,72,896]{2,1,0:T(8,128)(2,1)S(1)}, bf16[2,72,896]{2,1,0:T(8,128)(2,1)S(1)}, u32[]{:S(2)}, u32[]{:S(2)}) collective-permute-start(bf16[2,72,896]{2,1,0:T(8,128)(2,1)S(1)} %bitcast.142), channel_id=1, source_target_pairs={{0,1},{1,0},{2,3},{3,2},{4,5},{5,4},{6,7},{7,6},{8,9},{9,8},{10,11... | collective-permute-start | bytes 774152 | tf_op jit(solution)/shard_map/ppermute | solution.py:20
  12.4 19.7 %collective-permute-start = (bf16[2,72,1280]{2,1,0:T(8,128)(2,1)S(1)}, bf16[2,72,1280]{2,1,0:T(8,128)(2,1)S(1)}, u32[]{:S(2)}, u32[]{:S(2)}) collective-permute-start(bf16[2,72,1280]{2,1,0:T(8,128)(2,1)S(1)} %bitcast.133), channel_id=1, source_target_pairs={{0,1},{1,0},{2,3},{3,2},{4,5},{5,4},{6,7},{7,6},{8,9},{9,8},{10,11... | collective-permute-start | bytes 1105928 | tf_op jit(solution)/shard_map/ppermute | solution.py:20
  14.7 20.8 %collective-permute-start.3 = (bf16[2,72,1280]{2,1,0:T(8,128)(2,1)S(1)}, bf16[2,72,1280]{2,1,0:T(8,128)(2,1)S(1)}, u32[]{:S(2)}, u32[]{:S(2)}) collective-permute-start(bf16[2,72,1280]{2,1,0:T(8,128)(2,1)S(1)} %bitcast.132), channel_id=1, source_target_pairs={{0,2},{1,3},{2,0},{3,1},{4,6},{5,7},{6,4},{7,5},{8,10},{9,11},{10,... | collective-permute-start | bytes 1105928 | tf_op jit(solution)/shard_map/ppermute | solution.py:20
  22.3 17.8 %collective-permute-start.6 = (bf16[2,72,1280]{2,1,0:T(8,128)(2,1)S(1)}, bf16[2,72,1280]{2,1,0:T(8,128)(2,1)S(1)}, u32[]{:S(2)}, u32[]{:S(2)}) collective-permute-start(bf16[2,72,1280]{2,1,0:T(8,128)(2,1)S(1)} %bitcast.134), channel_id=1, source_target_pairs={{0,3},{1,2},{2,1},{3,0},{4,7},{5,6},{6,5},{7,4},{8,11},{9,10},{10,... | collective-permute-start | bytes 1105928 | tf_op jit(solution)/shard_map/ppermute | solution.py:20
  25.2 14.8 %collective-permute-start.5 = (bf16[2,72,896]{2,1,0:T(8,128)(2,1)S(1)}, bf16[2,72,896]{2,1,0:T(8,128)(2,1)S(1)}, u32[]{:S(2)}, u32[]{:S(2)}) collective-permute-start(bf16[2,72,896]{2,1,0:T(8,128)(2,1)S(1)} %collective-permute-done.4.refs_5_), channel_id=1, source_target_pairs={{0,4},{4,0},{8,12},{12,8},{1,5},{5,1},{9,13},{13,9},{2,6},{6,2},{1... | collective-permute-start | bytes 774152 | tf_op jit(solution)/shard_map/ppermute | solution.py:20
  26.8 13.2 %collective-permute-start.8 = (bf16[2,72,896]{2,1,0:T(8,128)(2,1)S(1)}, bf16[2,72,896]{2,1,0:T(8,128)(2,1)S(1)}, u32[]{:S(2)}, u32[]{:S(2)}) collective-permute-start(bf16[2,72,896]{2,1,0:T(8,128)(2,1)S(1)} %collective-permute-done.7.refs_8_), channel_id=1, source_target_pairs={{0,4},{4,0},{8,12},{12,8},{1,5},{5,1},{9,13},{13,9},{2,6},{6,2},{1... | collective-permute-start | bytes 774152 | tf_op jit(solution)/shard_map/ppermute | solution.py:20
  32.1 9.9 %collective-permute-start.2 = (bf16[2,72,896]{2,1,0:T(8,128)(2,1)S(1)}, bf16[2,72,896]{2,1,0:T(8,128)(2,1)S(1)}, u32[]{:S(2)}, u32[]{:S(2)}) collective-permute-start(bf16[2,72,896]{2,1,0:T(8,128)(2,1)S(1)} %collective-permute-done.1.refs_2_), channel_id=1, source_target_pairs={{0,4},{4,0},{8,12},{12,8},{1,5},{5,1},{9,13},{13,9},{2,6},{6,2},{1... | collective-permute-start | bytes 774152 | tf_op jit(solution)/shard_map/ppermute | solution.py:20
  35.6 9.9 %copy-start.7 = (bf16[2,72,1280]{2,1,0:T(8,128)(2,1)}, bf16[2,72,1280]{2,1,0:T(8,128)(2,1)S(1)}, u32[]{:S(2)}) copy-start(bf16[2,72,1280]{2,1,0:T(8,128)(2,1)S(1)} %collective-permute-done.3.refs_4_) | copy-start | bytes 1105924
  40.0 5.4 %copy-start.8 = (bf16[2,72,1280]{2,1,0:T(8,128)(2,1)}, bf16[2,72,1280]{2,1,0:T(8,128)(2,1)S(1)}, u32[]{:S(2)}) copy-start(bf16[2,72,1280]{2,1,0:T(8,128)(2,1)S(1)} %collective-permute-done.6.refs_7_) | copy-start | bytes 1105924
  42.0 39.5 %collective-permute-start.9 = (bf16[2,72,3072]{2,1,0:T(8,128)(2,1)S(1)}, bf16[2,72,3072]{2,1,0:T(8,128)(2,1)S(1)}, u32[]{:S(2)}, u32[]{:S(2)}) collective-permute-start(bf16[2,72,3072]{2,1,0:T(8,128)(2,1)S(1)} %bitcast.130), channel_id=1, source_target_pairs={{0,1},{1,0},{2,3},{3,2},{4,5},{5,4},{6,7},{7,6},{8,9},{9,8},{10,11... | collective-permute-start | bytes 2654216 | tf_op jit(solution)/shard_map/ppermute | solution.py:20
  42.5 41.3 %collective-permute-start.10 = (bf16[2,72,3072]{2,1,0:T(8,128)(2,1)S(1)}, bf16[2,72,3072]{2,1,0:T(8,128)(2,1)S(1)}, u32[]{:S(2)}, u32[]{:S(2)}) collective-permute-start(bf16[2,72,3072]{2,1,0:T(8,128)(2,1)S(1)} %bitcast.129), channel_id=1, source_target_pairs={{0,2},{1,3},{2,0},{3,1},{4,6},{5,7},{6,4},{7,5},{8,10},{9,11},{10,... | collective-permute-start | bytes 2654216 | tf_op jit(solution)/shard_map/ppermute | solution.py:20
  43.1 40.7 %collective-permute-start.11 = (bf16[2,72,3072]{2,1,0:T(8,128)(2,1)S(1)}, bf16[2,72,3072]{2,1,0:T(8,128)(2,1)S(1)}, u32[]{:S(2)}, u32[]{:S(2)}) collective-permute-start(bf16[2,72,3072]{2,1,0:T(8,128)(2,1)S(1)} %bitcast.128), channel_id=1, source_target_pairs={{0,3},{1,2},{2,1},{3,0},{4,7},{5,6},{6,5},{7,4},{8,11},{9,10},{10,... | collective-permute-start | bytes 2654216 | tf_op jit(solution)/shard_map/ppermute | solution.py:20
  80.2 41.2 %collective-permute-start.15 = (bf16[2,72,3072]{2,1,0:T(8,128)(2,1)}, bf16[2,72,3072]{2,1,0:T(8,128)(2,1)S(1)}, u32[]{:S(2)}, u32[]{:S(2)}) collective-permute-start(bf16[2,72,3072]{2,1,0:T(8,128)(2,1)} %get-tuple-element.96), channel_id=1, source_target_pairs={{0,1},{1,0},{2,3},{3,2},{4,5},{5,4},{6,7},{7,6},{8,9},{9,8},{10,11... | collective-permute-start | bytes 2654216 | tf_op jit(solution)/shard_map/ppermute | solution.py:20
  80.8 39.6 %collective-permute-start.16 = (bf16[2,72,3072]{2,1,0:T(8,128)(2,1)}, bf16[2,72,3072]{2,1,0:T(8,128)(2,1)S(1)}, u32[]{:S(2)}, u32[]{:S(2)}) collective-permute-start(bf16[2,72,3072]{2,1,0:T(8,128)(2,1)} %get-tuple-element.97), channel_id=1, source_target_pairs={{0,2},{1,3},{2,0},{3,1},{4,6},{5,7},{6,4},{7,5},{8,10},{9,11},{10,... | collective-permute-start | bytes 2654216 | tf_op jit(solution)/shard_map/ppermute | solution.py:20
  81.4 2.4 %copy-start.4 = (bf16[2,72,3072]{2,1,0:T(8,128)(2,1)}, bf16[2,72,3072]{2,1,0:T(8,128)(2,1)S(1)}, u32[]{:S(2)}) copy-start(bf16[2,72,3072]{2,1,0:T(8,128)(2,1)S(1)} %collective-permute-done.9.refs_1_) | copy-start | bytes 2654212
  81.4 37.9 %collective-permute-start.17 = (bf16[2,72,3072]{2,1,0:T(8,128)(2,1)}, bf16[2,72,3072]{2,1,0:T(8,128)(2,1)S(1)}, u32[]{:S(2)}, u32[]{:S(2)}) collective-permute-start(bf16[2,72,3072]{2,1,0:T(8,128)(2,1)} %get-tuple-element.98), channel_id=1, source_target_pairs={{0,3},{1,2},{2,1},{3,0},{4,7},{5,6},{6,5},{7,4},{8,11},{9,10},{10,... | collective-permute-start | bytes 2654216 | tf_op jit(solution)/shard_map/ppermute | solution.py:20
  83.8 1.0 copy-start.5
  83.8 1.2 copy-start.6
  121.4 1.2 copy-start.3
  125.5 10.6 %collective-permute-start.18 = (bf16[192,1024]{1,0:T(8,128)(2,1)}, bf16[192,1024]{1,0:T(8,128)(2,1)}, u32[]{:S(2)}, u32[]{:S(2)}) collective-permute-start(bf16[192,1024]{1,0:T(8,128)(2,1)} %get-tuple-element.144), channel_id=1, source_target_pairs={{0,4},{4,0},{8,12},{12,8},{1,5},{5,1},{9,13},{13,9},{2,6},{6,2},{1... | collective-permute-start | bytes 1179656 | tf_op jit(solution)/shard_map/ppermute | solution.py:20
  127.1 10.2 %collective-permute-start.12 = (bf16[2,72,1024]{2,1,0:T(8,128)(2,1)S(1)}, bf16[2,72,1024]{2,1,0:T(8,128)(2,1)}, u32[]{:S(2)}, u32[]{:S(2)}) collective-permute-start(bf16[2,72,1024]{2,1,0:T(8,128)(2,1)S(1)} %get-tuple-element.88), channel_id=1, source_target_pairs={{0,1},{1,0},{2,3},{3,2},{4,5},{5,4},{6,7},{7,6},{8,9},{9,8},{10,11... | collective-permute-start | bytes 884744 | tf_op jit(solution)/shard_map/ppermute | solution.py:20
  127.6 11.6 %collective-permute-start.13 = (bf16[2,72,1024]{2,1,0:T(8,128)(2,1)}, bf16[2,72,1024]{2,1,0:T(8,128)(2,1)S(1)}, u32[]{:S(2)}, u32[]{:S(2)}) collective-permute-start(bf16[2,72,1024]{2,1,0:T(8,128)(2,1)} %get-tuple-element.89), channel_id=1, source_target_pairs={{0,2},{1,3},{2,0},{3,1},{4,6},{5,7},{6,4},{7,5},{8,10},{9,11},{10,... | collective-permute-start | bytes 884744 | tf_op jit(solution)/shard_map/ppermute | solution.py:20
  128.0 11.2 %collective-permute-start.14 = (bf16[2,72,1024]{2,1,0:T(8,128)(2,1)}, bf16[2,72,1024]{2,1,0:T(8,128)(2,1)}, u32[]{:S(2)}, u32[]{:S(2)}) collective-permute-start(bf16[2,72,1024]{2,1,0:T(8,128)(2,1)} %get-tuple-element.90), channel_id=1, source_target_pairs={{0,3},{1,2},{2,1},{3,0},{4,7},{5,6},{6,5},{7,4},{8,11},{9,10},{10,... | collective-permute-start | bytes 884744 | tf_op jit(solution)/shard_map/ppermute | solution.py:20
  130.6 16.0 %collective-permute-start.19 = (bf16[192,1024]{1,0:T(8,128)(2,1)}, bf16[192,1024]{1,0:T(8,128)(2,1)S(1)}, u32[]{:S(2)}, u32[]{:S(2)}) collective-permute-start(bf16[192,1024]{1,0:T(8,128)(2,1)} %get-tuple-element.143), channel_id=1, source_target_pairs={{0,4},{4,0},{8,12},{12,8},{1,5},{5,1},{9,13},{13,9},{2,6},{6,2},{1... | collective-permute-start | bytes 1179656 | tf_op jit(solution)/shard_map/ppermute | solution.py:20
  139.2 7.6 %collective-permute-start.22 = (bf16[2,72,1024]{2,1,0:T(8,128)(2,1)S(1)}, bf16[2,72,1024]{2,1,0:T(8,128)(2,1)S(1)}, u32[]{:S(2)}, u32[]{:S(2)}) collective-permute-start(bf16[2,72,1024]{2,1,0:T(8,128)(2,1)S(1)} %get-tuple-element.102), channel_id=1, source_target_pairs={{0,1},{1,0},{2,3},{3,2},{4,5},{5,4},{6,7},{7,6},{8,9},{9,8},{10,11... | collective-permute-start | bytes 884744 | tf_op jit(solution)/shard_map/ppermute | solution.py:20
  141.3 9.8 %collective-permute-start.23 = (bf16[2,72,1024]{2,1,0:T(8,128)(2,1)}, bf16[2,72,1024]{2,1,0:T(8,128)(2,1)S(1)}, u32[]{:S(2)}, u32[]{:S(2)}) collective-permute-start(bf16[2,72,1024]{2,1,0:T(8,128)(2,1)} %get-tuple-element.103), channel_id=1, source_target_pairs={{0,2},{1,3},{2,0},{3,1},{4,6},{5,7},{6,4},{7,5},{8,10},{9,11},{10,... | collective-permute-start | bytes 884744 | tf_op jit(solution)/shard_map/ppermute | solution.py:20
  142.1 10.4 %collective-permute-start.24 = (bf16[2,72,1024]{2,1,0:T(8,128)(2,1)}, bf16[2,72,1024]{2,1,0:T(8,128)(2,1)S(1)}, u32[]{:S(2)}, u32[]{:S(2)}) collective-permute-start(bf16[2,72,1024]{2,1,0:T(8,128)(2,1)} %get-tuple-element.104), channel_id=1, source_target_pairs={{0,3},{1,2},{2,1},{3,0},{4,7},{5,6},{6,5},{7,4},{8,11},{9,10},{10,... | collective-permute-start | bytes 884744 | tf_op jit(solution)/shard_map/ppermute | solution.py:20
  142.7 3.9 %collective-permute-start.20 = (bf16[192,1024]{1,0:T(8,128)(2,1)S(1)}, bf16[192,1024]{1,0:T(8,128)(2,1)S(1)}, u32[]{:S(2)}, u32[]{:S(2)}) collective-permute-start(bf16[192,1024]{1,0:T(8,128)(2,1)S(1)} %add_convert_fusion.11), channel_id=1, source_target_pairs={{0,0},{4,8},{8,4},{12,12},{1,1},{5,9},{9,5},{13,13},{2,2},{6,10},{... | collective-permute-start | bytes 1179656 | tf_op jit(solution)/shard_map/ppermute | solution.py:187
  145.2 9.1 %copy-start.10 = (bf16[2,72,1024]{2,1,0:T(8,128)(2,1)S(1)}, bf16[2,72,1024]{2,1,0:T(8,128)(2,1)}, u32[]{:S(2)}) copy-start(bf16[2,72,1024]{2,1,0:T(8,128)(2,1)} %get-tuple-element.119) | copy-start | bytes 884740
  145.3 9.3 %copy-start.9 = (bf16[2,72,1024]{2,1,0:T(8,128)(2,1)S(1)}, bf16[2,72,1024]{2,1,0:T(8,128)(2,1)}, u32[]{:S(2)}) copy-start(bf16[2,72,1024]{2,1,0:T(8,128)(2,1)} %get-tuple-element.120) | copy-start | bytes 884740
  152.4 12.2 %collective-permute-start.28 = (bf16[2,72,1024]{2,1,0:T(8,128)(2,1)S(1)}, bf16[2,72,1024]{2,1,0:T(8,128)(2,1)S(1)}, u32[]{:S(2)}, u32[]{:S(2)}) collective-permute-start(bf16[2,72,1024]{2,1,0:T(8,128)(2,1)S(1)} %get-tuple-element.118), channel_id=1, source_target_pairs={{0,1},{1,0},{2,3},{3,2},{4,5},{5,4},{6,7},{7,6},{8,9},{9,8},{10,11... | collective-permute-start | bytes 884744 | tf_op jit(solution)/shard_map/ppermute | solution.py:20
  154.3 10.3 %collective-permute-start.29 = (bf16[2,72,1024]{2,1,0:T(8,128)(2,1)S(1)}, bf16[2,72,1024]{2,1,0:T(8,128)(2,1)S(1)}, u32[]{:S(2)}, u32[]{:S(2)}) collective-permute-start(bf16[2,72,1024]{2,1,0:T(8,128)(2,1)S(1)} %copy-done.10), channel_id=1, source_target_pairs={{0,2},{1,3},{2,0},{3,1},{4,6},{5,7},{6,4},{7,5},{8,10},{9,11},{10,... | collective-permute-start | bytes 884744 | tf_op jit(solution)/shard_map/ppermute | solution.py:20
  154.5 10.1 %collective-permute-start.30 = (bf16[2,72,1024]{2,1,0:T(8,128)(2,1)S(1)}, bf16[2,72,1024]{2,1,0:T(8,128)(2,1)S(1)}, u32[]{:S(2)}, u32[]{:S(2)}) collective-permute-start(bf16[2,72,1024]{2,1,0:T(8,128)(2,1)S(1)} %copy-done.9), channel_id=1, source_target_pairs={{0,3},{1,2},{2,1},{3,0},{4,7},{5,6},{6,5},{7,4},{8,11},{9,10},{10,... | collective-permute-start | bytes 884744 | tf_op jit(solution)/shard_map/ppermute | solution.py:20
  156.1 7.8 %collective-permute-start.21 = (bf16[192,1024]{1,0:T(8,128)(2,1)S(1)}, bf16[192,1024]{1,0:T(8,128)(2,1)S(1)}, u32[]{:S(2)}, u32[]{:S(2)}) collective-permute-start(bf16[192,1024]{1,0:T(8,128)(2,1)S(1)} %broadcast_select_fusion.9), channel_id=1, source_target_pairs={{0,4},{4,0},{8,12},{12,8},{1,5},{5,1},{9,13},{13,9},{2,6},{6,2},{1... | collective-permute-start | bytes 1179656 | tf_op jit(solution)/shard_map/ppermute | solution.py:20
  157.6 6.4 %collective-permute-start.25 = (bf16[192,1024]{1,0:T(8,128)(2,1)S(1)}, bf16[192,1024]{1,0:T(8,128)(2,1)S(1)}, u32[]{:S(2)}, u32[]{:S(2)}) collective-permute-start(bf16[192,1024]{1,0:T(8,128)(2,1)S(1)} %add_convert_fusion.9), channel_id=1, source_target_pairs={{0,0},{4,8},{8,4},{12,12},{1,1},{5,9},{9,5},{13,13},{2,2},{6,10},{... | collective-permute-start | bytes 1179656 | tf_op jit(solution)/shard_map/ppermute | solution.py:187
  164.0 1.7 collective-permute-start.26
  164.0 17.7 %collective-permute-start.32 = (bf16[192,1024]{1,0:T(8,128)(2,1)S(1)}, bf16[192,1024]{1,0:T(8,128)(2,1)S(1)}, u32[]{:S(2)}, u32[]{:S(2)}) collective-permute-start(bf16[192,1024]{1,0:T(8,128)(2,1)S(1)} %fusion.11), channel_id=1, source_target_pairs={{0,16},{16,0},{1,17},{17,1},{2,18},{18,2},{3,19},{19,3},{4,20},{20... | collective-permute-start | bytes 1179656 | tf_op jit(solution)/shard_map/ppermute | solution.py:20
  164.7 8.1 %collective-permute-start.31 = (bf16[192,1024]{1,0:T(8,128)(2,1)S(1)}, bf16[192,1024]{1,0:T(8,128)(2,1)S(1)}, u32[]{:S(2)}, u32[]{:S(2)}) collective-permute-start(bf16[192,1024]{1,0:T(8,128)(2,1)S(1)} %add_convert_fusion.7), channel_id=1, source_target_pairs={{0,0},{4,8},{8,4},{12,12},{1,1},{5,9},{9,5},{13,13},{2,2},{6,10},{... | collective-permute-start | bytes 1179656 | tf_op jit(solution)/shard_map/ppermute | solution.py:187
  165.9 15.8 %collective-permute-start.27 = (bf16[192,1024]{1,0:T(8,128)(2,1)S(1)}, bf16[192,1024]{1,0:T(8,128)(2,1)S(1)}, u32[]{:S(2)}, u32[]{:S(2)}) collective-permute-start(bf16[192,1024]{1,0:T(8,128)(2,1)S(1)} %broadcast_select_fusion.7), channel_id=1, source_target_pairs={{0,4},{4,0},{8,12},{12,8},{1,5},{5,1},{9,13},{13,9},{2,6},{6,2},{1... | collective-permute-start | bytes 1179656 | tf_op jit(solution)/shard_map/ppermute | solution.py:20
  181.9 10.8 %collective-permute-start.33 = (bf16[192,1024]{1,0:T(8,128)(2,1)S(1)}, bf16[192,1024]{1,0:T(8,128)(2,1)S(1)}, u32[]{:S(2)}, u32[]{:S(2)}) collective-permute-start(bf16[192,1024]{1,0:T(8,128)(2,1)S(1)} %broadcast_select_fusion.5), channel_id=1, source_target_pairs={{0,4},{4,0},{8,12},{12,8},{1,5},{5,1},{9,13},{13,9},{2,6},{6,2},{1... | collective-permute-start | bytes 1179656 | tf_op jit(solution)/shard_map/ppermute | solution.py:20
  183.9 8.9 %collective-permute-start.34 = (bf16[192,1024]{1,0:T(8,128)(2,1)S(1)}, bf16[192,1024]{1,0:T(8,128)(2,1)S(1)}, u32[]{:S(2)}, u32[]{:S(2)}) collective-permute-start(bf16[192,1024]{1,0:T(8,128)(2,1)S(1)} %add_convert_fusion.5), channel_id=1, source_target_pairs={{0,0},{4,8},{8,4},{12,12},{1,1},{5,9},{9,5},{13,13},{2,2},{6,10},{... | collective-permute-start | bytes 1179656 | tf_op jit(solution)/shard_map/ppermute | solution.py:187
  184.9 7.9 %collective-permute-start.35 = (bf16[192,1024]{1,0:T(8,128)(2,1)S(1)}, bf16[192,1024]{1,0:T(8,128)(2,1)S(1)}, u32[]{:S(2)}, u32[]{:S(2)}) collective-permute-start(bf16[192,1024]{1,0:T(8,128)(2,1)S(1)} %fusion.12), channel_id=1, source_target_pairs={{0,16},{16,0},{1,17},{17,1},{2,18},{18,2},{3,19},{19,3},{4,20},{20... | collective-permute-start | bytes 1179656 | tf_op jit(solution)/shard_map/ppermute | solution.py:20
  193.0 11.6 %collective-permute-start.36 = (bf16[192,1024]{1,0:T(8,128)(2,1)S(1)}, bf16[192,1024]{1,0:T(8,128)(2,1)S(1)}, u32[]{:S(2)}, u32[]{:S(2)}) collective-permute-start(bf16[192,1024]{1,0:T(8,128)(2,1)S(1)} %broadcast_select_fusion.3), channel_id=1, source_target_pairs={{0,4},{4,0},{8,12},{12,8},{1,5},{5,1},{9,13},{13,9},{2,6},{6,2},{1... | collective-permute-start | bytes 1179656 | tf_op jit(solution)/shard_map/ppermute | solution.py:20
  196.9 7.7 %collective-permute-start.37 = (bf16[192,1024]{1,0:T(8,128)(2,1)S(1)}, bf16[192,1024]{1,0:T(8,128)(2,1)S(1)}, u32[]{:S(2)}, u32[]{:S(2)}) collective-permute-start(bf16[192,1024]{1,0:T(8,128)(2,1)S(1)} %add_convert_fusion.3), channel_id=1, source_target_pairs={{0,0},{4,8},{8,4},{12,12},{1,1},{5,9},{9,5},{13,13},{2,2},{6,10},{... | collective-permute-start | bytes 1179656 | tf_op jit(solution)/shard_map/ppermute | solution.py:187
  204.9 7.4 %collective-permute-start.39 = (bf16[192,1024]{1,0:T(8,128)(2,1)S(1)}, bf16[192,1024]{1,0:T(8,128)(2,1)S(1)}, u32[]{:S(2)}, u32[]{:S(2)}) collective-permute-start(bf16[192,1024]{1,0:T(8,128)(2,1)S(1)} %add_convert_fusion.1), channel_id=1, source_target_pairs={{0,0},{4,8},{8,4},{12,12},{1,1},{5,9},{9,5},{13,13},{2,2},{6,10},{... | collective-permute-start | bytes 1179656 | tf_op jit(solution)/shard_map/ppermute | solution.py:187
  205.6 12.5 %collective-permute-start.38 = (bf16[192,1024]{1,0:T(8,128)(2,1)S(1)}, bf16[192,1024]{1,0:T(8,128)(2,1)S(1)}, u32[]{:S(2)}, u32[]{:S(2)}) collective-permute-start(bf16[192,1024]{1,0:T(8,128)(2,1)S(1)} %add_convert_fusion.2), channel_id=1, source_target_pairs={{0,4},{4,0},{8,12},{12,8},{1,5},{5,1},{9,13},{13,9},{2,6},{6,2},{1... | collective-permute-start | bytes 1179656 | tf_op jit(solution)/shard_map/ppermute | solution.py:20
  218.2 7.8 %collective-permute-start.40 = (bf16[192,1024]{1,0:T(8,128)(2,1)S(1)}, bf16[192,1024]{1,0:T(8,128)(2,1)S(1)}, u32[]{:S(2)}, u32[]{:S(2)}) collective-permute-start(bf16[192,1024]{1,0:T(8,128)(2,1)S(1)} %add_convert_fusion), channel_id=1, source_target_pairs={{0,4},{4,0},{8,12},{12,8},{1,5},{5,1},{9,13},{13,9},{2,6},{6,2},{1... | collective-permute-start | bytes 1179656 | tf_op jit(solution)/shard_map/ppermute | solution.py:20
  220.4 6.8 %copy-start.1 = (bf16[1,192,3072]{2,1,0:T(8,128)(2,1)S(1)}, bf16[1,192,3072]{2,1,0:T(8,128)(2,1)}, u32[]{:S(2)}) copy-start(bf16[1,192,3072]{2,1,0:T(8,128)(2,1)} %param.10) | copy-start | bytes 3538948

commit v4 on v3

--- a/solution.py
+++ b/solution.py
@@ -227,10 +227,10 @@
     straight = [picked(d, activations[:, :direct], False) for d in others]
     straight = [swap(straight[d - 1], "expert", d) for d in others]
     far = [swap(one, "dp", 1) for one in near]
-    x = [[straight[d], near[d], far[d]] for d in range(groups - 1)]
     c_sent = [picked(d, upstream, True) for d in others]
     c_own = picked(0, upstream, True)
-    x, c_sent, c_own = lax.optimization_barrier((x, c_sent, c_own))
+    straight, c_sent, c_own = lax.optimization_barrier((straight, c_sent, c_own))
+    x = [[straight[d], near[d], far[d]] for d in range(groups - 1)]
     c = [[swap(c_sent[d - 1], "expert", d)] for d in others]
     chip_half = half.astype(jnp.int32).reshape(1)
     *out, p, q = expert_call(
@@ -243,11 +243,9 @@
 
     out[0], grad[0] = lax.optimization_barrier((out[0], grad[0]))
     high = weighting.astype(BF)
-    low = (weighting - high.astype(F32)).astype(BF)
     total = 0.0
     for d in range(groups):
-        piece = out[d].reshape(rows, model)
-        total = total + nn(high[:, part[d]], piece) + nn(low[:, part[d]], piece)
+        total = total + nn(high[:, part[d]], out[d].reshape(rows, model))
     total = total.astype(BF)
     wide = model // CHUNKS
     blocks = [total[:, k * wide : (k + 1) * wide] for k in range(CHUNKS)]

time: 228 us -> 225 us (0.987)
  matrix products: 16.1 us -> 13.7 us
    dot_general x31 -> x27, matrix products: 16.1 us -> 13.7 us  [nn(): lax.dot_general(a, b, (((1,), (0,)), ((), ())), preferred_element_type=F32)]
  transfers between devices with their start and end apart: 41 -> 41, of which waited for: 14 -> 12; matrix products, arithmetic and copies ran while one was open for 8% -> 8% of each run, Pallas kernels for 30% -> 31%
where the time goes in v4:
time: 225 us; the launch traced here: 224 us
  Pallas kernels  69.2 us (31%)
  waiting for transfers between devices  65.1 us (29%)
  starting transfers between devices  61.3 us (27%)
  matrix products  13.7 us (6%)
  other arithmetic  9.86 us (4%)
  local copies, waits for them, and re-layouts  3.89 us (2%)
    pallas_call x2, Pallas kernels, expert_call(): pl.pallas_call(functools.partial(kernel, counts), grid=(local, width // t...  69.2 us
    ppermute x35, waiting for transfers between devices, swap(): return lax.ppermute(block, axis, [(i, i ^ flip) for i in range(size)])  65.1 us
    ppermute x35, starting transfers between devices, swap(): return lax.ppermute(block, axis, [(i, i ^ flip) for i in range(size)])  57.2 us
    dot_general x27, matrix products, nn(): lax.dot_general(a, b, (((1,), (0,)), ((), ())), preferred_element_type=F32)  13.7 us
  transfers between devices with their start and end apart: 41, of which 12 were waited for; matrix products, arithmetic and copies ran while one was open for 8% of the time, Pallas kernels for 31%

profile of v4, /device:TPU:0, one launch (start us, length us, event | category | flops | bytes accessed | tf_op | source)
XLA Modules:
  0.0 224.3 jit_solution(4483454790859771634)
XLA Ops:
  0.6 0.9 copy.19
  1.9 0.9 reduce-window.6
  3.3 0.7 multiply_add_fusion
  4.1 1.2 slice_select_fusion
  5.3 1.0 select_reduce_fusion
  6.6 3.0 %collective-permute-start.5 = (bf16[2,72,896]{2,1,0:T(8,128)(2,1)S(1)}, bf16[2,72,896]{2,1,0:T(8,128)(2,1)S(1)}, u32[]{:S(2)}, u32[]{:S(2)}) collective-permute-start(bf16[2,72,896]{2,1,0:T(8,128)(2,1)S(1)} %bitcast.136), channel_id=1, source_target_pairs={{0,2},{1,3},{2,0},{3,1},{4,6},{5,7},{6,4},{7,5},{8,10},{9,11},{10,... | collective-permute-start | bytes 774152 | tf_op jit(solution)/shard_map/ppermute | solution.py:20
  10.0 1.5 collective-permute-start.7
  12.3 2.0 collective-permute-start
  14.7 1.6 collective-permute-start.1
  18.2 4.0 %collective-permute-done.5.refs_5_ = bf16[2,72,896]{2,1,0:T(8,128)(2,1)S(1)} collective-permute-done((bf16[2,72,896]{2,1,0:T(8,128)(2,1)S(1)}, bf16[2,72,896]{2,1,0:T(8,128)(2,1)S(1)}, u32[]{:S(2)}, u32[]{:S(2)}) %collective-permute-start.5) | collective-permute-done | bytes 258080 | tf_op jit(solution)/shard_map/ppermute | solution.py:20
  22.2 3.0 %collective-permute-start.2 = (bf16[2,72,1280]{2,1,0:T(8,128)(2,1)S(1)}, bf16[2,72,1280]{2,1,0:T(8,128)(2,1)S(1)}, u32[]{:S(2)}, u32[]{:S(2)}) collective-permute-start(bf16[2,72,1280]{2,1,0:T(8,128)(2,1)S(1)} %bitcast.126), channel_id=1, source_target_pairs={{0,3},{1,2},{2,1},{3,0},{4,7},{5,6},{6,5},{7,4},{8,11},{9,10},{10,... | collective-permute-start | bytes 1105928 | tf_op jit(solution)/shard_map/ppermute | solution.py:20
  25.2 1.3 fusion.5
  26.6 1.6 collective-permute-start.6
  28.6 3.5 %collective-permute-done.refs_1_ = bf16[2,72,1280]{2,1,0:T(8,128)(2,1)S(1)} collective-permute-done((bf16[2,72,1280]{2,1,0:T(8,128)(2,1)S(1)}, bf16[2,72,1280]{2,1,0:T(8,128)(2,1)S(1)}, u32[]{:S(2)}, u32[]{:S(2)}) %collective-permute-start) | collective-permute-done | bytes 368672 | tf_op jit(solution)/shard_map/ppermute | solution.py:20
  32.1 2.1 collective-permute-start.4
  34.2 1.3 convolution_convert_fusion
  35.5 4.5 %collective-permute-done.2.refs_7_ = bf16[2,72,1280]{2,1,0:T(8,128)(2,1)S(1)} collective-permute-done((bf16[2,72,1280]{2,1,0:T(8,128)(2,1)S(1)}, bf16[2,72,1280]{2,1,0:T(8,128)(2,1)S(1)}, u32[]{:S(2)}, u32[]{:S(2)}) %collective-permute-start.2) | collective-permute-done | bytes 368672 | tf_op jit(solution)/shard_map/ppermute | solution.py:20
  40.0 1.5 collective-permute-start.9
  42.0 1.5 collective-permute-start.11
  43.5 34.8 %shard_map.86 = (bf16[2,72,3072]{2,1,0:T(8,128)(2,1)}, bf16[2,72,3072]{2,1,0:T(8,128)(2,1)}, bf16[2,72,3072]{2,1,0:T(8,128)(2,1)}, bf16[2,72,3072]{2,1,0:T(8,128...) custom-call(s32[1]{0:T(128)} %bitcast.half_ref, bf16[2,72,3072]{2,1,0:T(8,128)(2,1)} %bitcast.121, ...), custom_call_target="tpu_custom_call" | custom-call | flops 21743271936 | bytes 75497472 | tf_op jit(solution)/shard_map/pallas_call | solution.py:153
  78.4 1.5 collective-permute-start.15
  79.9 0.5 collective-permute-start.16
  80.4 1.5 collective-permute-start.17
  82.0 1.0 copy-done.4
  83.2 34.4 %shard_map.87 = (bf16[2,72,1024]{2,1,0:T(8,128)(2,1)S(1)}, bf16[2,72,1024]{2,1,0:T(8,128)(2,1)S(1)}, bf16[2,72,1024]{2,1,0:T(8,128)(2,1)S(1)}, bf16[2,72,1024]{2...) custom-call(s32[1]{0:T(128)} %bitcast.half_ref, ...), custom_call_target="tpu_custom_call" | custom-call | flops 21743271936 | bytes 75497472 | tf_op jit(solution)/shard_map/pallas_call | solution.py:153
  118.0 0.5 fusion.16
  118.6 0.5 convolution_add_fusion.1
  119.1 0.5 fusion.1
  119.6 0.9 fusion.63
  120.6 1.6 collective-permute-start.18
  122.1 1.4 collective-permute-start.12
  123.6 0.6 collective-permute-start.13
  124.2 1.4 collective-permute-start.14
  126.1 6.9 %collective-permute-done.18 = bf16[192,1024]{1,0:T(8,128)(2,1)} collective-permute-done((bf16[192,1024]{1,0:T(8,128)(2,1)}, bf16[192,1024]{1,0:T(8,128)(2,1)}, u32[]{:S(2)}, u32[]{:S(2)}) %collective-permute-start.18) | collective-permute-done | bytes 393248 | tf_op jit(solution)/shard_map/ppermute | solution.py:20
  132.9 1.1 add_convert_fusion.11
  134.1 2.2 collective-permute-done.13
  136.7 2.0 collective-permute-start.23
  138.7 1.1 collective-permute-start.24
  139.8 0.7 collective-permute-start.20
  140.5 1.3 fusion.34
  142.4 1.3 fusion.6
  143.9 5.2 %collective-permute-done.23 = bf16[2,72,1024]{2,1,0:T(8,128)(2,1)S(1)} collective-permute-done((bf16[2,72,1024]{2,1,0:T(8,128)(2,1)}, bf16[2,72,1024]{2,1,0:T(8,128)(2,1)S(1)}, u32[]{:S(2)}, u32[]{:S(2)}) %collective-permute-start.23) | collective-permute-done | bytes 294944 | tf_op jit(solution)/shard_map/ppermute | solution.py:20
  149.0 0.9 collective-permute-start.28
  149.9 2.2 collective-permute-start.29
  152.7 1.9 collective-permute-start.21
  154.6 0.7 collective-permute-start.25
  156.5 4.1 %collective-permute-done.21 = bf16[192,1024]{1,0:T(8,128)(2,1)S(1)} collective-permute-done((bf16[192,1024]{1,0:T(8,128)(2,1)S(1)}, bf16[192,1024]{1,0:T(8,128)(2,1)S(1)}, u32[]{:S(2)}, u32[]{:S(2)}) %collective-permute-start.21) | collective-permute-done | bytes 393248 | tf_op jit(solution)/shard_map/ppermute | solution.py:20
  160.6 0.5 collective-permute-start.32
  161.2 0.7 collective-permute-start.31
  162.5 6.5 %collective-permute-start.27 = (bf16[192,1024]{1,0:T(8,128)(2,1)S(1)}, bf16[192,1024]{1,0:T(8,128)(2,1)S(1)}, u32[]{:S(2)}, u32[]{:S(2)}) collective-permute-start(bf16[192,1024]{1,0:T(8,128)(2,1)S(1)} %broadcast_select_fusion.7), channel_id=1, source_target_pairs={{0,4},{4,0},{8,12},{12,8},{1,5},{5,1},{9,13},{13,9},{2,6},{6,2},{1... | collective-permute-start | bytes 1179656 | tf_op jit(solution)/shard_map/ppermute | solution.py:20
  169.6 8.9 %collective-permute-done.27 = bf16[192,1024]{1,0:T(8,128)(2,1)S(1)} collective-permute-done((bf16[192,1024]{1,0:T(8,128)(2,1)S(1)}, bf16[192,1024]{1,0:T(8,128)(2,1)S(1)}, u32[]{:S(2)}, u32[]{:S(2)}) %collective-permute-start.27) | collective-permute-done | bytes 393248 | tf_op jit(solution)/shard_map/ppermute | solution.py:20
  178.7 1.8 collective-permute-start.33
  180.6 0.7 collective-permute-start.34
  181.7 7.8 %collective-permute-done.33 = bf16[192,1024]{1,0:T(8,128)(2,1)S(1)} collective-permute-done((bf16[192,1024]{1,0:T(8,128)(2,1)S(1)}, bf16[192,1024]{1,0:T(8,128)(2,1)S(1)}, u32[]{:S(2)}, u32[]{:S(2)}) %collective-permute-start.33) | collective-permute-done | bytes 393248 | tf_op jit(solution)/shard_map/ppermute | solution.py:20
  189.7 3.8 %collective-permute-start.36 = (bf16[192,1024]{1,0:T(8,128)(2,1)S(1)}, bf16[192,1024]{1,0:T(8,128)(2,1)S(1)}, u32[]{:S(2)}, u32[]{:S(2)}) collective-permute-start(bf16[192,1024]{1,0:T(8,128)(2,1)S(1)} %broadcast_select_fusion.3), channel_id=1, source_target_pairs={{0,4},{4,0},{8,12},{12,8},{1,5},{5,1},{9,13},{13,9},{2,6},{6,2},{1... | collective-permute-start | bytes 1179656 | tf_op jit(solution)/shard_map/ppermute | solution.py:20
  193.7 0.7 collective-permute-start.37
  194.8 6.6 %collective-permute-done.36 = bf16[192,1024]{1,0:T(8,128)(2,1)S(1)} collective-permute-done((bf16[192,1024]{1,0:T(8,128)(2,1)S(1)}, bf16[192,1024]{1,0:T(8,128)(2,1)S(1)}, u32[]{:S(2)}, u32[]{:S(2)}) %collective-permute-start.36) | collective-permute-done | bytes 393248 | tf_op jit(solution)/shard_map/ppermute | solution.py:20
  201.6 0.7 collective-permute-start.39
  202.3 5.6 %collective-permute-start.38 = (bf16[192,1024]{1,0:T(8,128)(2,1)S(1)}, bf16[192,1024]{1,0:T(8,128)(2,1)S(1)}, u32[]{:S(2)}, u32[]{:S(2)}) collective-permute-start(bf16[192,1024]{1,0:T(8,128)(2,1)S(1)} %add_convert_fusion.2), channel_id=1, source_target_pairs={{0,4},{4,0},{8,12},{12,8},{1,5},{5,1},{9,13},{13,9},{2,6},{6,2},{1... | collective-permute-start | bytes 1179656 | tf_op jit(solution)/shard_map/ppermute | solution.py:20
  208.2 1.1 maximum_bitcast_fusion
  209.3 5.8 %collective-permute-done.38 = bf16[192,1024]{1,0:T(8,128)(2,1)S(1)} collective-permute-done((bf16[192,1024]{1,0:T(8,128)(2,1)S(1)}, bf16[192,1024]{1,0:T(8,128)(2,1)S(1)}, u32[]{:S(2)}, u32[]{:S(2)}) %collective-permute-start.38) | collective-permute-done | bytes 393248 | tf_op jit(solution)/shard_map/ppermute | solution.py:20
  215.1 2.1 collective-permute-start.40
  217.5 5.6 %collective-permute-done.40 = bf16[192,1024]{1,0:T(8,128)(2,1)S(1)} collective-permute-done((bf16[192,1024]{1,0:T(8,128)(2,1)S(1)}, bf16[192,1024]{1,0:T(8,128)(2,1)S(1)}, u32[]{:S(2)}, u32[]{:S(2)}) %collective-permute-start.40) | collective-permute-done | bytes 393248 | tf_op jit(solution)/shard_map/ppermute | solution.py:20
  223.2 1.1 maximum_bitcast_fusion.1
  (106 shorter events, 13.2 us)
Async XLA Ops:
  0.6 15.7 %copy-start = (bf16[1,192,3072]{2,1,0:T(8,128)(2,1)S(1)}, bf16[1,192,3072]{2,1,0:T(8,128)(2,1)}, u32[]{:S(2)}) copy-start(bf16[1,192,3072]{2,1,0:T(8,128)(2,1)} %param.10) | copy-start | bytes 3538948
  4.0 7.9 %copy-start.2 = (bf16[1,192,3072]{2,1,0:T(8,128)(2,1)S(1)}, bf16[1,192,3072]{2,1,0:T(8,128)(2,1)}, u32[]{:S(2)}) copy-start(bf16[1,192,3072]{2,1,0:T(8,128)(2,1)} %param.7) | copy-start | bytes 3538948
  6.6 15.6 %collective-permute-start.5 = (bf16[2,72,896]{2,1,0:T(8,128)(2,1)S(1)}, bf16[2,72,896]{2,1,0:T(8,128)(2,1)S(1)}, u32[]{:S(2)}, u32[]{:S(2)}) collective-permute-start(bf16[2,72,896]{2,1,0:T(8,128)(2,1)S(1)} %bitcast.136), channel_id=1, source_target_pairs={{0,2},{1,3},{2,0},{3,1},{4,6},{5,7},{6,4},{7,5},{8,10},{9,11},{10,... | collective-permute-start | bytes 774152 | tf_op jit(solution)/shard_map/ppermute | solution.py:20
  10.0 16.6 %collective-permute-start.7 = (bf16[2,72,896]{2,1,0:T(8,128)(2,1)S(1)}, bf16[2,72,896]{2,1,0:T(8,128)(2,1)S(1)}, u32[]{:S(2)}, u32[]{:S(2)}) collective-permute-start(bf16[2,72,896]{2,1,0:T(8,128)(2,1)S(1)} %bitcast.135), channel_id=1, source_target_pairs={{0,3},{1,2},{2,1},{3,0},{4,7},{5,6},{6,5},{7,4},{8,11},{9,10},{10,... | collective-permute-start | bytes 774152 | tf_op jit(solution)/shard_map/ppermute | solution.py:20
  11.8 16.3 %collective-permute-start.3 = (bf16[2,72,896]{2,1,0:T(8,128)(2,1)S(1)}, bf16[2,72,896]{2,1,0:T(8,128)(2,1)S(1)}, u32[]{:S(2)}, u32[]{:S(2)}) collective-permute-start(bf16[2,72,896]{2,1,0:T(8,128)(2,1)S(1)} %bitcast.134), channel_id=1, source_target_pairs={{0,1},{1,0},{2,3},{3,2},{4,5},{5,4},{6,7},{7,6},{8,9},{9,8},{10,11... | collective-permute-start | bytes 774152 | tf_op jit(solution)/shard_map/ppermute | solution.py:20
  12.3 19.7 %collective-permute-start = (bf16[2,72,1280]{2,1,0:T(8,128)(2,1)S(1)}, bf16[2,72,1280]{2,1,0:T(8,128)(2,1)S(1)}, u32[]{:S(2)}, u32[]{:S(2)}) collective-permute-start(bf16[2,72,1280]{2,1,0:T(8,128)(2,1)S(1)} %bitcast.125), channel_id=1, source_target_pairs={{0,1},{1,0},{2,3},{3,2},{4,5},{5,4},{6,7},{7,6},{8,9},{9,8},{10,11... | collective-permute-start | bytes 1105928 | tf_op jit(solution)/shard_map/ppermute | solution.py:20
  14.7 20.8 %collective-permute-start.1 = (bf16[2,72,1280]{2,1,0:T(8,128)(2,1)S(1)}, bf16[2,72,1280]{2,1,0:T(8,128)(2,1)S(1)}, u32[]{:S(2)}, u32[]{:S(2)}) collective-permute-start(bf16[2,72,1280]{2,1,0:T(8,128)(2,1)S(1)} %bitcast.124), channel_id=1, source_target_pairs={{0,2},{1,3},{2,0},{3,1},{4,6},{5,7},{6,4},{7,5},{8,10},{9,11},{10,... | collective-permute-start | bytes 1105928 | tf_op jit(solution)/shard_map/ppermute | solution.py:20
  22.2 17.8 %collective-permute-start.2 = (bf16[2,72,1280]{2,1,0:T(8,128)(2,1)S(1)}, bf16[2,72,1280]{2,1,0:T(8,128)(2,1)S(1)}, u32[]{:S(2)}, u32[]{:S(2)}) collective-permute-start(bf16[2,72,1280]{2,1,0:T(8,128)(2,1)S(1)} %bitcast.126), channel_id=1, source_target_pairs={{0,3},{1,2},{2,1},{3,0},{4,7},{5,6},{6,5},{7,4},{8,11},{9,10},{10,... | collective-permute-start | bytes 1105928 | tf_op jit(solution)/shard_map/ppermute | solution.py:20
  26.6 15.5 %collective-permute-start.6 = (bf16[2,72,896]{2,1,0:T(8,128)(2,1)S(1)}, bf16[2,72,896]{2,1,0:T(8,128)(2,1)S(1)}, u32[]{:S(2)}, u32[]{:S(2)}) collective-permute-start(bf16[2,72,896]{2,1,0:T(8,128)(2,1)S(1)} %collective-permute-done.5.refs_5_), channel_id=1, source_target_pairs={{0,4},{4,0},{8,12},{12,8},{1,5},{5,1},{9,13},{13,9},{2,6},{6,2},{1... | collective-permute-start | bytes 774152 | tf_op jit(solution)/shard_map/ppermute | solution.py:20
  28.1 15.4 %collective-permute-start.8 = (bf16[2,72,896]{2,1,0:T(8,128)(2,1)S(1)}, bf16[2,72,896]{2,1,0:T(8,128)(2,1)S(1)}, u32[]{:S(2)}, u32[]{:S(2)}) collective-permute-start(bf16[2,72,896]{2,1,0:T(8,128)(2,1)S(1)} %collective-permute-done.7.refs_8_), channel_id=1, source_target_pairs={{0,4},{4,0},{8,12},{12,8},{1,5},{5,1},{9,13},{13,9},{2,6},{6,2},{1... | collective-permute-start | bytes 774152 | tf_op jit(solution)/shard_map/ppermute | solution.py:20
  32.1 11.5 %collective-permute-start.4 = (bf16[2,72,896]{2,1,0:T(8,128)(2,1)S(1)}, bf16[2,72,896]{2,1,0:T(8,128)(2,1)S(1)}, u32[]{:S(2)}, u32[]{:S(2)}) collective-permute-start(bf16[2,72,896]{2,1,0:T(8,128)(2,1)S(1)} %collective-permute-done.3.refs_2_), channel_id=1, source_target_pairs={{0,4},{4,0},{8,12},{12,8},{1,5},{5,1},{9,13},{13,9},{2,6},{6,2},{1... | collective-permute-start | bytes 774152 | tf_op jit(solution)/shard_map/ppermute | solution.py:20
  35.5 8.0 %copy-start.7 = (bf16[2,72,1280]{2,1,0:T(8,128)(2,1)}, bf16[2,72,1280]{2,1,0:T(8,128)(2,1)S(1)}, u32[]{:S(2)}) copy-start(bf16[2,72,1280]{2,1,0:T(8,128)(2,1)S(1)} %collective-permute-done.1.refs_4_) | copy-start | bytes 1105924
  40.0 3.5 %copy-start.8 = (bf16[2,72,1280]{2,1,0:T(8,128)(2,1)}, bf16[2,72,1280]{2,1,0:T(8,128)(2,1)S(1)}, u32[]{:S(2)}) copy-start(bf16[2,72,1280]{2,1,0:T(8,128)(2,1)S(1)} %collective-permute-done.2.refs_7_) | copy-start | bytes 1105924
  40.0 40.4 %collective-permute-start.9 = (bf16[2,72,3072]{2,1,0:T(8,128)(2,1)S(1)}, bf16[2,72,3072]{2,1,0:T(8,128)(2,1)S(1)}, u32[]{:S(2)}, u32[]{:S(2)}) collective-permute-start(bf16[2,72,3072]{2,1,0:T(8,128)(2,1)S(1)} %bitcast.120), channel_id=1, source_target_pairs={{0,1},{1,0},{2,3},{3,2},{4,5},{5,4},{6,7},{7,6},{8,9},{9,8},{10,11... | collective-permute-start | bytes 2654216 | tf_op jit(solution)/shard_map/ppermute | solution.py:20
  41.5 40.4 %collective-permute-start.10 = (bf16[2,72,3072]{2,1,0:T(8,128)(2,1)S(1)}, bf16[2,72,3072]{2,1,0:T(8,128)(2,1)S(1)}, u32[]{:S(2)}, u32[]{:S(2)}) collective-permute-start(bf16[2,72,3072]{2,1,0:T(8,128)(2,1)S(1)} %bitcast.119), channel_id=1, source_target_pairs={{0,2},{1,3},{2,0},{3,1},{4,6},{5,7},{6,4},{7,5},{8,10},{9,11},{10,... | collective-permute-start | bytes 2654216 | tf_op jit(solution)/shard_map/ppermute | solution.py:20
  42.0 39.9 %collective-permute-start.11 = (bf16[2,72,3072]{2,1,0:T(8,128)(2,1)S(1)}, bf16[2,72,3072]{2,1,0:T(8,128)(2,1)S(1)}, u32[]{:S(2)}, u32[]{:S(2)}) collective-permute-start(bf16[2,72,3072]{2,1,0:T(8,128)(2,1)S(1)} %bitcast.118), channel_id=1, source_target_pairs={{0,3},{1,2},{2,1},{3,0},{4,7},{5,6},{6,5},{7,4},{8,11},{9,10},{10,... | collective-permute-start | bytes 2654216 | tf_op jit(solution)/shard_map/ppermute | solution.py:20
  78.4 40.2 %collective-permute-start.15 = (bf16[2,72,3072]{2,1,0:T(8,128)(2,1)}, bf16[2,72,3072]{2,1,0:T(8,128)(2,1)S(1)}, u32[]{:S(2)}, u32[]{:S(2)}) collective-permute-start(bf16[2,72,3072]{2,1,0:T(8,128)(2,1)} %get-tuple-element.84), channel_id=1, source_target_pairs={{0,1},{1,0},{2,3},{3,2},{4,5},{5,4},{6,7},{7,6},{8,9},{9,8},{10,11... | collective-permute-start | bytes 2654216 | tf_op jit(solution)/shard_map/ppermute | solution.py:20
  79.9 39.2 %collective-permute-start.16 = (bf16[2,72,3072]{2,1,0:T(8,128)(2,1)}, bf16[2,72,3072]{2,1,0:T(8,128)(2,1)S(1)}, u32[]{:S(2)}, u32[]{:S(2)}) collective-permute-start(bf16[2,72,3072]{2,1,0:T(8,128)(2,1)} %get-tuple-element.85), channel_id=1, source_target_pairs={{0,2},{1,3},{2,0},{3,1},{4,6},{5,7},{6,4},{7,5},{8,10},{9,11},{10,... | collective-permute-start | bytes 2654216 | tf_op jit(solution)/shard_map/ppermute | solution.py:20
  80.4 1.5 copy-start.3
  80.4 37.6 %collective-permute-start.17 = (bf16[2,72,3072]{2,1,0:T(8,128)(2,1)}, bf16[2,72,3072]{2,1,0:T(8,128)(2,1)S(1)}, u32[]{:S(2)}, u32[]{:S(2)}) collective-permute-start(bf16[2,72,3072]{2,1,0:T(8,128)(2,1)} %get-tuple-element.86), channel_id=1, source_target_pairs={{0,3},{1,2},{2,1},{3,0},{4,7},{5,6},{6,5},{7,4},{8,11},{9,10},{10,... | collective-permute-start | bytes 2654216 | tf_op jit(solution)/shard_map/ppermute | solution.py:20
  81.9 1.0 copy-start.4
  81.9 1.3 copy-start.5
  83.2 34.4 %copy-start.6 = (bf16[2,72,3072]{2,1,0:T(8,128)(2,1)S(1)}, bf16[2,72,3072]{2,1,0:T(8,128)(2,1)}, u32[]{:S(2)}) copy-start(bf16[2,72,3072]{2,1,0:T(8,128)(2,1)} %get-tuple-element.83) | copy-start | bytes 2654212
  120.6 12.4 %collective-permute-start.18 = (bf16[192,1024]{1,0:T(8,128)(2,1)}, bf16[192,1024]{1,0:T(8,128)(2,1)}, u32[]{:S(2)}, u32[]{:S(2)}) collective-permute-start(bf16[192,1024]{1,0:T(8,128)(2,1)} %get-tuple-element.130), channel_id=1, source_target_pairs={{0,4},{4,0},{8,12},{12,8},{1,5},{5,1},{9,13},{13,9},{2,6},{6,2},{1... | collective-permute-start | bytes 1179656 | tf_op jit(solution)/shard_map/ppermute | solution.py:20
  122.1 11.9 %collective-permute-start.12 = (bf16[2,72,1024]{2,1,0:T(8,128)(2,1)S(1)}, bf16[2,72,1024]{2,1,0:T(8,128)(2,1)}, u32[]{:S(2)}, u32[]{:S(2)}) collective-permute-start(bf16[2,72,1024]{2,1,0:T(8,128)(2,1)S(1)} %get-tuple-element.76), channel_id=1, source_target_pairs={{0,1},{1,0},{2,3},{3,2},{4,5},{5,4},{6,7},{7,6},{8,9},{9,8},{10,11... | collective-permute-start | bytes 884744 | tf_op jit(solution)/shard_map/ppermute | solution.py:20
  123.6 12.8 %collective-permute-start.13 = (bf16[2,72,1024]{2,1,0:T(8,128)(2,1)}, bf16[2,72,1024]{2,1,0:T(8,128)(2,1)S(1)}, u32[]{:S(2)}, u32[]{:S(2)}) collective-permute-start(bf16[2,72,1024]{2,1,0:T(8,128)(2,1)} %get-tuple-element.77), channel_id=1, source_target_pairs={{0,2},{1,3},{2,0},{3,1},{4,6},{5,7},{6,4},{7,5},{8,10},{9,11},{10,... | collective-permute-start | bytes 884744 | tf_op jit(solution)/shard_map/ppermute | solution.py:20
  124.2 12.1 %collective-permute-start.14 = (bf16[2,72,1024]{2,1,0:T(8,128)(2,1)}, bf16[2,72,1024]{2,1,0:T(8,128)(2,1)}, u32[]{:S(2)}, u32[]{:S(2)}) collective-permute-start(bf16[2,72,1024]{2,1,0:T(8,128)(2,1)} %get-tuple-element.78), channel_id=1, source_target_pairs={{0,3},{1,2},{2,1},{3,0},{4,7},{5,6},{6,5},{7,4},{8,11},{9,10},{10,... | collective-permute-start | bytes 884744 | tf_op jit(solution)/shard_map/ppermute | solution.py:20
  125.6 18.1 %collective-permute-start.19 = (bf16[192,1024]{1,0:T(8,128)(2,1)}, bf16[192,1024]{1,0:T(8,128)(2,1)S(1)}, u32[]{:S(2)}, u32[]{:S(2)}) collective-permute-start(bf16[192,1024]{1,0:T(8,128)(2,1)} %get-tuple-element.129), channel_id=1, source_target_pairs={{0,4},{4,0},{8,12},{12,8},{1,5},{5,1},{9,13},{13,9},{2,6},{6,2},{1... | collective-permute-start | bytes 1179656 | tf_op jit(solution)/shard_map/ppermute | solution.py:20
  136.3 7.5 %collective-permute-start.22 = (bf16[2,72,1024]{2,1,0:T(8,128)(2,1)S(1)}, bf16[2,72,1024]{2,1,0:T(8,128)(2,1)S(1)}, u32[]{:S(2)}, u32[]{:S(2)}) collective-permute-start(bf16[2,72,1024]{2,1,0:T(8,128)(2,1)S(1)} %get-tuple-element.90), channel_id=1, source_target_pairs={{0,1},{1,0},{2,3},{3,2},{4,5},{5,4},{6,7},{7,6},{8,9},{9,8},{10,11... | collective-permute-start | bytes 884744 | tf_op jit(solution)/shard_map/ppermute | solution.py:20
  136.7 12.3 %collective-permute-start.23 = (bf16[2,72,1024]{2,1,0:T(8,128)(2,1)}, bf16[2,72,1024]{2,1,0:T(8,128)(2,1)S(1)}, u32[]{:S(2)}, u32[]{:S(2)}) collective-permute-start(bf16[2,72,1024]{2,1,0:T(8,128)(2,1)} %get-tuple-element.91), channel_id=1, source_target_pairs={{0,2},{1,3},{2,0},{3,1},{4,6},{5,7},{6,4},{7,5},{8,10},{9,11},{10,... | collective-permute-start | bytes 884744 | tf_op jit(solution)/shard_map/ppermute | solution.py:20
  138.7 10.3 %collective-permute-start.24 = (bf16[2,72,1024]{2,1,0:T(8,128)(2,1)}, bf16[2,72,1024]{2,1,0:T(8,128)(2,1)S(1)}, u32[]{:S(2)}, u32[]{:S(2)}) collective-permute-start(bf16[2,72,1024]{2,1,0:T(8,128)(2,1)} %get-tuple-element.92), channel_id=1, source_target_pairs={{0,3},{1,2},{2,1},{3,0},{4,7},{5,6},{6,5},{7,4},{8,11},{9,10},{10,... | collective-permute-start | bytes 884744 | tf_op jit(solution)/shard_map/ppermute | solution.py:20
  139.8 3.9 %collective-permute-start.20 = (bf16[192,1024]{1,0:T(8,128)(2,1)S(1)}, bf16[192,1024]{1,0:T(8,128)(2,1)S(1)}, u32[]{:S(2)}, u32[]{:S(2)}) collective-permute-start(bf16[192,1024]{1,0:T(8,128)(2,1)S(1)} %add_convert_fusion.11), channel_id=1, source_target_pairs={{0,0},{4,8},{8,4},{12,12},{1,1},{5,9},{9,5},{13,13},{2,2},{6,10},{... | collective-permute-start | bytes 1179656 | tf_op jit(solution)/shard_map/ppermute | solution.py:187
  142.3 7.6 %copy-start.10 = (bf16[2,72,1024]{2,1,0:T(8,128)(2,1)S(1)}, bf16[2,72,1024]{2,1,0:T(8,128)(2,1)}, u32[]{:S(2)}) copy-start(bf16[2,72,1024]{2,1,0:T(8,128)(2,1)} %get-tuple-element.107) | copy-start | bytes 884740
  142.3 9.8 %copy-start.9 = (bf16[2,72,1024]{2,1,0:T(8,128)(2,1)S(1)}, bf16[2,72,1024]{2,1,0:T(8,128)(2,1)}, u32[]{:S(2)}) copy-start(bf16[2,72,1024]{2,1,0:T(8,128)(2,1)} %get-tuple-element.108) | copy-start | bytes 884740
  149.0 12.2 %collective-permute-start.28 = (bf16[2,72,1024]{2,1,0:T(8,128)(2,1)S(1)}, bf16[2,72,1024]{2,1,0:T(8,128)(2,1)S(1)}, u32[]{:S(2)}, u32[]{:S(2)}) collective-permute-start(bf16[2,72,1024]{2,1,0:T(8,128)(2,1)S(1)} %get-tuple-element.106), channel_id=1, source_target_pairs={{0,1},{1,0},{2,3},{3,2},{4,5},{5,4},{6,7},{7,6},{8,9},{9,8},{10,11... | collective-permute-start | bytes 884744 | tf_op jit(solution)/shard_map/ppermute | solution.py:20
  149.9 11.3 %collective-permute-start.29 = (bf16[2,72,1024]{2,1,0:T(8,128)(2,1)S(1)}, bf16[2,72,1024]{2,1,0:T(8,128)(2,1)S(1)}, u32[]{:S(2)}, u32[]{:S(2)}) collective-permute-start(bf16[2,72,1024]{2,1,0:T(8,128)(2,1)S(1)} %copy-done.10), channel_id=1, source_target_pairs={{0,2},{1,3},{2,0},{3,1},{4,6},{5,7},{6,4},{7,5},{8,10},{9,11},{10,... | collective-permute-start | bytes 884744 | tf_op jit(solution)/shard_map/ppermute | solution.py:20
  152.2 9.0 %collective-permute-start.30 = (bf16[2,72,1024]{2,1,0:T(8,128)(2,1)S(1)}, bf16[2,72,1024]{2,1,0:T(8,128)(2,1)S(1)}, u32[]{:S(2)}, u32[]{:S(2)}) collective-permute-start(bf16[2,72,1024]{2,1,0:T(8,128)(2,1)S(1)} %copy-done.9), channel_id=1, source_target_pairs={{0,3},{1,2},{2,1},{3,0},{4,7},{5,6},{6,5},{7,4},{8,11},{9,10},{10,... | collective-permute-start | bytes 884744 | tf_op jit(solution)/shard_map/ppermute | solution.py:20
  152.7 7.8 %collective-permute-start.21 = (bf16[192,1024]{1,0:T(8,128)(2,1)S(1)}, bf16[192,1024]{1,0:T(8,128)(2,1)S(1)}, u32[]{:S(2)}, u32[]{:S(2)}) collective-permute-start(bf16[192,1024]{1,0:T(8,128)(2,1)S(1)} %broadcast_select_fusion.9), channel_id=1, source_target_pairs={{0,4},{4,0},{8,12},{12,8},{1,5},{5,1},{9,13},{13,9},{2,6},{6,2},{1... | collective-permute-start | bytes 1179656 | tf_op jit(solution)/shard_map/ppermute | solution.py:20
  154.6 6.0 %collective-permute-start.25 = (bf16[192,1024]{1,0:T(8,128)(2,1)S(1)}, bf16[192,1024]{1,0:T(8,128)(2,1)S(1)}, u32[]{:S(2)}, u32[]{:S(2)}) collective-permute-start(bf16[192,1024]{1,0:T(8,128)(2,1)S(1)} %add_convert_fusion.9), channel_id=1, source_target_pairs={{0,0},{4,8},{8,4},{12,12},{1,1},{5,9},{9,5},{13,13},{2,2},{6,10},{... | collective-permute-start | bytes 1179656 | tf_op jit(solution)/shard_map/ppermute | solution.py:187
  160.6 1.7 collective-permute-start.26
  160.6 17.9 %collective-permute-start.32 = (bf16[192,1024]{1,0:T(8,128)(2,1)S(1)}, bf16[192,1024]{1,0:T(8,128)(2,1)S(1)}, u32[]{:S(2)}, u32[]{:S(2)}) collective-permute-start(bf16[192,1024]{1,0:T(8,128)(2,1)S(1)} %fusion.7), channel_id=1, source_target_pairs={{0,16},{16,0},{1,17},{17,1},{2,18},{18,2},{3,19},{19,3},{4,20},{20... | collective-permute-start | bytes 1179656 | tf_op jit(solution)/shard_map/ppermute | solution.py:20
  161.2 8.3 %collective-permute-start.31 = (bf16[192,1024]{1,0:T(8,128)(2,1)S(1)}, bf16[192,1024]{1,0:T(8,128)(2,1)S(1)}, u32[]{:S(2)}, u32[]{:S(2)}) collective-permute-start(bf16[192,1024]{1,0:T(8,128)(2,1)S(1)} %add_convert_fusion.7), channel_id=1, source_target_pairs={{0,0},{4,8},{8,4},{12,12},{1,1},{5,9},{9,5},{13,13},{2,2},{6,10},{... | collective-permute-start | bytes 1179656 | tf_op jit(solution)/shard_map/ppermute | solution.py:187
  162.5 16.0 %collective-permute-start.27 = (bf16[192,1024]{1,0:T(8,128)(2,1)S(1)}, bf16[192,1024]{1,0:T(8,128)(2,1)S(1)}, u32[]{:S(2)}, u32[]{:S(2)}) collective-permute-start(bf16[192,1024]{1,0:T(8,128)(2,1)S(1)} %broadcast_select_fusion.7), channel_id=1, source_target_pairs={{0,4},{4,0},{8,12},{12,8},{1,5},{5,1},{9,13},{13,9},{2,6},{6,2},{1... | collective-permute-start | bytes 1179656 | tf_op jit(solution)/shard_map/ppermute | solution.py:20
  178.7 10.8 %collective-permute-start.33 = (bf16[192,1024]{1,0:T(8,128)(2,1)S(1)}, bf16[192,1024]{1,0:T(8,128)(2,1)S(1)}, u32[]{:S(2)}, u32[]{:S(2)}) collective-permute-start(bf16[192,1024]{1,0:T(8,128)(2,1)S(1)} %broadcast_select_fusion.5), channel_id=1, source_target_pairs={{0,4},{4,0},{8,12},{12,8},{1,5},{5,1},{9,13},{13,9},{2,6},{6,2},{1... | collective-permute-start | bytes 1179656 | tf_op jit(solution)/shard_map/ppermute | solution.py:20
  180.6 8.9 %collective-permute-start.34 = (bf16[192,1024]{1,0:T(8,128)(2,1)S(1)}, bf16[192,1024]{1,0:T(8,128)(2,1)S(1)}, u32[]{:S(2)}, u32[]{:S(2)}) collective-permute-start(bf16[192,1024]{1,0:T(8,128)(2,1)S(1)} %add_convert_fusion.5), channel_id=1, source_target_pairs={{0,0},{4,8},{8,4},{12,12},{1,1},{5,9},{9,5},{13,13},{2,2},{6,10},{... | collective-permute-start | bytes 1179656 | tf_op jit(solution)/shard_map/ppermute | solution.py:187
  181.6 7.9 %collective-permute-start.35 = (bf16[192,1024]{1,0:T(8,128)(2,1)S(1)}, bf16[192,1024]{1,0:T(8,128)(2,1)S(1)}, u32[]{:S(2)}, u32[]{:S(2)}) collective-permute-start(bf16[192,1024]{1,0:T(8,128)(2,1)S(1)} %fusion.8), channel_id=1, source_target_pairs={{0,16},{16,0},{1,17},{17,1},{2,18},{18,2},{3,19},{19,3},{4,20},{20... | collective-permute-start | bytes 1179656 | tf_op jit(solution)/shard_map/ppermute | solution.py:20
  189.7 11.6 %collective-permute-start.36 = (bf16[192,1024]{1,0:T(8,128)(2,1)S(1)}, bf16[192,1024]{1,0:T(8,128)(2,1)S(1)}, u32[]{:S(2)}, u32[]{:S(2)}) collective-permute-start(bf16[192,1024]{1,0:T(8,128)(2,1)S(1)} %broadcast_select_fusion.3), channel_id=1, source_target_pairs={{0,4},{4,0},{8,12},{12,8},{1,5},{5,1},{9,13},{13,9},{2,6},{6,2},{1... | collective-permute-start | bytes 1179656 | tf_op jit(solution)/shard_map/ppermute | solution.py:20
  193.7 7.7 %collective-permute-start.37 = (bf16[192,1024]{1,0:T(8,128)(2,1)S(1)}, bf16[192,1024]{1,0:T(8,128)(2,1)S(1)}, u32[]{:S(2)}, u32[]{:S(2)}) collective-permute-start(bf16[192,1024]{1,0:T(8,128)(2,1)S(1)} %add_convert_fusion.3), channel_id=1, source_target_pairs={{0,0},{4,8},{8,4},{12,12},{1,1},{5,9},{9,5},{13,13},{2,2},{6,10},{... | collective-permute-start | bytes 1179656 | tf_op jit(solution)/shard_map/ppermute | solution.py:187
  201.6 7.6 %collective-permute-start.39 = (bf16[192,1024]{1,0:T(8,128)(2,1)S(1)}, bf16[192,1024]{1,0:T(8,128)(2,1)S(1)}, u32[]{:S(2)}, u32[]{:S(2)}) collective-permute-start(bf16[192,1024]{1,0:T(8,128)(2,1)S(1)} %add_convert_fusion.1), channel_id=1, source_target_pairs={{0,0},{4,8},{8,4},{12,12},{1,1},{5,9},{9,5},{13,13},{2,2},{6,10},{... | collective-permute-start | bytes 1179656 | tf_op jit(solution)/shard_map/ppermute | solution.py:187
  202.3 12.7 %collective-permute-start.38 = (bf16[192,1024]{1,0:T(8,128)(2,1)S(1)}, bf16[192,1024]{1,0:T(8,128)(2,1)S(1)}, u32[]{:S(2)}, u32[]{:S(2)}) collective-permute-start(bf16[192,1024]{1,0:T(8,128)(2,1)S(1)} %add_convert_fusion.2), channel_id=1, source_target_pairs={{0,4},{4,0},{8,12},{12,8},{1,5},{5,1},{9,13},{13,9},{2,6},{6,2},{1... | collective-permute-start | bytes 1179656 | tf_op jit(solution)/shard_map/ppermute | solution.py:20
  215.1 8.0 %collective-permute-start.40 = (bf16[192,1024]{1,0:T(8,128)(2,1)S(1)}, bf16[192,1024]{1,0:T(8,128)(2,1)S(1)}, u32[]{:S(2)}, u32[]{:S(2)}) collective-permute-start(bf16[192,1024]{1,0:T(8,128)(2,1)S(1)} %add_convert_fusion), channel_id=1, source_target_pairs={{0,4},{4,0},{8,12},{12,8},{1,5},{5,1},{9,13},{13,9},{2,6},{6,2},{1... | collective-permute-start | bytes 1179656 | tf_op jit(solution)/shard_map/ppermute | solution.py:20
  217.4 6.8 %copy-start.1 = (bf16[1,192,3072]{2,1,0:T(8,128)(2,1)S(1)}, bf16[1,192,3072]{2,1,0:T(8,128)(2,1)}, u32[]{:S(2)}) copy-start(bf16[1,192,3072]{2,1,0:T(8,128)(2,1)} %param.10) | copy-start | bytes 3538948

commit v5 on v4

--- a/solution.py
+++ b/solution.py
@@ -221,8 +221,7 @@
     half = lax.rem(lax.axis_index("dp"), 2)
     helped = PAIR if model > 2 * PAIR else 0
     direct = model - 2 * helped
-    low, high = activations[:, direct : direct + helped], activations[:, direct + helped :]
-    fetched = jnp.where(half == 1, high, low)
+    fetched = lax.dynamic_slice_in_dim(activations, direct + half * helped, helped, axis=1)
     near = [swap(picked(d, fetched, False), "expert", d) for d in others]
     straight = [picked(d, activations[:, :direct], False) for d in others]
     straight = [swap(straight[d - 1], "expert", d) for d in others]
@@ -251,20 +250,23 @@
     blocks = [total[:, k * wide : (k + 1) * wide] for k in range(CHUNKS)]
     plain = routing.astype(BF)
 
-    travelling = exchange(grad[0::CHUNKS])
+    travelling = {0: exchange(grad[0::CHUNKS])}
 
     def supply(t, arrived):
-        nonlocal travelling
-        if t < CHUNKS:
-            pieces, following, arrived = lax.optimization_barrier(
-                (travelling, grad[t + 1 :: CHUNKS] if t + 1 < CHUNKS else [], arrived)
-            )
+        if 1 <= t <= CHUNKS:
+            last, arrived = lax.optimization_barrier((travelling[t - 1][-1], arrived))
+            pieces = travelling[t - 1][:-1] + [last]
             total = 0.0
             for d in range(groups):
                 total = total + nn(plain[:, part[d]], pieces[d].reshape(rows, wide))
             blocks.append(swap(total.astype(BF), "section", 1))
+        if t < CHUNKS:
+            following = grad[t + 1 :: CHUNKS] if t + 1 < CHUNKS else []
+            travelling[t][:-1], following, arrived = lax.optimization_barrier(
+                (travelling[t][:-1], following, arrived)
+            )
             if following:
-                travelling = exchange(following)
+                travelling[t + 1] = exchange(following)
         return arrived
 
     done = sum_over(blocks, 2 * CHUNKS, "dp", supply)

time: 225 us -> 223 us (level)
  transfers between devices with their start and end apart: 41 -> 41, of which waited for: 12 -> 14; matrix products, arithmetic and copies ran while one was open for 8% -> 7% of each run, Pallas kernels for 31% -> 31%
where the time goes in v5:
time: 223 us
  Pallas kernels  69.2 us (31%)
  waiting for transfers between devices  63.1 us (28%)
  starting transfers between devices  61.3 us (27%)
  matrix products  13.6 us (6%)
  other arithmetic  8.64 us (4%)
  local copies, waits for them, and re-layouts  5.84 us (3%)
    pallas_call x2, Pallas kernels, expert_call(): pl.pallas_call(functools.partial(kernel, counts), grid=(local, width // t...  69.2 us
    ppermute x35, waiting for transfers between devices, swap(): return lax.ppermute(block, axis, [(i, i ^ flip) for i in range(size)])  63.1 us
    ppermute x35, starting transfers between devices, swap(): return lax.ppermute(block, axis, [(i, i ^ flip) for i in range(size)])  57.3 us
    dot_general x27, matrix products, nn(): lax.dot_general(a, b, (((1,), (0,)), ((), ())), preferred_element_type=F32)  13.6 us
  transfers between devices with their start and end apart: 41, of which 14 were waited for; matrix products, arithmetic and copies ran while one was open for 7% of the time, Pallas kernels for 31%

profile of v5, /device:TPU:0, one launch (start us, length us, event | category | flops | bytes accessed | tf_op | source)
XLA Modules:
  0.0 222.9 jit_solution(1629619257764876437)
XLA Ops:
  0.7 0.9 copy.19
  2.0 0.9 reduce-window.6
  3.4 0.7 multiply_add_fusion
  4.1 1.0 select_reduce_fusion
  5.1 1.3 convolution_convert_fusion.4
  6.4 4.0 %collective-permute-start.7 = (bf16[2,72,896]{2,1,0:T(8,128)(2,1)S(1)}, bf16[2,72,896]{2,1,0:T(8,128)(2,1)S(1)}, u32[]{:S(2)}, u32[]{:S(2)}) collective-permute-start(bf16[2,72,896]{2,1,0:T(8,128)(2,1)S(1)} %bitcast.140), channel_id=1, source_target_pairs={{0,3},{1,2},{2,1},{3,0},{4,7},{5,6},{6,5},{7,4},{8,11},{9,10},{10,... | collective-permute-start | bytes 774152 | tf_op jit(solution)/shard_map/ppermute | solution.py:20
  10.7 0.6 collective-permute-start.5
  12.2 2.0 collective-permute-start
  14.5 1.6 collective-permute-start.1
  18.1 2.3 %collective-permute-start.2 = (bf16[2,72,1280]{2,1,0:T(8,128)(2,1)S(1)}, bf16[2,72,1280]{2,1,0:T(8,128)(2,1)S(1)}, u32[]{:S(2)}, u32[]{:S(2)}) collective-permute-start(bf16[2,72,1280]{2,1,0:T(8,128)(2,1)S(1)} %bitcast.129), channel_id=1, source_target_pairs={{0,3},{1,2},{2,1},{3,0},{4,7},{5,6},{6,5},{7,4},{8,11},{9,10},{10,... | collective-permute-start | bytes 1105928 | tf_op jit(solution)/shard_map/ppermute | solution.py:20
  20.4 1.3 fusion.5
  22.2 1.8 collective-permute-start.8
  24.0 1.1 collective-permute-start.6
  25.2 6.3 %collective-permute-done.refs_1_ = bf16[2,72,1280]{2,1,0:T(8,128)(2,1)S(1)} collective-permute-done((bf16[2,72,1280]{2,1,0:T(8,128)(2,1)S(1)}, bf16[2,72,1280]{2,1,0:T(8,128)(2,1)S(1)}, u32[]{:S(2)}, u32[]{:S(2)}) %collective-permute-start) | collective-permute-done | bytes 368672 | tf_op jit(solution)/shard_map/ppermute | solution.py:20
  31.5 1.6 collective-permute-start.4
  33.1 1.3 convolution_convert_fusion
  34.4 3.6 %collective-permute-done.2.refs_7_ = bf16[2,72,1280]{2,1,0:T(8,128)(2,1)S(1)} collective-permute-done((bf16[2,72,1280]{2,1,0:T(8,128)(2,1)S(1)}, bf16[2,72,1280]{2,1,0:T(8,128)(2,1)S(1)}, u32[]{:S(2)}, u32[]{:S(2)}) %collective-permute-start.2) | collective-permute-done | bytes 368672 | tf_op jit(solution)/shard_map/ppermute | solution.py:20
  38.0 0.8 copy-done.8
  38.8 1.7 collective-permute-start.9
  40.5 1.5 collective-permute-start.10
  42.3 34.8 %shard_map.86 = (bf16[2,72,3072]{2,1,0:T(8,128)(2,1)}, bf16[2,72,3072]{2,1,0:T(8,128)(2,1)}, bf16[2,72,3072]{2,1,0:T(8,128)(2,1)}, bf16[2,72,3072]{2,1,0:T(8,128...) custom-call(s32[1]{0:T(128)} %bitcast.half_ref, bf16[2,72,3072]{2,1,0:T(8,128)(2,1)} %bitcast.124, ...), custom_call_target="tpu_custom_call" | custom-call | flops 21743271936 | bytes 75497472 | tf_op jit(solution)/shard_map/pallas_call | solution.py:153
  77.1 1.8 collective-permute-start.14
  78.9 1.5 collective-permute-start.15
  80.7 0.6 copy-done.3
  81.9 34.3 %shard_map.87 = (bf16[2,72,1024]{2,1,0:T(8,128)(2,1)S(1)}, bf16[2,72,1024]{2,1,0:T(8,128)(2,1)S(1)}, bf16[2,72,1024]{2,1,0:T(8,128)(2,1)S(1)}, bf16[2,72,1024]{2...) custom-call(s32[1]{0:T(128)} %bitcast.half_ref, ...), custom_call_target="tpu_custom_call" | custom-call | flops 21743271936 | bytes 75497472 | tf_op jit(solution)/shard_map/pallas_call | solution.py:153
  116.7 0.8 collective-permute-done.16
  119.1 0.9 fusion.72
  120.0 1.6 collective-permute-start.17
  121.6 1.4 collective-permute-start.12
  123.0 1.1 collective-permute-start.13
  124.1 1.0 collective-permute-start.23
  125.5 6.8 %collective-permute-done.17 = bf16[192,1024]{1,0:T(8,128)(2,1)} collective-permute-done((bf16[192,1024]{1,0:T(8,128)(2,1)}, bf16[192,1024]{1,0:T(8,128)(2,1)}, u32[]{:S(2)}, u32[]{:S(2)}) %collective-permute-start.17) | collective-permute-done | bytes 393248 | tf_op jit(solution)/shard_map/ppermute | solution.py:20
  132.4 1.1 add_convert_fusion.11
  133.5 1.7 collective-permute-done.13
  135.2 1.7 collective-permute-start.22
  136.9 0.7 collective-permute-start.19
  137.6 1.3 fusion.40
  139.5 0.6 copy-done.11
  140.1 1.8 collective-permute-start.29
  142.0 1.4 collective-permute-done.21
  143.4 2.5 %collective-permute-done.22 = bf16[2,72,1024]{2,1,0:T(8,128)(2,1)S(1)} collective-permute-done((bf16[2,72,1024]{2,1,0:T(8,128)(2,1)S(1)}, bf16[2,72,1024]{2,1,0:T(8,128)(2,1)S(1)}, u32[]{:S(2)}, u32[]{:S(2)}) %collective-permute-start.22) | collective-permute-done | bytes 294944 | tf_op jit(solution)/shard_map/ppermute | solution.py:20
  145.9 3.0 %collective-permute-start.28 = (bf16[2,72,1024]{2,1,0:T(8,128)(2,1)S(1)}, bf16[2,72,1024]{2,1,0:T(8,128)(2,1)S(1)}, u32[]{:S(2)}, u32[]{:S(2)}) collective-permute-start(bf16[2,72,1024]{2,1,0:T(8,128)(2,1)S(1)} %copy-done.10), channel_id=1, source_target_pairs={{0,2},{1,3},{2,0},{3,1},{4,6},{5,7},{6,4},{7,5},{8,10},{9,11},{10,... | collective-permute-start | bytes 884744 | tf_op jit(solution)/shard_map/ppermute | solution.py:20
  149.1 1.8 collective-permute-start.20
  150.9 0.7 collective-permute-start.24
  152.7 4.2 %collective-permute-done.20 = bf16[192,1024]{1,0:T(8,128)(2,1)S(1)} collective-permute-done((bf16[192,1024]{1,0:T(8,128)(2,1)S(1)}, bf16[192,1024]{1,0:T(8,128)(2,1)S(1)}, u32[]{:S(2)}, u32[]{:S(2)}) %collective-permute-start.20) | collective-permute-done | bytes 393248 | tf_op jit(solution)/shard_map/ppermute | solution.py:20
  156.9 1.5 collective-permute-start.33
  158.5 0.7 collective-permute-start.30
  159.5 0.6 collective-permute-start.31
  160.6 6.0 %collective-permute-start.26 = (bf16[192,1024]{1,0:T(8,128)(2,1)S(1)}, bf16[192,1024]{1,0:T(8,128)(2,1)S(1)}, u32[]{:S(2)}, u32[]{:S(2)}) collective-permute-start(bf16[192,1024]{1,0:T(8,128)(2,1)S(1)} %broadcast_select_fusion.7), channel_id=1, source_target_pairs={{0,4},{4,0},{8,12},{12,8},{1,5},{5,1},{9,13},{13,9},{2,6},{6,2},{1... | collective-permute-start | bytes 1179656 | tf_op jit(solution)/shard_map/ppermute | solution.py:20
  167.2 9.0 %collective-permute-done.26 = bf16[192,1024]{1,0:T(8,128)(2,1)S(1)} collective-permute-done((bf16[192,1024]{1,0:T(8,128)(2,1)S(1)}, bf16[192,1024]{1,0:T(8,128)(2,1)S(1)}, u32[]{:S(2)}, u32[]{:S(2)}) %collective-permute-start.26) | collective-permute-done | bytes 393248 | tf_op jit(solution)/shard_map/ppermute | solution.py:20
  176.5 1.8 collective-permute-start.32
  178.3 0.7 collective-permute-start.34
  179.4 8.0 %collective-permute-done.32 = bf16[192,1024]{1,0:T(8,128)(2,1)S(1)} collective-permute-done((bf16[192,1024]{1,0:T(8,128)(2,1)S(1)}, bf16[192,1024]{1,0:T(8,128)(2,1)S(1)}, u32[]{:S(2)}, u32[]{:S(2)}) %collective-permute-start.32) | collective-permute-done | bytes 393248 | tf_op jit(solution)/shard_map/ppermute | solution.py:20
  187.6 3.7 %collective-permute-start.36 = (bf16[192,1024]{1,0:T(8,128)(2,1)S(1)}, bf16[192,1024]{1,0:T(8,128)(2,1)S(1)}, u32[]{:S(2)}, u32[]{:S(2)}) collective-permute-start(bf16[192,1024]{1,0:T(8,128)(2,1)S(1)} %broadcast_select_fusion.3), channel_id=1, source_target_pairs={{0,4},{4,0},{8,12},{12,8},{1,5},{5,1},{9,13},{13,9},{2,6},{6,2},{1... | collective-permute-start | bytes 1179656 | tf_op jit(solution)/shard_map/ppermute | solution.py:20
  191.4 0.7 collective-permute-start.37
  192.5 6.6 %collective-permute-done.36 = bf16[192,1024]{1,0:T(8,128)(2,1)S(1)} collective-permute-done((bf16[192,1024]{1,0:T(8,128)(2,1)S(1)}, bf16[192,1024]{1,0:T(8,128)(2,1)S(1)}, u32[]{:S(2)}, u32[]{:S(2)}) %collective-permute-start.36) | collective-permute-done | bytes 393248 | tf_op jit(solution)/shard_map/ppermute | solution.py:20
  199.5 0.7 collective-permute-start.39
  200.2 5.7 %collective-permute-start.38 = (bf16[192,1024]{1,0:T(8,128)(2,1)S(1)}, bf16[192,1024]{1,0:T(8,128)(2,1)S(1)}, u32[]{:S(2)}, u32[]{:S(2)}) collective-permute-start(bf16[192,1024]{1,0:T(8,128)(2,1)S(1)} %add_convert_fusion.2), channel_id=1, source_target_pairs={{0,4},{4,0},{8,12},{12,8},{1,5},{5,1},{9,13},{13,9},{2,6},{6,2},{1... | collective-permute-start | bytes 1179656 | tf_op jit(solution)/shard_map/ppermute | solution.py:20
  206.0 1.1 maximum_bitcast_fusion
  207.1 5.8 %collective-permute-done.38 = bf16[192,1024]{1,0:T(8,128)(2,1)S(1)} collective-permute-done((bf16[192,1024]{1,0:T(8,128)(2,1)S(1)}, bf16[192,1024]{1,0:T(8,128)(2,1)S(1)}, u32[]{:S(2)}, u32[]{:S(2)}) %collective-permute-start.38) | collective-permute-done | bytes 393248 | tf_op jit(solution)/shard_map/ppermute | solution.py:20
  213.0 2.1 collective-permute-start.40
  215.4 5.9 %collective-permute-done.40 = bf16[192,1024]{1,0:T(8,128)(2,1)S(1)} collective-permute-done((bf16[192,1024]{1,0:T(8,128)(2,1)S(1)}, bf16[192,1024]{1,0:T(8,128)(2,1)S(1)}, u32[]{:S(2)}, u32[]{:S(2)}) %collective-permute-start.40) | collective-permute-done | bytes 393248 | tf_op jit(solution)/shard_map/ppermute | solution.py:20
  221.3 1.1 maximum_bitcast_fusion.1
  222.4 0.6 copy-done.1
  (109 shorter events, 14.4 us)
Async XLA Ops:
  0.6 15.6 %copy-start = (bf16[1,192,3072]{2,1,0:T(8,128)(2,1)S(1)}, bf16[1,192,3072]{2,1,0:T(8,128)(2,1)}, u32[]{:S(2)}) copy-start(bf16[1,192,3072]{2,1,0:T(8,128)(2,1)} %param.10) | copy-start | bytes 3538948
  0.6 9.8 %copy-start.2 = (bf16[1,192,3072]{2,1,0:T(8,128)(2,1)S(1)}, bf16[1,192,3072]{2,1,0:T(8,128)(2,1)}, u32[]{:S(2)}) copy-start(bf16[1,192,3072]{2,1,0:T(8,128)(2,1)} %param.7) | copy-start | bytes 3538948
  6.4 11.6 %collective-permute-start.7 = (bf16[2,72,896]{2,1,0:T(8,128)(2,1)S(1)}, bf16[2,72,896]{2,1,0:T(8,128)(2,1)S(1)}, u32[]{:S(2)}, u32[]{:S(2)}) collective-permute-start(bf16[2,72,896]{2,1,0:T(8,128)(2,1)S(1)} %bitcast.140), channel_id=1, source_target_pairs={{0,3},{1,2},{2,1},{3,0},{4,7},{5,6},{6,5},{7,4},{8,11},{9,10},{10,... | collective-permute-start | bytes 774152 | tf_op jit(solution)/shard_map/ppermute | solution.py:20
  10.7 11.5 %collective-permute-start.5 = (bf16[2,72,896]{2,1,0:T(8,128)(2,1)S(1)}, bf16[2,72,896]{2,1,0:T(8,128)(2,1)S(1)}, u32[]{:S(2)}, u32[]{:S(2)}) collective-permute-start(bf16[2,72,896]{2,1,0:T(8,128)(2,1)S(1)} %bitcast.139), channel_id=1, source_target_pairs={{0,2},{1,3},{2,0},{3,1},{4,6},{5,7},{6,4},{7,5},{8,10},{9,11},{10,... | collective-permute-start | bytes 774152 | tf_op jit(solution)/shard_map/ppermute | solution.py:20
  11.7 12.4 %collective-permute-start.3 = (bf16[2,72,896]{2,1,0:T(8,128)(2,1)S(1)}, bf16[2,72,896]{2,1,0:T(8,128)(2,1)S(1)}, u32[]{:S(2)}, u32[]{:S(2)}) collective-permute-start(bf16[2,72,896]{2,1,0:T(8,128)(2,1)S(1)} %bitcast.138), channel_id=1, source_target_pairs={{0,1},{1,0},{2,3},{3,2},{4,5},{5,4},{6,7},{7,6},{8,9},{9,8},{10,11... | collective-permute-start | bytes 774152 | tf_op jit(solution)/shard_map/ppermute | solution.py:20
  12.2 19.3 %collective-permute-start = (bf16[2,72,1280]{2,1,0:T(8,128)(2,1)S(1)}, bf16[2,72,1280]{2,1,0:T(8,128)(2,1)S(1)}, u32[]{:S(2)}, u32[]{:S(2)}) collective-permute-start(bf16[2,72,1280]{2,1,0:T(8,128)(2,1)S(1)} %bitcast.128), channel_id=1, source_target_pairs={{0,1},{1,0},{2,3},{3,2},{4,5},{5,4},{6,7},{7,6},{8,9},{9,8},{10,11... | collective-permute-start | bytes 1105928 | tf_op jit(solution)/shard_map/ppermute | solution.py:20
  14.5 19.9 %collective-permute-start.1 = (bf16[2,72,1280]{2,1,0:T(8,128)(2,1)S(1)}, bf16[2,72,1280]{2,1,0:T(8,128)(2,1)S(1)}, u32[]{:S(2)}, u32[]{:S(2)}) collective-permute-start(bf16[2,72,1280]{2,1,0:T(8,128)(2,1)S(1)} %bitcast.127), channel_id=1, source_target_pairs={{0,2},{1,3},{2,0},{3,1},{4,6},{5,7},{6,4},{7,5},{8,10},{9,11},{10,... | collective-permute-start | bytes 1105928 | tf_op jit(solution)/shard_map/ppermute | solution.py:20
  18.1 19.9 %collective-permute-start.2 = (bf16[2,72,1280]{2,1,0:T(8,128)(2,1)S(1)}, bf16[2,72,1280]{2,1,0:T(8,128)(2,1)S(1)}, u32[]{:S(2)}, u32[]{:S(2)}) collective-permute-start(bf16[2,72,1280]{2,1,0:T(8,128)(2,1)S(1)} %bitcast.129), channel_id=1, source_target_pairs={{0,3},{1,2},{2,1},{3,0},{4,7},{5,6},{6,5},{7,4},{8,11},{9,10},{10,... | collective-permute-start | bytes 1105928 | tf_op jit(solution)/shard_map/ppermute | solution.py:20
  22.2 19.7 %collective-permute-start.8 = (bf16[2,72,896]{2,1,0:T(8,128)(2,1)S(1)}, bf16[2,72,896]{2,1,0:T(8,128)(2,1)S(1)}, u32[]{:S(2)}, u32[]{:S(2)}) collective-permute-start(bf16[2,72,896]{2,1,0:T(8,128)(2,1)S(1)} %collective-permute-done.7.refs_8_), channel_id=1, source_target_pairs={{0,4},{4,0},{8,12},{12,8},{1,5},{5,1},{9,13},{13,9},{2,6},{6,2},{1... | collective-permute-start | bytes 774152 | tf_op jit(solution)/shard_map/ppermute | solution.py:20
  24.0 18.3 %collective-permute-start.6 = (bf16[2,72,896]{2,1,0:T(8,128)(2,1)S(1)}, bf16[2,72,896]{2,1,0:T(8,128)(2,1)S(1)}, u32[]{:S(2)}, u32[]{:S(2)}) collective-permute-start(bf16[2,72,896]{2,1,0:T(8,128)(2,1)S(1)} %collective-permute-done.5.refs_5_), channel_id=1, source_target_pairs={{0,4},{4,0},{8,12},{12,8},{1,5},{5,1},{9,13},{13,9},{2,6},{6,2},{1... | collective-permute-start | bytes 774152 | tf_op jit(solution)/shard_map/ppermute | solution.py:20
  31.5 10.8 %collective-permute-start.4 = (bf16[2,72,896]{2,1,0:T(8,128)(2,1)S(1)}, bf16[2,72,896]{2,1,0:T(8,128)(2,1)S(1)}, u32[]{:S(2)}, u32[]{:S(2)}) collective-permute-start(bf16[2,72,896]{2,1,0:T(8,128)(2,1)S(1)} %collective-permute-done.3.refs_2_), channel_id=1, source_target_pairs={{0,4},{4,0},{8,12},{12,8},{1,5},{5,1},{9,13},{13,9},{2,6},{6,2},{1... | collective-permute-start | bytes 774152 | tf_op jit(solution)/shard_map/ppermute | solution.py:20
  34.4 7.9 %copy-start.7 = (bf16[2,72,1280]{2,1,0:T(8,128)(2,1)}, bf16[2,72,1280]{2,1,0:T(8,128)(2,1)S(1)}, u32[]{:S(2)}) copy-start(bf16[2,72,1280]{2,1,0:T(8,128)(2,1)S(1)} %collective-permute-done.1.refs_4_) | copy-start | bytes 1105924
  38.0 0.8 copy-start.8
  38.8 41.6 %collective-permute-start.9 = (bf16[2,72,3072]{2,1,0:T(8,128)(2,1)S(1)}, bf16[2,72,3072]{2,1,0:T(8,128)(2,1)S(1)}, u32[]{:S(2)}, u32[]{:S(2)}) collective-permute-start(bf16[2,72,3072]{2,1,0:T(8,128)(2,1)S(1)} %bitcast.123), channel_id=1, source_target_pairs={{0,1},{1,0},{2,3},{3,2},{4,5},{5,4},{6,7},{7,6},{8,9},{9,8},{10,11... | collective-permute-start | bytes 2654216 | tf_op jit(solution)/shard_map/ppermute | solution.py:20
  40.5 40.2 %collective-permute-start.10 = (bf16[2,72,3072]{2,1,0:T(8,128)(2,1)S(1)}, bf16[2,72,3072]{2,1,0:T(8,128)(2,1)S(1)}, u32[]{:S(2)}, u32[]{:S(2)}) collective-permute-start(bf16[2,72,3072]{2,1,0:T(8,128)(2,1)S(1)} %bitcast.122), channel_id=1, source_target_pairs={{0,2},{1,3},{2,0},{3,1},{4,6},{5,7},{6,4},{7,5},{8,10},{9,11},{10,... | collective-permute-start | bytes 2654216 | tf_op jit(solution)/shard_map/ppermute | solution.py:20
  42.0 38.7 %collective-permute-start.11 = (bf16[2,72,3072]{2,1,0:T(8,128)(2,1)S(1)}, bf16[2,72,3072]{2,1,0:T(8,128)(2,1)S(1)}, u32[]{:S(2)}, u32[]{:S(2)}) collective-permute-start(bf16[2,72,3072]{2,1,0:T(8,128)(2,1)S(1)} %bitcast.121), channel_id=1, source_target_pairs={{0,3},{1,2},{2,1},{3,0},{4,7},{5,6},{6,5},{7,4},{8,11},{9,10},{10,... | collective-permute-start | bytes 2654216 | tf_op jit(solution)/shard_map/ppermute | solution.py:20
  77.1 40.9 %collective-permute-start.14 = (bf16[2,72,3072]{2,1,0:T(8,128)(2,1)}, bf16[2,72,3072]{2,1,0:T(8,128)(2,1)S(1)}, u32[]{:S(2)}, u32[]{:S(2)}) collective-permute-start(bf16[2,72,3072]{2,1,0:T(8,128)(2,1)} %get-tuple-element.86), channel_id=1, source_target_pairs={{0,1},{1,0},{2,3},{3,2},{4,5},{5,4},{6,7},{7,6},{8,9},{9,8},{10,11... | collective-permute-start | bytes 2654216 | tf_op jit(solution)/shard_map/ppermute | solution.py:20
  78.9 39.6 %collective-permute-start.15 = (bf16[2,72,3072]{2,1,0:T(8,128)(2,1)}, bf16[2,72,3072]{2,1,0:T(8,128)(2,1)S(1)}, u32[]{:S(2)}, u32[]{:S(2)}) collective-permute-start(bf16[2,72,3072]{2,1,0:T(8,128)(2,1)} %get-tuple-element.87), channel_id=1, source_target_pairs={{0,2},{1,3},{2,0},{3,1},{4,6},{5,7},{6,4},{7,5},{8,10},{9,11},{10,... | collective-permute-start | bytes 2654216 | tf_op jit(solution)/shard_map/ppermute | solution.py:20
  80.4 0.9 copy-start.3
  80.4 37.1 %collective-permute-start.16 = (bf16[2,72,3072]{2,1,0:T(8,128)(2,1)}, bf16[2,72,3072]{2,1,0:T(8,128)(2,1)S(1)}, u32[]{:S(2)}, u32[]{:S(2)}) collective-permute-start(bf16[2,72,3072]{2,1,0:T(8,128)(2,1)} %get-tuple-element.88), channel_id=1, source_target_pairs={{0,3},{1,2},{2,1},{3,0},{4,7},{5,6},{6,5},{7,4},{8,11},{9,10},{10,... | collective-permute-start | bytes 2654216 | tf_op jit(solution)/shard_map/ppermute | solution.py:20
  80.7 1.0 copy-start.4
  80.7 1.2 copy-start.5
  81.9 34.3 %copy-start.6 = (bf16[2,72,3072]{2,1,0:T(8,128)(2,1)S(1)}, bf16[2,72,3072]{2,1,0:T(8,128)(2,1)}, u32[]{:S(2)}) copy-start(bf16[2,72,3072]{2,1,0:T(8,128)(2,1)} %get-tuple-element.85) | copy-start | bytes 2654212
  120.0 12.4 %collective-permute-start.17 = (bf16[192,1024]{1,0:T(8,128)(2,1)}, bf16[192,1024]{1,0:T(8,128)(2,1)}, u32[]{:S(2)}, u32[]{:S(2)}) collective-permute-start(bf16[192,1024]{1,0:T(8,128)(2,1)} %get-tuple-element.136), channel_id=1, source_target_pairs={{0,4},{4,0},{8,12},{12,8},{1,5},{5,1},{9,13},{13,9},{2,6},{6,2},{1... | collective-permute-start | bytes 1179656 | tf_op jit(solution)/shard_map/ppermute | solution.py:20
  121.6 11.9 %collective-permute-start.12 = (bf16[2,72,1024]{2,1,0:T(8,128)(2,1)S(1)}, bf16[2,72,1024]{2,1,0:T(8,128)(2,1)}, u32[]{:S(2)}, u32[]{:S(2)}) collective-permute-start(bf16[2,72,1024]{2,1,0:T(8,128)(2,1)S(1)} %get-tuple-element.79), channel_id=1, source_target_pairs={{0,1},{1,0},{2,3},{3,2},{4,5},{5,4},{6,7},{7,6},{8,9},{9,8},{10,11... | collective-permute-start | bytes 884744 | tf_op jit(solution)/shard_map/ppermute | solution.py:20
  123.0 12.3 %collective-permute-start.13 = (bf16[2,72,1024]{2,1,0:T(8,128)(2,1)}, bf16[2,72,1024]{2,1,0:T(8,128)(2,1)S(1)}, u32[]{:S(2)}, u32[]{:S(2)}) collective-permute-start(bf16[2,72,1024]{2,1,0:T(8,128)(2,1)} %get-tuple-element.80), channel_id=1, source_target_pairs={{0,2},{1,3},{2,0},{3,1},{4,6},{5,7},{6,4},{7,5},{8,10},{9,11},{10,... | collective-permute-start | bytes 884744 | tf_op jit(solution)/shard_map/ppermute | solution.py:20
  124.1 11.1 %copy-start.12 = (bf16[2,72,1024]{2,1,0:T(8,128)(2,1)S(1)}, bf16[2,72,1024]{2,1,0:T(8,128)(2,1)}, u32[]{:S(2)}) copy-start(bf16[2,72,1024]{2,1,0:T(8,128)(2,1)} %get-tuple-element.93) | copy-start | bytes 884740
  124.1 17.9 %collective-permute-start.23 = (bf16[2,72,1024]{2,1,0:T(8,128)(2,1)}, bf16[2,72,1024]{2,1,0:T(8,128)(2,1)S(1)}, u32[]{:S(2)}, u32[]{:S(2)}) collective-permute-start(bf16[2,72,1024]{2,1,0:T(8,128)(2,1)} %get-tuple-element.98), channel_id=1, source_target_pairs={{0,3},{1,2},{2,1},{3,0},{4,7},{5,6},{6,5},{7,4},{8,11},{9,10},{10,... | collective-permute-start | bytes 884744 | tf_op jit(solution)/shard_map/ppermute | solution.py:20
  125.1 14.4 %collective-permute-start.18 = (bf16[192,1024]{1,0:T(8,128)(2,1)}, bf16[192,1024]{1,0:T(8,128)(2,1)S(1)}, u32[]{:S(2)}, u32[]{:S(2)}) collective-permute-start(bf16[192,1024]{1,0:T(8,128)(2,1)} %get-tuple-element.135), channel_id=1, source_target_pairs={{0,4},{4,0},{8,12},{12,8},{1,5},{5,1},{9,13},{13,9},{2,6},{6,2},{1... | collective-permute-start | bytes 1179656 | tf_op jit(solution)/shard_map/ppermute | solution.py:20
  135.2 8.2 %collective-permute-start.21 = (bf16[2,72,1024]{2,1,0:T(8,128)(2,1)S(1)}, bf16[2,72,1024]{2,1,0:T(8,128)(2,1)S(1)}, u32[]{:S(2)}, u32[]{:S(2)}) collective-permute-start(bf16[2,72,1024]{2,1,0:T(8,128)(2,1)S(1)} %get-tuple-element.92), channel_id=1, source_target_pairs={{0,1},{1,0},{2,3},{3,2},{4,5},{5,4},{6,7},{7,6},{8,9},{9,8},{10,11... | collective-permute-start | bytes 884744 | tf_op jit(solution)/shard_map/ppermute | solution.py:20
  135.2 10.6 %collective-permute-start.22 = (bf16[2,72,1024]{2,1,0:T(8,128)(2,1)S(1)}, bf16[2,72,1024]{2,1,0:T(8,128)(2,1)S(1)}, u32[]{:S(2)}, u32[]{:S(2)}) collective-permute-start(bf16[2,72,1024]{2,1,0:T(8,128)(2,1)S(1)} %copy-done.12), channel_id=1, source_target_pairs={{0,2},{1,3},{2,0},{3,1},{4,6},{5,7},{6,4},{7,5},{8,10},{9,11},{10,... | collective-permute-start | bytes 884744 | tf_op jit(solution)/shard_map/ppermute | solution.py:20
  136.9 4.9 %collective-permute-start.19 = (bf16[192,1024]{1,0:T(8,128)(2,1)S(1)}, bf16[192,1024]{1,0:T(8,128)(2,1)S(1)}, u32[]{:S(2)}, u32[]{:S(2)}) collective-permute-start(bf16[192,1024]{1,0:T(8,128)(2,1)S(1)} %add_convert_fusion.11), channel_id=1, source_target_pairs={{0,0},{4,8},{8,4},{12,12},{1,1},{5,9},{9,5},{13,13},{2,2},{6,10},{... | collective-permute-start | bytes 1179656 | tf_op jit(solution)/shard_map/ppermute | solution.py:187
  139.1 1.0 copy-start.11
  139.2 6.7 %copy-start.10 = (bf16[2,72,1024]{2,1,0:T(8,128)(2,1)S(1)}, bf16[2,72,1024]{2,1,0:T(8,128)(2,1)}, u32[]{:S(2)}) copy-start(bf16[2,72,1024]{2,1,0:T(8,128)(2,1)} %get-tuple-element.110) | copy-start | bytes 884740
  140.1 18.4 %collective-permute-start.29 = (bf16[2,72,1024]{2,1,0:T(8,128)(2,1)S(1)}, bf16[2,72,1024]{2,1,0:T(8,128)(2,1)S(1)}, u32[]{:S(2)}, u32[]{:S(2)}) collective-permute-start(bf16[2,72,1024]{2,1,0:T(8,128)(2,1)S(1)} %copy-done.11), channel_id=1, source_target_pairs={{0,3},{1,2},{2,1},{3,0},{4,7},{5,6},{6,5},{7,4},{8,11},{9,10},{10,... | collective-permute-start | bytes 884744 | tf_op jit(solution)/shard_map/ppermute | solution.py:20
  145.9 12.7 %collective-permute-start.27 = (bf16[2,72,1024]{2,1,0:T(8,128)(2,1)S(1)}, bf16[2,72,1024]{2,1,0:T(8,128)(2,1)S(1)}, u32[]{:S(2)}, u32[]{:S(2)}) collective-permute-start(bf16[2,72,1024]{2,1,0:T(8,128)(2,1)S(1)} %get-tuple-element.109), channel_id=1, source_target_pairs={{0,1},{1,0},{2,3},{3,2},{4,5},{5,4},{6,7},{7,6},{8,9},{9,8},{10,11... | collective-permute-start | bytes 884744 | tf_op jit(solution)/shard_map/ppermute | solution.py:20
  145.9 12.7 %collective-permute-start.28 = (bf16[2,72,1024]{2,1,0:T(8,128)(2,1)S(1)}, bf16[2,72,1024]{2,1,0:T(8,128)(2,1)S(1)}, u32[]{:S(2)}, u32[]{:S(2)}) collective-permute-start(bf16[2,72,1024]{2,1,0:T(8,128)(2,1)S(1)} %copy-done.10), channel_id=1, source_target_pairs={{0,2},{1,3},{2,0},{3,1},{4,6},{5,7},{6,4},{7,5},{8,10},{9,11},{10,... | collective-permute-start | bytes 884744 | tf_op jit(solution)/shard_map/ppermute | solution.py:20
  149.1 7.8 %collective-permute-start.20 = (bf16[192,1024]{1,0:T(8,128)(2,1)S(1)}, bf16[192,1024]{1,0:T(8,128)(2,1)S(1)}, u32[]{:S(2)}, u32[]{:S(2)}) collective-permute-start(bf16[192,1024]{1,0:T(8,128)(2,1)S(1)} %broadcast_select_fusion.9), channel_id=1, source_target_pairs={{0,4},{4,0},{8,12},{12,8},{1,5},{5,1},{9,13},{13,9},{2,6},{6,2},{1... | collective-permute-start | bytes 1179656 | tf_op jit(solution)/shard_map/ppermute | solution.py:20
  150.9 7.5 %collective-permute-start.24 = (bf16[192,1024]{1,0:T(8,128)(2,1)S(1)}, bf16[192,1024]{1,0:T(8,128)(2,1)S(1)}, u32[]{:S(2)}, u32[]{:S(2)}) collective-permute-start(bf16[192,1024]{1,0:T(8,128)(2,1)S(1)} %add_convert_fusion.9), channel_id=1, source_target_pairs={{0,0},{4,8},{8,4},{12,12},{1,1},{5,9},{9,5},{13,13},{2,2},{6,10},{... | collective-permute-start | bytes 1179656 | tf_op jit(solution)/shard_map/ppermute | solution.py:187
  152.4 4.5 %copy-start.9 = (bf16[2,72,1024]{2,1,0:T(8,128)(2,1)S(1)}, bf16[2,72,1024]{2,1,0:T(8,128)(2,1)}, u32[]{:S(2)}) copy-start(bf16[2,72,1024]{2,1,0:T(8,128)(2,1)} %get-tuple-element.120) | copy-start | bytes 884740
  156.9 19.4 %collective-permute-start.33 = (bf16[2,72,1024]{2,1,0:T(8,128)(2,1)S(1)}, bf16[2,72,1024]{2,1,0:T(8,128)(2,1)S(1)}, u32[]{:S(2)}, u32[]{:S(2)}) collective-permute-start(bf16[2,72,1024]{2,1,0:T(8,128)(2,1)S(1)} %copy-done.9), channel_id=1, source_target_pairs={{0,3},{1,2},{2,1},{3,0},{4,7},{5,6},{6,5},{7,4},{8,11},{9,10},{10,... | collective-permute-start | bytes 884744 | tf_op jit(solution)/shard_map/ppermute | solution.py:20
  158.4 2.1 collective-permute-start.25
  158.5 8.6 %collective-permute-start.30 = (bf16[192,1024]{1,0:T(8,128)(2,1)S(1)}, bf16[192,1024]{1,0:T(8,128)(2,1)S(1)}, u32[]{:S(2)}, u32[]{:S(2)}) collective-permute-start(bf16[192,1024]{1,0:T(8,128)(2,1)S(1)} %add_convert_fusion.7), channel_id=1, source_target_pairs={{0,0},{4,8},{8,4},{12,12},{1,1},{5,9},{9,5},{13,13},{2,2},{6,10},{... | collective-permute-start | bytes 1179656 | tf_op jit(solution)/shard_map/ppermute | solution.py:187
  159.5 16.8 %collective-permute-start.31 = (bf16[192,1024]{1,0:T(8,128)(2,1)S(1)}, bf16[192,1024]{1,0:T(8,128)(2,1)S(1)}, u32[]{:S(2)}, u32[]{:S(2)}) collective-permute-start(bf16[192,1024]{1,0:T(8,128)(2,1)S(1)} %fusion.7), channel_id=1, source_target_pairs={{0,16},{16,0},{1,17},{17,1},{2,18},{18,2},{3,19},{19,3},{4,20},{20... | collective-permute-start | bytes 1179656 | tf_op jit(solution)/shard_map/ppermute | solution.py:20
  160.6 15.5 %collective-permute-start.26 = (bf16[192,1024]{1,0:T(8,128)(2,1)S(1)}, bf16[192,1024]{1,0:T(8,128)(2,1)S(1)}, u32[]{:S(2)}, u32[]{:S(2)}) collective-permute-start(bf16[192,1024]{1,0:T(8,128)(2,1)S(1)} %broadcast_select_fusion.7), channel_id=1, source_target_pairs={{0,4},{4,0},{8,12},{12,8},{1,5},{5,1},{9,13},{13,9},{2,6},{6,2},{1... | collective-permute-start | bytes 1179656 | tf_op jit(solution)/shard_map/ppermute | solution.py:20
  176.5 10.9 %collective-permute-start.32 = (bf16[192,1024]{1,0:T(8,128)(2,1)S(1)}, bf16[192,1024]{1,0:T(8,128)(2,1)S(1)}, u32[]{:S(2)}, u32[]{:S(2)}) collective-permute-start(bf16[192,1024]{1,0:T(8,128)(2,1)S(1)} %broadcast_select_fusion.5), channel_id=1, source_target_pairs={{0,4},{4,0},{8,12},{12,8},{1,5},{5,1},{9,13},{13,9},{2,6},{6,2},{1... | collective-permute-start | bytes 1179656 | tf_op jit(solution)/shard_map/ppermute | solution.py:20
  178.3 9.1 %collective-permute-start.34 = (bf16[192,1024]{1,0:T(8,128)(2,1)S(1)}, bf16[192,1024]{1,0:T(8,128)(2,1)S(1)}, u32[]{:S(2)}, u32[]{:S(2)}) collective-permute-start(bf16[192,1024]{1,0:T(8,128)(2,1)S(1)} %add_convert_fusion.5), channel_id=1, source_target_pairs={{0,0},{4,8},{8,4},{12,12},{1,1},{5,9},{9,5},{13,13},{2,2},{6,10},{... | collective-permute-start | bytes 1179656 | tf_op jit(solution)/shard_map/ppermute | solution.py:187
  179.3 8.1 %collective-permute-start.35 = (bf16[192,1024]{1,0:T(8,128)(2,1)S(1)}, bf16[192,1024]{1,0:T(8,128)(2,1)S(1)}, u32[]{:S(2)}, u32[]{:S(2)}) collective-permute-start(bf16[192,1024]{1,0:T(8,128)(2,1)S(1)} %fusion.8), channel_id=1, source_target_pairs={{0,16},{16,0},{1,17},{17,1},{2,18},{18,2},{3,19},{19,3},{4,20},{20... | collective-permute-start | bytes 1179656 | tf_op jit(solution)/shard_map/ppermute | solution.py:20
  187.6 11.6 %collective-permute-start.36 = (bf16[192,1024]{1,0:T(8,128)(2,1)S(1)}, bf16[192,1024]{1,0:T(8,128)(2,1)S(1)}, u32[]{:S(2)}, u32[]{:S(2)}) collective-permute-start(bf16[192,1024]{1,0:T(8,128)(2,1)S(1)} %broadcast_select_fusion.3), channel_id=1, source_target_pairs={{0,4},{4,0},{8,12},{12,8},{1,5},{5,1},{9,13},{13,9},{2,6},{6,2},{1... | collective-permute-start | bytes 1179656 | tf_op jit(solution)/shard_map/ppermute | solution.py:20
  191.4 7.7 %collective-permute-start.37 = (bf16[192,1024]{1,0:T(8,128)(2,1)S(1)}, bf16[192,1024]{1,0:T(8,128)(2,1)S(1)}, u32[]{:S(2)}, u32[]{:S(2)}) collective-permute-start(bf16[192,1024]{1,0:T(8,128)(2,1)S(1)} %add_convert_fusion.3), channel_id=1, source_target_pairs={{0,0},{4,8},{8,4},{12,12},{1,1},{5,9},{9,5},{13,13},{2,2},{6,10},{... | collective-permute-start | bytes 1179656 | tf_op jit(solution)/shard_map/ppermute | solution.py:187
  199.5 7.7 %collective-permute-start.39 = (bf16[192,1024]{1,0:T(8,128)(2,1)S(1)}, bf16[192,1024]{1,0:T(8,128)(2,1)S(1)}, u32[]{:S(2)}, u32[]{:S(2)}) collective-permute-start(bf16[192,1024]{1,0:T(8,128)(2,1)S(1)} %add_convert_fusion.1), channel_id=1, source_target_pairs={{0,0},{4,8},{8,4},{12,12},{1,1},{5,9},{9,5},{13,13},{2,2},{6,10},{... | collective-permute-start | bytes 1179656 | tf_op jit(solution)/shard_map/ppermute | solution.py:187
  200.2 12.7 %collective-permute-start.38 = (bf16[192,1024]{1,0:T(8,128)(2,1)S(1)}, bf16[192,1024]{1,0:T(8,128)(2,1)S(1)}, u32[]{:S(2)}, u32[]{:S(2)}) collective-permute-start(bf16[192,1024]{1,0:T(8,128)(2,1)S(1)} %add_convert_fusion.2), channel_id=1, source_target_pairs={{0,4},{4,0},{8,12},{12,8},{1,5},{5,1},{9,13},{13,9},{2,6},{6,2},{1... | collective-permute-start | bytes 1179656 | tf_op jit(solution)/shard_map/ppermute | solution.py:20
  213.0 8.2 %collective-permute-start.40 = (bf16[192,1024]{1,0:T(8,128)(2,1)S(1)}, bf16[192,1024]{1,0:T(8,128)(2,1)S(1)}, u32[]{:S(2)}, u32[]{:S(2)}) collective-permute-start(bf16[192,1024]{1,0:T(8,128)(2,1)S(1)} %add_convert_fusion), channel_id=1, source_target_pairs={{0,4},{4,0},{8,12},{12,8},{1,5},{5,1},{9,13},{13,9},{2,6},{6,2},{1... | collective-permute-start | bytes 1179656 | tf_op jit(solution)/shard_map/ppermute | solution.py:20
  221.3 1.7 copy-start.1

commit v6 on v5

--- a/solution.py
+++ b/solution.py
@@ -22,22 +22,20 @@
 
 def slot_tables(chosen, weights_two, experts, local, capacity, me):
     number = chosen.shape[0]
-    relative = ((chosen // local) ^ me) * local + chosen % local
-    flattened = relative.reshape(-1)
-    one_hot = (flattened[:, None] == jnp.arange(experts, dtype=jnp.int32)[None, :]).astype(
-        jnp.int32
-    )
-    earlier = jnp.cumsum(one_hot, axis=0) - one_hot
-    position = jnp.sum(earlier * one_hot, axis=1)
-    slot_index = flattened * capacity + position
-    selection = (
-        slot_index[:, None] == jnp.arange(experts * capacity, dtype=jnp.int32)[None, :]
-    ).astype(F32)
-    selection = selection.reshape(number, 2, experts * capacity)
-    routing = jnp.sum(selection, axis=1)
-    weighting = jnp.sum(selection * weights_two[:, :, None], axis=1)
-    slot_weight = jnp.sum(weighting, axis=0)
-    return routing, weighting, slot_weight
+    relative = (((chosen // local) ^ me) * local + chosen % local).T
+    numbers = jnp.arange(experts, dtype=jnp.int32)[:, None]
+    first, second = relative[0:1] == numbers, relative[1:2] == numbers
+    member = first | second
+    token = jnp.arange(number, dtype=jnp.int32)
+    before = (token[:, None] < token[None, :]).astype(BF)
+    place = nn(member.astype(BF), before).astype(jnp.int32)
+    place = jnp.where(member, place, -1)
+    slots = jnp.arange(capacity, dtype=jnp.int32)[None, :, None]
+    routing = (place[:, None, :] == slots).astype(F32)
+    weight = jnp.where(first, weights_two[:, 0][None, :], 0.0)
+    weight = weight + jnp.where(second, weights_two[:, 1][None, :], 0.0)
+    weighting = (routing * weight[:, None, :]).reshape(experts * capacity, number)
+    return routing.reshape(experts * capacity, number), weighting, jnp.sum(weighting, axis=1)
 
 
 def nn(a, b):
@@ -204,7 +202,7 @@
     routing, weighting, slot_weight = slot_tables(
         chosen, weights_two, local * groups, local, CAP, me
     )
-    picker = routing.T.astype(BF)
+    picker = lax.optimization_barrier(routing.astype(BF))
     rows = local * CAP
     part = [slice(d * rows, (d + 1) * rows) for d in range(groups)]
 
@@ -228,7 +226,10 @@
     far = [swap(one, "dp", 1) for one in near]
     c_sent = [picked(d, upstream, True) for d in others]
     c_own = picked(0, upstream, True)
-    straight, c_sent, c_own = lax.optimization_barrier((straight, c_sent, c_own))
+    plain, high = picker.T, weighting.T.astype(BF)
+    straight, c_sent, c_own, plain, high = lax.optimization_barrier(
+        (straight, c_sent, c_own, plain, high)
+    )
     x = [[straight[d], near[d], far[d]] for d in range(groups - 1)]
     c = [[swap(c_sent[d - 1], "expert", d)] for d in others]
     chip_half = half.astype(jnp.int32).reshape(1)
@@ -241,14 +242,12 @@
     )
 
     out[0], grad[0] = lax.optimization_barrier((out[0], grad[0]))
-    high = weighting.astype(BF)
     total = 0.0
     for d in range(groups):
         total = total + nn(high[:, part[d]], out[d].reshape(rows, model))
     total = total.astype(BF)
     wide = model // CHUNKS
     blocks = [total[:, k * wide : (k + 1) * wide] for k in range(CHUNKS)]
-    plain = routing.astype(BF)
 
     travelling = {0: exchange(grad[0::CHUNKS])}
 

time: 223 us -> 223 us (level)
  matrix products: 13.6 us -> 22.3 us
  starting transfers between devices: 61.3 us -> 56.6 us
    dot_general x27 -> x28, matrix products: 13.6 us -> 22.3 us  [nn(): lax.dot_general(a, b, (((1,), (0,)), ((), ())), preferred_element_type=F32)]
    ppermute x35, starting transfers between devices: 57.3 us -> 52.3 us  [swap(): return lax.ppermute(block, axis, [(i, i ^ flip) for i in range(size)])]
  transfers between devices with their start and end apart: 41 -> 41, of which waited for: 14 -> 15; matrix products, arithmetic and copies ran while one was open for 7% -> 11% of each run, Pallas kernels for 31% -> 31%
where the time goes in v6:
time: 223 us
  Pallas kernels  69.3 us (31%)
  waiting for transfers between devices  62 us (28%)
  starting transfers between devices  56.6 us (25%)
  matrix products  22.3 us (10%)
  other arithmetic  7.27 us (3%)
  local copies, waits for them, and re-layouts  3.83 us (2%)
    pallas_call x2, Pallas kernels, expert_call(): pl.pallas_call(functools.partial(kernel, counts), grid=(local, width // t...  69.3 us
    ppermute x35, waiting for transfers between devices, swap(): return lax.ppermute(block, axis, [(i, i ^ flip) for i in range(size)])  62 us
    ppermute x35, starting transfers between devices, swap(): return lax.ppermute(block, axis, [(i, i ^ flip) for i in range(size)])  52.3 us
    dot_general x28, matrix products, nn(): lax.dot_general(a, b, (((1,), (0,)), ((), ())), preferred_element_type=F32)  22.3 us
  transfers between devices with their start and end apart: 41, of which 15 were waited for; matrix products, arithmetic and copies ran while one was open for 11% of the time, Pallas kernels for 31%

profile of v6, /device:TPU:0, one launch (start us, length us, event | category | flops | bytes accessed | tf_op | source)
XLA Modules:
  0.0 222.6 jit_solution(4627976473980875328)
XLA Ops:
  0.7 0.8 fusion.63
  1.9 1.9 convolution_convert_fusion.4
  3.8 3.9 %collective-permute-start.7 = (bf16[2,72,896]{2,1,0:T(8,128)(2,1)}, bf16[2,72,896]{2,1,0:T(8,128)(2,1)S(1)}, u32[]{:S(2)}, u32[]{:S(2)}) collective-permute-start(bf16[2,72,896]{2,1,0:T(8,128)(2,1)} %bitcast.25), channel_id=1, source_target_pairs={{0,3},{1,2},{2,1},{3,0},{4,7},{5,6},{6,5},{7,4},{8,11},{9,10},{10,... | collective-permute-start | bytes 774152 | tf_op jit(solution)/shard_map/ppermute | solution.py:20
  7.7 1.9 convolution_convert_fusion.5
  10.1 0.9 convolution_convert_fusion.6
  11.2 1.0 convolution_convert_fusion.3
  12.2 2.0 collective-permute-start
  14.1 2.0 convolution_convert_fusion.2
  16.2 1.5 collective-permute-start.1
  18.2 1.3 fusion.2
  19.5 1.3 fusion.3
  21.2 2.0 convolution_convert_fusion.1
  23.4 1.3 fusion.5
  24.9 2.1 collective-permute-start.8
  27.1 2.0 collective-permute-done.refs_1_
  29.0 1.6 collective-permute-start.4
  30.6 1.3 convolution_convert_fusion
  31.9 3.6 %collective-permute-done.2.refs_7_ = bf16[2,72,1280]{2,1,0:T(8,128)(2,1)S(1)} collective-permute-done((bf16[2,72,1280]{2,1,0:T(8,128)(2,1)}, bf16[2,72,1280]{2,1,0:T(8,128)(2,1)S(1)}, u32[]{:S(2)}, u32[]{:S(2)}) %collective-permute-start.2) | collective-permute-done | bytes 368672 | tf_op jit(solution)/shard_map/ppermute | solution.py:20
  35.5 1.7 collective-permute-start.9
  37.2 1.5 collective-permute-start.10
  39.0 0.6 collective-permute-done.6.refs_6_
  39.6 2.9 %collective-permute-done.4.refs_3_ = bf16[2,72,896]{2,1,0:T(8,128)(2,1)S(1)} collective-permute-done((bf16[2,72,896]{2,1,0:T(8,128)(2,1)S(1)}, bf16[2,72,896]{2,1,0:T(8,128)(2,1)S(1)}, u32[]{:S(2)}, u32[]{:S(2)}) %collective-permute-start.4) | collective-permute-done | bytes 258080 | tf_op jit(solution)/shard_map/ppermute | solution.py:20
  42.6 35.0 %shard_map.86 = (bf16[2,72,3072]{2,1,0:T(8,128)(2,1)}, bf16[2,72,3072]{2,1,0:T(8,128)(2,1)}, bf16[2,72,3072]{2,1,0:T(8,128)(2,1)}, bf16[2,72,3072]{2,1,0:T(8,128...) custom-call(s32[1]{0:T(128)} %bitcast.half_ref, bf16[2,72,3072]{2,1,0:T(8,128)(2,1)} %bitcast.141, ...), custom_call_target="tpu_custom_call" | custom-call | flops 21743271936 | bytes 75497472 | tf_op jit(solution)/shard_map/pallas_call | solution.py:151
  77.5 1.7 collective-permute-start.14
  79.3 1.5 collective-permute-start.15
  81.1 0.6 copy-done.4
  82.3 34.3 %shard_map.87 = (bf16[2,72,1024]{2,1,0:T(8,128)(2,1)S(1)}, bf16[2,72,1024]{2,1,0:T(8,128)(2,1)S(1)}, bf16[2,72,1024]{2,1,0:T(8,128)(2,1)S(1)}, bf16[2,72,1024]{2...) custom-call(s32[1]{0:T(128)} %bitcast.half_ref, ...), custom_call_target="tpu_custom_call" | custom-call | flops 21743271936 | bytes 75497472 | tf_op jit(solution)/shard_map/pallas_call | solution.py:151
  117.8 0.7 copy-done.9
  119.6 0.9 fusion.68
  120.5 1.6 collective-permute-start.17
  122.1 1.4 collective-permute-start.12
  123.5 1.5 collective-permute-start.13
  126.0 6.6 %collective-permute-done.17 = bf16[192,1024]{1,0:T(8,128)(2,1)} collective-permute-done((bf16[192,1024]{1,0:T(8,128)(2,1)}, bf16[192,1024]{1,0:T(8,128)(2,1)}, u32[]{:S(2)}, u32[]{:S(2)}) %collective-permute-start.17) | collective-permute-done | bytes 393248 | tf_op jit(solution)/shard_map/ppermute | solution.py:20
  132.6 1.1 add_convert_fusion.11
  134.2 1.0 collective-permute-start.21
  135.2 1.5 collective-permute-start.22
  136.7 0.7 collective-permute-start.19
  138.0 1.3 convolution_add_fusion.9
  139.4 1.2 collective-permute-start.29
  140.8 2.3 %collective-permute-done.21 = bf16[2,72,1024]{2,1,0:T(8,128)(2,1)S(1)} collective-permute-done((bf16[2,72,1024]{2,1,0:T(8,128)(2,1)S(1)}, bf16[2,72,1024]{2,1,0:T(8,128)(2,1)S(1)}, u32[]{:S(2)}, u32[]{:S(2)}) %collective-permute-start.21) | collective-permute-done | bytes 294944 | tf_op jit(solution)/shard_map/ppermute | solution.py:20
  143.1 3.6 %collective-permute-done.22 = bf16[2,72,1024]{2,1,0:T(8,128)(2,1)S(1)} collective-permute-done((bf16[2,72,1024]{2,1,0:T(8,128)(2,1)S(1)}, bf16[2,72,1024]{2,1,0:T(8,128)(2,1)S(1)}, u32[]{:S(2)}, u32[]{:S(2)}) %collective-permute-start.22) | collective-permute-done | bytes 294944 | tf_op jit(solution)/shard_map/ppermute | solution.py:20
  146.6 2.1 collective-permute-start.28
  148.9 1.3 collective-permute-start.20
  150.3 0.7 collective-permute-start.24
  152.2 4.6 %collective-permute-done.20 = bf16[192,1024]{1,0:T(8,128)(2,1)S(1)} collective-permute-done((bf16[192,1024]{1,0:T(8,128)(2,1)S(1)}, bf16[192,1024]{1,0:T(8,128)(2,1)S(1)}, u32[]{:S(2)}, u32[]{:S(2)}) %collective-permute-start.20) | collective-permute-done | bytes 393248 | tf_op jit(solution)/shard_map/ppermute | solution.py:20
  156.8 1.5 collective-permute-start.33
  158.4 0.9 collective-permute-start.30
  159.7 0.6 collective-permute-start.31
  160.7 5.5 %collective-permute-start.26 = (bf16[192,1024]{1,0:T(8,128)(2,1)S(1)}, bf16[192,1024]{1,0:T(8,128)(2,1)S(1)}, u32[]{:S(2)}, u32[]{:S(2)}) collective-permute-start(bf16[192,1024]{1,0:T(8,128)(2,1)S(1)} %broadcast_select_fusion.7), channel_id=1, source_target_pairs={{0,4},{4,0},{8,12},{12,8},{1,5},{5,1},{9,13},{13,9},{2,6},{6,2},{1... | collective-permute-start | bytes 1179656 | tf_op jit(solution)/shard_map/ppermute | solution.py:20
  166.9 8.9 %collective-permute-done.26 = bf16[192,1024]{1,0:T(8,128)(2,1)S(1)} collective-permute-done((bf16[192,1024]{1,0:T(8,128)(2,1)S(1)}, bf16[192,1024]{1,0:T(8,128)(2,1)S(1)}, u32[]{:S(2)}, u32[]{:S(2)}) %collective-permute-start.26) | collective-permute-done | bytes 393248 | tf_op jit(solution)/shard_map/ppermute | solution.py:20
  176.2 1.8 collective-permute-start.32
  178.0 0.7 collective-permute-start.34
  179.1 8.0 %collective-permute-done.32 = bf16[192,1024]{1,0:T(8,128)(2,1)S(1)} collective-permute-done((bf16[192,1024]{1,0:T(8,128)(2,1)S(1)}, bf16[192,1024]{1,0:T(8,128)(2,1)S(1)}, u32[]{:S(2)}, u32[]{:S(2)}) %collective-permute-start.32) | collective-permute-done | bytes 393248 | tf_op jit(solution)/shard_map/ppermute | solution.py:20
  187.3 3.7 %collective-permute-start.36 = (bf16[192,1024]{1,0:T(8,128)(2,1)S(1)}, bf16[192,1024]{1,0:T(8,128)(2,1)S(1)}, u32[]{:S(2)}, u32[]{:S(2)}) collective-permute-start(bf16[192,1024]{1,0:T(8,128)(2,1)S(1)} %broadcast_select_fusion.3), channel_id=1, source_target_pairs={{0,4},{4,0},{8,12},{12,8},{1,5},{5,1},{9,13},{13,9},{2,6},{6,2},{1... | collective-permute-start | bytes 1179656 | tf_op jit(solution)/shard_map/ppermute | solution.py:20
  191.1 0.7 collective-permute-start.37
  192.2 6.6 %collective-permute-done.36 = bf16[192,1024]{1,0:T(8,128)(2,1)S(1)} collective-permute-done((bf16[192,1024]{1,0:T(8,128)(2,1)S(1)}, bf16[192,1024]{1,0:T(8,128)(2,1)S(1)}, u32[]{:S(2)}, u32[]{:S(2)}) %collective-permute-start.36) | collective-permute-done | bytes 393248 | tf_op jit(solution)/shard_map/ppermute | solution.py:20
  199.1 0.7 collective-permute-start.39
  199.8 5.7 %collective-permute-start.38 = (bf16[192,1024]{1,0:T(8,128)(2,1)S(1)}, bf16[192,1024]{1,0:T(8,128)(2,1)S(1)}, u32[]{:S(2)}, u32[]{:S(2)}) collective-permute-start(bf16[192,1024]{1,0:T(8,128)(2,1)S(1)} %add_convert_fusion.2), channel_id=1, source_target_pairs={{0,4},{4,0},{8,12},{12,8},{1,5},{5,1},{9,13},{13,9},{2,6},{6,2},{1... | collective-permute-start | bytes 1179656 | tf_op jit(solution)/shard_map/ppermute | solution.py:20
  205.7 1.1 maximum_bitcast_fusion
  206.8 5.8 %collective-permute-done.38 = bf16[192,1024]{1,0:T(8,128)(2,1)S(1)} collective-permute-done((bf16[192,1024]{1,0:T(8,128)(2,1)S(1)}, bf16[192,1024]{1,0:T(8,128)(2,1)S(1)}, u32[]{:S(2)}, u32[]{:S(2)}) %collective-permute-start.38) | collective-permute-done | bytes 393248 | tf_op jit(solution)/shard_map/ppermute | solution.py:20
  212.7 2.1 collective-permute-start.40
  215.0 5.9 %collective-permute-done.40 = bf16[192,1024]{1,0:T(8,128)(2,1)S(1)} collective-permute-done((bf16[192,1024]{1,0:T(8,128)(2,1)S(1)}, bf16[192,1024]{1,0:T(8,128)(2,1)S(1)}, u32[]{:S(2)}, u32[]{:S(2)}) %collective-permute-start.40) | collective-permute-done | bytes 393248 | tf_op jit(solution)/shard_map/ppermute | solution.py:20
  220.9 1.1 maximum_bitcast_fusion.1
  222.0 0.6 copy-done.1
  (115 shorter events, 13.1 us)
Async XLA Ops:
  0.6 17.6 %copy-start = (bf16[1,192,3072]{2,1,0:T(8,128)(2,1)S(1)}, bf16[1,192,3072]{2,1,0:T(8,128)(2,1)}, u32[]{:S(2)}) copy-start(bf16[1,192,3072]{2,1,0:T(8,128)(2,1)} %param.10) | copy-start | bytes 3538948
  0.6 9.5 %copy-start.2 = (bf16[1,192,3072]{2,1,0:T(8,128)(2,1)S(1)}, bf16[1,192,3072]{2,1,0:T(8,128)(2,1)}, u32[]{:S(2)}) copy-start(bf16[1,192,3072]{2,1,0:T(8,128)(2,1)} %param.7) | copy-start | bytes 3538948
  3.8 19.5 %collective-permute-start.7 = (bf16[2,72,896]{2,1,0:T(8,128)(2,1)}, bf16[2,72,896]{2,1,0:T(8,128)(2,1)S(1)}, u32[]{:S(2)}, u32[]{:S(2)}) collective-permute-start(bf16[2,72,896]{2,1,0:T(8,128)(2,1)} %bitcast.25), channel_id=1, source_target_pairs={{0,3},{1,2},{2,1},{3,0},{4,7},{5,6},{6,5},{7,4},{8,11},{9,10},{10,... | collective-permute-start | bytes 774152 | tf_op jit(solution)/shard_map/ppermute | solution.py:20
  9.6 8.1 %copy-start.10 = (f32[1,192,2]{1,2,0:T(2,128)S(1)}, f32[1,192,2]{1,2,0:T(2,128)}, u32[]{:S(2)}) copy-start(f32[1,192,2]{1,2,0:T(2,128)} %param.9) | copy-start | bytes 4612
  9.6 15.2 %collective-permute-start.5 = (bf16[2,72,896]{2,1,0:T(8,128)(2,1)}, bf16[2,72,896]{2,1,0:T(8,128)(2,1)S(1)}, u32[]{:S(2)}, u32[]{:S(2)}) collective-permute-start(bf16[2,72,896]{2,1,0:T(8,128)(2,1)} %bitcast.24), channel_id=1, source_target_pairs={{0,2},{1,3},{2,0},{3,1},{4,6},{5,7},{6,4},{7,5},{8,10},{9,11},{10,... | collective-permute-start | bytes 774152 | tf_op jit(solution)/shard_map/ppermute | solution.py:20
  11.1 15.9 %collective-permute-start.3 = (bf16[2,72,896]{2,1,0:T(8,128)(2,1)}, bf16[2,72,896]{2,1,0:T(8,128)(2,1)S(1)}, u32[]{:S(2)}, u32[]{:S(2)}) collective-permute-start(bf16[2,72,896]{2,1,0:T(8,128)(2,1)} %bitcast.23), channel_id=1, source_target_pairs={{0,1},{1,0},{2,3},{3,2},{4,5},{5,4},{6,7},{7,6},{8,9},{9,8},{10,11... | collective-permute-start | bytes 774152 | tf_op jit(solution)/shard_map/ppermute | solution.py:20
  12.2 16.9 %collective-permute-start = (bf16[2,72,1280]{2,1,0:T(8,128)(2,1)}, bf16[2,72,1280]{2,1,0:T(8,128)(2,1)S(1)}, u32[]{:S(2)}, u32[]{:S(2)}) collective-permute-start(bf16[2,72,1280]{2,1,0:T(8,128)(2,1)} %bitcast.8), channel_id=1, source_target_pairs={{0,1},{1,0},{2,3},{3,2},{4,5},{5,4},{6,7},{7,6},{8,9},{9,8},{10,11... | collective-permute-start | bytes 1105928 | tf_op jit(solution)/shard_map/ppermute | solution.py:20
  16.2 15.7 %collective-permute-start.1 = (bf16[2,72,1280]{2,1,0:T(8,128)(2,1)}, bf16[2,72,1280]{2,1,0:T(8,128)(2,1)}, u32[]{:S(2)}, u32[]{:S(2)}) collective-permute-start(bf16[2,72,1280]{2,1,0:T(8,128)(2,1)} %bitcast.9), channel_id=1, source_target_pairs={{0,2},{1,3},{2,0},{3,1},{4,6},{5,7},{6,4},{7,5},{8,10},{9,11},{10,... | collective-permute-start | bytes 1105928 | tf_op jit(solution)/shard_map/ppermute | solution.py:20
  23.4 7.2 %copy-start.3 = (bf16[1,192,3072]{2,1,0:T(8,128)(2,1)S(1)}, bf16[1,192,3072]{2,1,0:T(8,128)(2,1)}, u32[]{:S(2)}) copy-start(bf16[1,192,3072]{2,1,0:T(8,128)(2,1)} %param.7) | copy-start | bytes 3538948
  23.4 12.2 %collective-permute-start.2 = (bf16[2,72,1280]{2,1,0:T(8,128)(2,1)}, bf16[2,72,1280]{2,1,0:T(8,128)(2,1)S(1)}, u32[]{:S(2)}, u32[]{:S(2)}) collective-permute-start(bf16[2,72,1280]{2,1,0:T(8,128)(2,1)} %bitcast.144), channel_id=1, source_target_pairs={{0,3},{1,2},{2,1},{3,0},{4,7},{5,6},{6,5},{7,4},{8,11},{9,10},{10,... | collective-permute-start | bytes 1105928 | tf_op jit(solution)/shard_map/ppermute | solution.py:20
  24.7 10.8 %copy-start.8 = (bf16[144,3072]{1,0:T(8,128)(2,1)S(1)}, bf16[144,3072]{1,0:T(8,128)(2,1)}, u32[]{:S(2)}) copy-start(bf16[144,3072]{1,0:T(8,128)(2,1)} %fusion.2) | copy-start | bytes 2654212
  24.7 12.5 %copy-start.7 = (bf16[144,3072]{1,0:T(8,128)(2,1)S(1)}, bf16[144,3072]{1,0:T(8,128)(2,1)}, u32[]{:S(2)}) copy-start(bf16[144,3072]{1,0:T(8,128)(2,1)} %fusion.3) | copy-start | bytes 2654212
  24.9 13.9 %collective-permute-start.8 = (bf16[2,72,896]{2,1,0:T(8,128)(2,1)S(1)}, bf16[2,72,896]{2,1,0:T(8,128)(2,1)S(1)}, u32[]{:S(2)}, u32[]{:S(2)}) collective-permute-start(bf16[2,72,896]{2,1,0:T(8,128)(2,1)S(1)} %collective-permute-done.7.refs_8_), channel_id=1, source_target_pairs={{0,4},{4,0},{8,12},{12,8},{1,5},{5,1},{9,13},{13,9},{2,6},{6,2},{1... | collective-permute-start | bytes 774152 | tf_op jit(solution)/shard_map/ppermute | solution.py:20
  27.0 12.7 %collective-permute-start.6 = (bf16[2,72,896]{2,1,0:T(8,128)(2,1)S(1)}, bf16[2,72,896]{2,1,0:T(8,128)(2,1)S(1)}, u32[]{:S(2)}, u32[]{:S(2)}) collective-permute-start(bf16[2,72,896]{2,1,0:T(8,128)(2,1)S(1)} %collective-permute-done.5.refs_5_), channel_id=1, source_target_pairs={{0,4},{4,0},{8,12},{12,8},{1,5},{5,1},{9,13},{13,9},{2,6},{6,2},{1... | collective-permute-start | bytes 774152 | tf_op jit(solution)/shard_map/ppermute | solution.py:20
  29.0 13.5 %collective-permute-start.4 = (bf16[2,72,896]{2,1,0:T(8,128)(2,1)S(1)}, bf16[2,72,896]{2,1,0:T(8,128)(2,1)S(1)}, u32[]{:S(2)}, u32[]{:S(2)}) collective-permute-start(bf16[2,72,896]{2,1,0:T(8,128)(2,1)S(1)} %collective-permute-done.3.refs_2_), channel_id=1, source_target_pairs={{0,4},{4,0},{8,12},{12,8},{1,5},{5,1},{9,13},{13,9},{2,6},{6,2},{1... | collective-permute-start | bytes 774152 | tf_op jit(solution)/shard_map/ppermute | solution.py:20
  35.5 7.0 %copy-start.11 = (bf16[2,72,1280]{2,1,0:T(8,128)(2,1)}, bf16[2,72,1280]{2,1,0:T(8,128)(2,1)S(1)}, u32[]{:S(2)}) copy-start(bf16[2,72,1280]{2,1,0:T(8,128)(2,1)S(1)} %collective-permute-done.2.refs_7_) | copy-start | bytes 1105924
  35.5 45.2 %collective-permute-start.9 = (bf16[2,72,3072]{2,1,0:T(8,128)(2,1)S(1)}, bf16[2,72,3072]{2,1,0:T(8,128)(2,1)S(1)}, u32[]{:S(2)}, u32[]{:S(2)}) collective-permute-start(bf16[2,72,3072]{2,1,0:T(8,128)(2,1)S(1)} %bitcast.140), channel_id=1, source_target_pairs={{0,1},{1,0},{2,3},{3,2},{4,5},{5,4},{6,7},{7,6},{8,9},{9,8},{10,11... | collective-permute-start | bytes 2654216 | tf_op jit(solution)/shard_map/ppermute | solution.py:20
  37.2 43.9 %collective-permute-start.10 = (bf16[2,72,3072]{2,1,0:T(8,128)(2,1)S(1)}, bf16[2,72,3072]{2,1,0:T(8,128)(2,1)S(1)}, u32[]{:S(2)}, u32[]{:S(2)}) collective-permute-start(bf16[2,72,3072]{2,1,0:T(8,128)(2,1)S(1)} %bitcast.139), channel_id=1, source_target_pairs={{0,2},{1,3},{2,0},{3,1},{4,6},{5,7},{6,4},{7,5},{8,10},{9,11},{10,... | collective-permute-start | bytes 2654216 | tf_op jit(solution)/shard_map/ppermute | solution.py:20
  38.7 42.4 %collective-permute-start.11 = (bf16[2,72,3072]{2,1,0:T(8,128)(2,1)S(1)}, bf16[2,72,3072]{2,1,0:T(8,128)(2,1)S(1)}, u32[]{:S(2)}, u32[]{:S(2)}) collective-permute-start(bf16[2,72,3072]{2,1,0:T(8,128)(2,1)S(1)} %bitcast.138), channel_id=1, source_target_pairs={{0,3},{1,2},{2,1},{3,0},{4,7},{5,6},{6,5},{7,4},{8,11},{9,10},{10,... | collective-permute-start | bytes 2654216 | tf_op jit(solution)/shard_map/ppermute | solution.py:20
  77.5 39.8 %collective-permute-start.14 = (bf16[2,72,3072]{2,1,0:T(8,128)(2,1)}, bf16[2,72,3072]{2,1,0:T(8,128)(2,1)S(1)}, u32[]{:S(2)}, u32[]{:S(2)}) collective-permute-start(bf16[2,72,3072]{2,1,0:T(8,128)(2,1)} %get-tuple-element.89), channel_id=1, source_target_pairs={{0,1},{1,0},{2,3},{3,2},{4,5},{5,4},{6,7},{7,6},{8,9},{9,8},{10,11... | collective-permute-start | bytes 2654216 | tf_op jit(solution)/shard_map/ppermute | solution.py:20
  79.3 39.8 %collective-permute-start.15 = (bf16[2,72,3072]{2,1,0:T(8,128)(2,1)}, bf16[2,72,3072]{2,1,0:T(8,128)(2,1)S(1)}, u32[]{:S(2)}, u32[]{:S(2)}) collective-permute-start(bf16[2,72,3072]{2,1,0:T(8,128)(2,1)} %get-tuple-element.90), channel_id=1, source_target_pairs={{0,2},{1,3},{2,0},{3,1},{4,6},{5,7},{6,4},{7,5},{8,10},{9,11},{10,... | collective-permute-start | bytes 2654216 | tf_op jit(solution)/shard_map/ppermute | solution.py:20
  80.8 0.9 copy-start.4
  80.8 36.0 %collective-permute-start.16 = (bf16[2,72,3072]{2,1,0:T(8,128)(2,1)}, bf16[2,72,3072]{2,1,0:T(8,128)(2,1)S(1)}, u32[]{:S(2)}, u32[]{:S(2)}) collective-permute-start(bf16[2,72,3072]{2,1,0:T(8,128)(2,1)} %get-tuple-element.91), channel_id=1, source_target_pairs={{0,3},{1,2},{2,1},{3,0},{4,7},{5,6},{6,5},{7,4},{8,11},{9,10},{10,... | collective-permute-start | bytes 2654216 | tf_op jit(solution)/shard_map/ppermute | solution.py:20
  81.1 0.9 copy-start.5
  81.1 1.2 copy-start.6
  117.3 1.2 copy-start.9
  120.5 12.1 %collective-permute-start.17 = (bf16[192,1024]{1,0:T(8,128)(2,1)}, bf16[192,1024]{1,0:T(8,128)(2,1)}, u32[]{:S(2)}, u32[]{:S(2)}) collective-permute-start(bf16[192,1024]{1,0:T(8,128)(2,1)} %get-tuple-element.137), channel_id=1, source_target_pairs={{0,4},{4,0},{8,12},{12,8},{1,5},{5,1},{9,13},{13,9},{2,6},{6,2},{1... | collective-permute-start | bytes 1179656 | tf_op jit(solution)/shard_map/ppermute | solution.py:20
  122.1 11.6 %collective-permute-start.12 = (bf16[2,72,1024]{2,1,0:T(8,128)(2,1)S(1)}, bf16[2,72,1024]{2,1,0:T(8,128)(2,1)S(1)}, u32[]{:S(2)}, u32[]{:S(2)}) collective-permute-start(bf16[2,72,1024]{2,1,0:T(8,128)(2,1)S(1)} %get-tuple-element.81), channel_id=1, source_target_pairs={{0,1},{1,0},{2,3},{3,2},{4,5},{5,4},{6,7},{7,6},{8,9},{9,8},{10,11... | collective-permute-start | bytes 884744 | tf_op jit(solution)/shard_map/ppermute | solution.py:20
  123.5 10.7 %collective-permute-start.13 = (bf16[2,72,1024]{2,1,0:T(8,128)(2,1)}, bf16[2,72,1024]{2,1,0:T(8,128)(2,1)}, u32[]{:S(2)}, u32[]{:S(2)}) collective-permute-start(bf16[2,72,1024]{2,1,0:T(8,128)(2,1)} %get-tuple-element.82), channel_id=1, source_target_pairs={{0,2},{1,3},{2,0},{3,1},{4,6},{5,7},{6,4},{7,5},{8,10},{9,11},{10,... | collective-permute-start | bytes 884744 | tf_op jit(solution)/shard_map/ppermute | solution.py:20
  125.1 10.1 %copy-start.15 = (bf16[2,72,1024]{2,1,0:T(8,128)(2,1)S(1)}, bf16[2,72,1024]{2,1,0:T(8,128)(2,1)}, u32[]{:S(2)}) copy-start(bf16[2,72,1024]{2,1,0:T(8,128)(2,1)} %get-tuple-element.96) | copy-start | bytes 884740
  125.1 15.7 %collective-permute-start.23 = (bf16[2,72,1024]{2,1,0:T(8,128)(2,1)}, bf16[2,72,1024]{2,1,0:T(8,128)(2,1)S(1)}, u32[]{:S(2)}, u32[]{:S(2)}) collective-permute-start(bf16[2,72,1024]{2,1,0:T(8,128)(2,1)} %get-tuple-element.101), channel_id=1, source_target_pairs={{0,3},{1,2},{2,1},{3,0},{4,7},{5,6},{6,5},{7,4},{8,11},{9,10},{10,... | collective-permute-start | bytes 884744 | tf_op jit(solution)/shard_map/ppermute | solution.py:20
  125.6 13.8 %collective-permute-start.18 = (bf16[192,1024]{1,0:T(8,128)(2,1)}, bf16[192,1024]{1,0:T(8,128)(2,1)S(1)}, u32[]{:S(2)}, u32[]{:S(2)}) collective-permute-start(bf16[192,1024]{1,0:T(8,128)(2,1)} %get-tuple-element.136), channel_id=1, source_target_pairs={{0,4},{4,0},{8,12},{12,8},{1,5},{5,1},{9,13},{13,9},{2,6},{6,2},{1... | collective-permute-start | bytes 1179656 | tf_op jit(solution)/shard_map/ppermute | solution.py:20
  134.2 8.8 %collective-permute-start.21 = (bf16[2,72,1024]{2,1,0:T(8,128)(2,1)S(1)}, bf16[2,72,1024]{2,1,0:T(8,128)(2,1)S(1)}, u32[]{:S(2)}, u32[]{:S(2)}) collective-permute-start(bf16[2,72,1024]{2,1,0:T(8,128)(2,1)S(1)} %get-tuple-element.95), channel_id=1, source_target_pairs={{0,1},{1,0},{2,3},{3,2},{4,5},{5,4},{6,7},{7,6},{8,9},{9,8},{10,11... | collective-permute-start | bytes 884744 | tf_op jit(solution)/shard_map/ppermute | solution.py:20
  135.2 11.4 %collective-permute-start.22 = (bf16[2,72,1024]{2,1,0:T(8,128)(2,1)S(1)}, bf16[2,72,1024]{2,1,0:T(8,128)(2,1)S(1)}, u32[]{:S(2)}, u32[]{:S(2)}) collective-permute-start(bf16[2,72,1024]{2,1,0:T(8,128)(2,1)S(1)} %copy-done.15), channel_id=1, source_target_pairs={{0,2},{1,3},{2,0},{3,1},{4,6},{5,7},{6,4},{7,5},{8,10},{9,11},{10,... | collective-permute-start | bytes 884744 | tf_op jit(solution)/shard_map/ppermute | solution.py:20
  136.7 3.9 %collective-permute-start.19 = (bf16[192,1024]{1,0:T(8,128)(2,1)S(1)}, bf16[192,1024]{1,0:T(8,128)(2,1)S(1)}, u32[]{:S(2)}, u32[]{:S(2)}) collective-permute-start(bf16[192,1024]{1,0:T(8,128)(2,1)S(1)} %add_convert_fusion.11), channel_id=1, source_target_pairs={{0,0},{4,8},{8,4},{12,12},{1,1},{5,9},{9,5},{13,13},{2,2},{6,10},{... | collective-permute-start | bytes 1179656 | tf_op jit(solution)/shard_map/ppermute | solution.py:185
  138.0 1.4 copy-start.14
  138.0 8.6 %copy-start.13 = (bf16[2,72,1024]{2,1,0:T(8,128)(2,1)S(1)}, bf16[2,72,1024]{2,1,0:T(8,128)(2,1)}, u32[]{:S(2)}) copy-start(bf16[2,72,1024]{2,1,0:T(8,128)(2,1)} %get-tuple-element.114) | copy-start | bytes 884740
  139.4 19.0 %collective-permute-start.29 = (bf16[2,72,1024]{2,1,0:T(8,128)(2,1)S(1)}, bf16[2,72,1024]{2,1,0:T(8,128)(2,1)S(1)}, u32[]{:S(2)}, u32[]{:S(2)}) collective-permute-start(bf16[2,72,1024]{2,1,0:T(8,128)(2,1)S(1)} %copy-done.14), channel_id=1, source_target_pairs={{0,3},{1,2},{2,1},{3,0},{4,7},{5,6},{6,5},{7,4},{8,11},{9,10},{10,... | collective-permute-start | bytes 884744 | tf_op jit(solution)/shard_map/ppermute | solution.py:20
  146.6 11.8 %collective-permute-start.27 = (bf16[2,72,1024]{2,1,0:T(8,128)(2,1)S(1)}, bf16[2,72,1024]{2,1,0:T(8,128)(2,1)S(1)}, u32[]{:S(2)}, u32[]{:S(2)}) collective-permute-start(bf16[2,72,1024]{2,1,0:T(8,128)(2,1)S(1)} %get-tuple-element.113), channel_id=1, source_target_pairs={{0,1},{1,0},{2,3},{3,2},{4,5},{5,4},{6,7},{7,6},{8,9},{9,8},{10,11... | collective-permute-start | bytes 884744 | tf_op jit(solution)/shard_map/ppermute | solution.py:20
  146.6 11.8 %collective-permute-start.28 = (bf16[2,72,1024]{2,1,0:T(8,128)(2,1)S(1)}, bf16[2,72,1024]{2,1,0:T(8,128)(2,1)S(1)}, u32[]{:S(2)}, u32[]{:S(2)}) collective-permute-start(bf16[2,72,1024]{2,1,0:T(8,128)(2,1)S(1)} %copy-done.13), channel_id=1, source_target_pairs={{0,2},{1,3},{2,0},{3,1},{4,6},{5,7},{6,4},{7,5},{8,10},{9,11},{10,... | collective-permute-start | bytes 884744 | tf_op jit(solution)/shard_map/ppermute | solution.py:20
  148.9 7.8 %collective-permute-start.20 = (bf16[192,1024]{1,0:T(8,128)(2,1)S(1)}, bf16[192,1024]{1,0:T(8,128)(2,1)S(1)}, u32[]{:S(2)}, u32[]{:S(2)}) collective-permute-start(bf16[192,1024]{1,0:T(8,128)(2,1)S(1)} %broadcast_select_fusion.9), channel_id=1, source_target_pairs={{0,4},{4,0},{8,12},{12,8},{1,5},{5,1},{9,13},{13,9},{2,6},{6,2},{1... | collective-permute-start | bytes 1179656 | tf_op jit(solution)/shard_map/ppermute | solution.py:20
  150.3 8.0 %collective-permute-start.24 = (bf16[192,1024]{1,0:T(8,128)(2,1)S(1)}, bf16[192,1024]{1,0:T(8,128)(2,1)S(1)}, u32[]{:S(2)}, u32[]{:S(2)}) collective-permute-start(bf16[192,1024]{1,0:T(8,128)(2,1)S(1)} %add_convert_fusion.9), channel_id=1, source_target_pairs={{0,0},{4,8},{8,4},{12,12},{1,1},{5,9},{9,5},{13,13},{2,2},{6,10},{... | collective-permute-start | bytes 1179656 | tf_op jit(solution)/shard_map/ppermute | solution.py:185
  151.8 4.9 %copy-start.12 = (bf16[2,72,1024]{2,1,0:T(8,128)(2,1)S(1)}, bf16[2,72,1024]{2,1,0:T(8,128)(2,1)}, u32[]{:S(2)}) copy-start(bf16[2,72,1024]{2,1,0:T(8,128)(2,1)} %get-tuple-element.124) | copy-start | bytes 884740
  156.8 19.2 %collective-permute-start.33 = (bf16[2,72,1024]{2,1,0:T(8,128)(2,1)S(1)}, bf16[2,72,1024]{2,1,0:T(8,128)(2,1)S(1)}, u32[]{:S(2)}, u32[]{:S(2)}) collective-permute-start(bf16[2,72,1024]{2,1,0:T(8,128)(2,1)S(1)} %copy-done.12), channel_id=1, source_target_pairs={{0,3},{1,2},{2,1},{3,0},{4,7},{5,6},{6,5},{7,4},{8,11},{9,10},{10,... | collective-permute-start | bytes 884744 | tf_op jit(solution)/shard_map/ppermute | solution.py:20
  158.3 2.3 %collective-permute-start.25 = (bf16[192,1024]{1,0:T(8,128)(2,1)S(1)}, bf16[192,1024]{1,0:T(8,128)(2,1)S(1)}, u32[]{:S(2)}, u32[]{:S(2)}) collective-permute-start(bf16[192,1024]{1,0:T(8,128)(2,1)S(1)} %fusion.6), channel_id=1, source_target_pairs={{0,16},{16,0},{1,17},{17,1},{2,18},{18,2},{3,19},{19,3},{4,20},{20... | collective-permute-start | bytes 1179656 | tf_op jit(solution)/shard_map/ppermute | solution.py:20
  158.4 8.4 %collective-permute-start.30 = (bf16[192,1024]{1,0:T(8,128)(2,1)S(1)}, bf16[192,1024]{1,0:T(8,128)(2,1)S(1)}, u32[]{:S(2)}, u32[]{:S(2)}) collective-permute-start(bf16[192,1024]{1,0:T(8,128)(2,1)S(1)} %add_convert_fusion.7), channel_id=1, source_target_pairs={{0,0},{4,8},{8,4},{12,12},{1,1},{5,9},{9,5},{13,13},{2,2},{6,10},{... | collective-permute-start | bytes 1179656 | tf_op jit(solution)/shard_map/ppermute | solution.py:185
  159.7 16.3 %collective-permute-start.31 = (bf16[192,1024]{1,0:T(8,128)(2,1)S(1)}, bf16[192,1024]{1,0:T(8,128)(2,1)S(1)}, u32[]{:S(2)}, u32[]{:S(2)}) collective-permute-start(bf16[192,1024]{1,0:T(8,128)(2,1)S(1)} %fusion.7), channel_id=1, source_target_pairs={{0,16},{16,0},{1,17},{17,1},{2,18},{18,2},{3,19},{19,3},{4,20},{20... | collective-permute-start | bytes 1179656 | tf_op jit(solution)/shard_map/ppermute | solution.py:20
  160.7 15.1 %collective-permute-start.26 = (bf16[192,1024]{1,0:T(8,128)(2,1)S(1)}, bf16[192,1024]{1,0:T(8,128)(2,1)S(1)}, u32[]{:S(2)}, u32[]{:S(2)}) collective-permute-start(bf16[192,1024]{1,0:T(8,128)(2,1)S(1)} %broadcast_select_fusion.7), channel_id=1, source_target_pairs={{0,4},{4,0},{8,12},{12,8},{1,5},{5,1},{9,13},{13,9},{2,6},{6,2},{1... | collective-permute-start | bytes 1179656 | tf_op jit(solution)/shard_map/ppermute | solution.py:20
  176.2 10.9 %collective-permute-start.32 = (bf16[192,1024]{1,0:T(8,128)(2,1)S(1)}, bf16[192,1024]{1,0:T(8,128)(2,1)S(1)}, u32[]{:S(2)}, u32[]{:S(2)}) collective-permute-start(bf16[192,1024]{1,0:T(8,128)(2,1)S(1)} %broadcast_select_fusion.5), channel_id=1, source_target_pairs={{0,4},{4,0},{8,12},{12,8},{1,5},{5,1},{9,13},{13,9},{2,6},{6,2},{1... | collective-permute-start | bytes 1179656 | tf_op jit(solution)/shard_map/ppermute | solution.py:20
  178.0 9.1 %collective-permute-start.34 = (bf16[192,1024]{1,0:T(8,128)(2,1)S(1)}, bf16[192,1024]{1,0:T(8,128)(2,1)S(1)}, u32[]{:S(2)}, u32[]{:S(2)}) collective-permute-start(bf16[192,1024]{1,0:T(8,128)(2,1)S(1)} %add_convert_fusion.5), channel_id=1, source_target_pairs={{0,0},{4,8},{8,4},{12,12},{1,1},{5,9},{9,5},{13,13},{2,2},{6,10},{... | collective-permute-start | bytes 1179656 | tf_op jit(solution)/shard_map/ppermute | solution.py:185
  179.0 8.1 %collective-permute-start.35 = (bf16[192,1024]{1,0:T(8,128)(2,1)S(1)}, bf16[192,1024]{1,0:T(8,128)(2,1)S(1)}, u32[]{:S(2)}, u32[]{:S(2)}) collective-permute-start(bf16[192,1024]{1,0:T(8,128)(2,1)S(1)} %fusion.8), channel_id=1, source_target_pairs={{0,16},{16,0},{1,17},{17,1},{2,18},{18,2},{3,19},{19,3},{4,20},{20... | collective-permute-start | bytes 1179656 | tf_op jit(solution)/shard_map/ppermute | solution.py:20
  187.3 11.6 %collective-permute-start.36 = (bf16[192,1024]{1,0:T(8,128)(2,1)S(1)}, bf16[192,1024]{1,0:T(8,128)(2,1)S(1)}, u32[]{:S(2)}, u32[]{:S(2)}) collective-permute-start(bf16[192,1024]{1,0:T(8,128)(2,1)S(1)} %broadcast_select_fusion.3), channel_id=1, source_target_pairs={{0,4},{4,0},{8,12},{12,8},{1,5},{5,1},{9,13},{13,9},{2,6},{6,2},{1... | collective-permute-start | bytes 1179656 | tf_op jit(solution)/shard_map/ppermute | solution.py:20
  191.1 7.7 %collective-permute-start.37 = (bf16[192,1024]{1,0:T(8,128)(2,1)S(1)}, bf16[192,1024]{1,0:T(8,128)(2,1)S(1)}, u32[]{:S(2)}, u32[]{:S(2)}) collective-permute-start(bf16[192,1024]{1,0:T(8,128)(2,1)S(1)} %add_convert_fusion.3), channel_id=1, source_target_pairs={{0,0},{4,8},{8,4},{12,12},{1,1},{5,9},{9,5},{13,13},{2,2},{6,10},{... | collective-permute-start | bytes 1179656 | tf_op jit(solution)/shard_map/ppermute | solution.py:185
  199.1 7.7 %collective-permute-start.39 = (bf16[192,1024]{1,0:T(8,128)(2,1)S(1)}, bf16[192,1024]{1,0:T(8,128)(2,1)S(1)}, u32[]{:S(2)}, u32[]{:S(2)}) collective-permute-start(bf16[192,1024]{1,0:T(8,128)(2,1)S(1)} %add_convert_fusion.1), channel_id=1, source_target_pairs={{0,0},{4,8},{8,4},{12,12},{1,1},{5,9},{9,5},{13,13},{2,2},{6,10},{... | collective-permute-start | bytes 1179656 | tf_op jit(solution)/shard_map/ppermute | solution.py:185
  199.8 12.7 %collective-permute-start.38 = (bf16[192,1024]{1,0:T(8,128)(2,1)S(1)}, bf16[192,1024]{1,0:T(8,128)(2,1)S(1)}, u32[]{:S(2)}, u32[]{:S(2)}) collective-permute-start(bf16[192,1024]{1,0:T(8,128)(2,1)S(1)} %add_convert_fusion.2), channel_id=1, source_target_pairs={{0,4},{4,0},{8,12},{12,8},{1,5},{5,1},{9,13},{13,9},{2,6},{6,2},{1... | collective-permute-start | bytes 1179656 | tf_op jit(solution)/shard_map/ppermute | solution.py:20
  212.7 8.2 %collective-permute-start.40 = (bf16[192,1024]{1,0:T(8,128)(2,1)S(1)}, bf16[192,1024]{1,0:T(8,128)(2,1)S(1)}, u32[]{:S(2)}, u32[]{:S(2)}) collective-permute-start(bf16[192,1024]{1,0:T(8,128)(2,1)S(1)} %add_convert_fusion), channel_id=1, source_target_pairs={{0,4},{4,0},{8,12},{12,8},{1,5},{5,1},{9,13},{13,9},{2,6},{6,2},{1... | collective-permute-start | bytes 1179656 | tf_op jit(solution)/shard_map/ppermute | solution.py:20
  220.9 1.7 copy-start.1
